TPU v7x, 32 devices: a whole 2x2x4 slice. The times are simulated.
32 devices in a mesh: lat: 8 (over z, x), lon: 4 (over y, core).
Axes of the slice: x: 2, y: 2, z: 4, core: 2. Of those that a mesh axis runs over, the one named last changes fastest.
Arguments:
- inputs: bfloat16 [16, 64, 360, 256], P(None, 'lat', 'lon'), may hold values from -6 to 6
- legendre_forward: bfloat16 [96, 96, 64], P('lat'), may hold values from -0.75 to 0.75
- legendre_inverse: bfloat16 [96, 64, 96], P('lat'), may hold values from -0.625 to 0.625
- spectral_weight: float32 [2, 96, 256], P(None, None, 'lon'), may hold values from -5 to 5
- skip_weight: bfloat16 [256, 256], replicated, may hold values from -0.375 to 0.375
- gain_first: float32 [256], replicated, may hold values from 0.5 to 1.5
- bias_first: float32 [256], replicated, may hold values from -2 to 2
- gain_second: float32 [256], replicated, may hold values from 0.5 to 1.5
- bias_second: float32 [256], replicated, may hold values from -2 to 2
- mlp_in: bfloat16 [256, 512], replicated, may hold values from -0.375 to 0.375
- mlp_in_bias: float32 [512], replicated, may hold values from -2 to 2
- mlp_out: bfloat16 [512, 256], replicated, may hold values from -0.25 to 0.25
- mlp_out_bias: float32 [256], replicated, may hold values from -2 to 2
- cotangent: bfloat16 [16, 64, 360, 256], P(None, 'lat', 'lon'), may hold values from -6 to 6
Outputs:
- output: bfloat16 [16, 64, 360, 256], P(None, 'lat', 'lon')
- grad_inputs: float32 [16, 64, 360, 256], P(None, 'lat', 'lon')
- grad_spectral: float32 [2, 96, 256], P(None, None, 'lon')
- grad_skip: float32 [256, 256], replicated
- grad_gain_first: float32 [256], replicated
- grad_bias_first: float32 [256], replicated
- grad_gain_second: float32 [256], replicated
- grad_bias_second: float32 [256], replicated
- grad_mlp_in: float32 [256, 512], replicated
- grad_mlp_in_bias: float32 [512], replicated
- grad_mlp_out: float32 [512, 256], replicated
- grad_mlp_out_bias: float32 [256], replicated
All inputs are finite; a program needn't handle non-finite values.
Results may differ from a plain program's by a relative error of at most 0.012.
Values may be sent and summed in bfloat16 or wider, within the bound.
A program may use at most 256 MiB of HBM per device.

v0:
```python
import math

import jax
import jax.numpy as jnp
from jax import lax
from jax.sharding import PartitionSpec as P

epsilon = 1e-05


def fourier_tables(points, orders):
    longit = jnp.arange(points, dtype=jnp.int32)
    waves = jnp.arange(orders, dtype=jnp.int32)
    phase = (waves[:, None] * longit[None, :] % points).astype(jnp.float32) * (
        2.0 * math.pi / points
    )
    cosine = jnp.cos(phase)
    sine = jnp.sin(phase)
    factor = jnp.where(waves == 0, 1.0, 2.0).astype(jnp.float32)[:, None]
    forward = jnp.concatenate([cosine, -sine], axis=0).T
    inverse = jnp.stack([factor * cosine, -factor * sine], axis=0)
    return (forward.astype(jnp.bfloat16), inverse.astype(jnp.bfloat16))


def layer_norm(values, gain, bias):
    center = values - jnp.mean(values, axis=-1, keepdims=True)
    spread = jnp.mean(center * center, axis=-1, keepdims=True)
    scaled = lax.rsqrt(spread + epsilon)
    normal = center * scaled
    return (normal * gain + bias, normal, scaled)


def norm_back(grad_out, normal, scaled, gain):
    grad_norm = grad_out * gain
    inner = jnp.mean(grad_norm, axis=-1, keepdims=True)
    cross = jnp.mean(grad_norm * normal, axis=-1, keepdims=True)
    grad_value = scaled * (grad_norm - inner - normal * cross)
    return (
        grad_value,
        jnp.sum(grad_out * normal, axis=(0, 1, 2)),
        jnp.sum(grad_out, axis=(0, 1, 2)),
    )


def per_device(
    inputs,
    legendre_forward,
    legendre_inverse,
    spectral_weight,
    skip_weight,
    gain_first,
    bias_first,
    gain_second,
    bias_second,
    mlp_in,
    mlp_in_bias,
    mlp_out,
    mlp_out_bias,
    cotangent,
):
    batch, lat_rows, lon_cols, width = inputs.shape
    points = lon_cols * lax.axis_size("lon")
    slab_size = legendre_forward.shape[0]
    orders = slab_size * lax.axis_size("lat")
    degrees = legendre_forward.shape[1]
    narrow = width // lax.axis_size("lon")
    fourier_forward, fourier_inverse = fourier_tables(points, orders)
    order_index = lax.axis_index("lat") * slab_size + jnp.arange(slab_size, dtype=jnp.int32)
    degree_index = jnp.arange(degrees, dtype=jnp.int32)
    zero_low = jnp.zeros((), jnp.bfloat16)
    analysis = jnp.where(
        degree_index[None, :, None] >= order_index[:, None, None], legendre_forward, zero_low
    )
    synthesis = jnp.where(
        degree_index[None, None, :] >= order_index[:, None, None], legendre_inverse, zero_low
    )
    weight_real = spectral_weight[0].T[None, :, None, :]
    weight_imag = spectral_weight[1].T[None, :, None, :]
    inputs_full = inputs.astype(jnp.float32)
    normed, normal_one, scale_one = layer_norm(inputs_full, gain_first, bias_first)
    normed_low = normed.astype(jnp.bfloat16)
    spectrum = (
        jnp.einsum(
            "bjnc,nk->bjck",
            lax.all_to_all(normed_low, "lon", split_axis=3, concat_axis=2, tiled=True),
            fourier_forward,
            preferred_element_type=jnp.float32,
        )
        / points
    )
    spectrum = spectrum.astype(jnp.bfloat16).reshape(batch, lat_rows, narrow, 2, orders)
    slab = lax.all_to_all(spectrum, "lat", split_axis=4, concat_axis=1, tiled=True)
    coeffs = jnp.einsum("bjcrm,mlj->bcrml", slab, analysis, preferred_element_type=jnp.float32)
    filt_real = weight_real * coeffs[:, :, 0] - weight_imag * coeffs[:, :, 1]
    filt_imag = weight_real * coeffs[:, :, 1] + weight_imag * coeffs[:, :, 0]
    filtered = jnp.stack([filt_real, filt_imag], axis=2).astype(jnp.bfloat16)
    synth = jnp.einsum(
        "bcrml,mjl->bjcrm", filtered, synthesis, preferred_element_type=jnp.float32
    ).astype(jnp.bfloat16)
    synth_rows = lax.all_to_all(synth, "lat", split_axis=1, concat_axis=4, tiled=True)
    spatial = jnp.einsum(
        "bjcrm,rmn->bjnc", synth_rows, fourier_inverse, preferred_element_type=jnp.float32
    ).astype(jnp.bfloat16)
    spatial_grid = lax.all_to_all(spatial, "lon", split_axis=2, concat_axis=3, tiled=True)
    mixed = spatial_grid.astype(jnp.float32) + jnp.einsum(
        "bjnc,cd->bjnd", normed_low, skip_weight, preferred_element_type=jnp.float32
    )
    resid = inputs_full + mixed
    second, normal_two, scale_two = layer_norm(resid, gain_second, bias_second)
    second_low = second.astype(jnp.bfloat16)
    pre = (
        jnp.einsum("bjnc,ch->bjnh", second_low, mlp_in, preferred_element_type=jnp.float32)
        + mlp_in_bias
    )
    act_low = jax.nn.gelu(pre).astype(jnp.bfloat16)
    output = (
        resid
        + jnp.einsum("bjnh,hc->bjnc", act_low, mlp_out, preferred_element_type=jnp.float32)
        + mlp_out_bias
    )
    grad_out_weight = jnp.einsum(
        "bjnh,bjnc->hc", act_low, cotangent, preferred_element_type=jnp.float32
    )
    grad_out_bias = jnp.sum(cotangent.astype(jnp.float32), axis=(0, 1, 2))
    grad_act = jnp.einsum("bjnc,hc->bjnh", cotangent, mlp_out, preferred_element_type=jnp.float32)
    unused, gelu_pull = jax.vjp(jax.nn.gelu, pre)
    grad_pre = gelu_pull(grad_act)[0].astype(jnp.bfloat16)
    grad_in_weight = jnp.einsum(
        "bjnc,bjnh->ch", second_low, grad_pre, preferred_element_type=jnp.float32
    )
    grad_in_bias = jnp.sum(grad_pre.astype(jnp.float32), axis=(0, 1, 2))
    grad_second = jnp.einsum("bjnh,ch->bjnc", grad_pre, mlp_in, preferred_element_type=jnp.float32)
    grad_norm_two, grad_gain_two, grad_bias_two = norm_back(
        grad_second, normal_two, scale_two, gain_second
    )
    grad_resid = cotangent.astype(jnp.float32) + grad_norm_two
    grad_mixed = grad_resid.astype(jnp.bfloat16)
    grad_skip_weight = jnp.einsum(
        "bjnc,bjnd->cd", normed_low, grad_mixed, preferred_element_type=jnp.float32
    )
    grad_normed = jnp.einsum(
        "bjnd,cd->bjnc", grad_mixed, skip_weight, preferred_element_type=jnp.float32
    )
    grad_rows = lax.all_to_all(grad_mixed, "lon", split_axis=3, concat_axis=2, tiled=True)
    grad_synth = jnp.einsum(
        "bjnc,rmn->bjcrm", grad_rows, fourier_inverse, preferred_element_type=jnp.float32
    ).astype(jnp.bfloat16)
    grad_slab = lax.all_to_all(grad_synth, "lat", split_axis=4, concat_axis=1, tiled=True)
    grad_filtered = jnp.einsum(
        "bjcrm,mjl->bcrml", grad_slab, synthesis, preferred_element_type=jnp.float32
    )
    grad_real_part = grad_filtered[:, :, 0]
    grad_imag_part = grad_filtered[:, :, 1]
    kept_real = coeffs[:, :, 0]
    kept_imag = coeffs[:, :, 1]
    spec_real = jnp.sum(grad_real_part * kept_real + grad_imag_part * kept_imag, axis=(0, 2)).T
    spec_imag = jnp.sum(grad_imag_part * kept_real - grad_real_part * kept_imag, axis=(0, 2)).T
    grad_spec = lax.psum(jnp.stack([spec_real, spec_imag], axis=0), "lat")
    coeff_real = weight_real * grad_real_part + weight_imag * grad_imag_part
    coeff_imag = weight_real * grad_imag_part - weight_imag * grad_real_part
    grad_coeffs = jnp.stack([coeff_real, coeff_imag], axis=2).astype(jnp.bfloat16)
    grad_spectrum = jnp.einsum(
        "bcrml,mlj->bjcrm", grad_coeffs, analysis, preferred_element_type=jnp.float32
    ).astype(jnp.bfloat16)
    grad_bands = lax.all_to_all(grad_spectrum, "lat", split_axis=1, concat_axis=4, tiled=True)
    grad_bands = grad_bands.reshape(batch, lat_rows, narrow, 2 * orders)
    grad_sent = (
        jnp.einsum("bjck,nk->bjnc", grad_bands, fourier_forward, preferred_element_type=jnp.float32)
        / points
    ).astype(jnp.bfloat16)
    grad_grid = lax.all_to_all(grad_sent, "lon", split_axis=2, concat_axis=3, tiled=True)
    grad_normed = grad_normed + grad_grid.astype(jnp.float32)
    grad_norm_one, grad_gain_one, grad_bias_one = norm_back(
        grad_normed, normal_one, scale_one, gain_first
    )
    grad_inputs = grad_resid + grad_norm_one
    totals = lax.psum(
        (
            grad_skip_weight,
            grad_in_weight,
            grad_in_bias,
            grad_out_weight,
            grad_out_bias,
            grad_gain_one,
            grad_bias_one,
            grad_gain_two,
            grad_bias_two,
        ),
        ("lat", "lon"),
    )
    return (
        output.astype(jnp.bfloat16),
        grad_inputs,
        grad_spec,
        totals[0],
        totals[5],
        totals[6],
        totals[7],
        totals[8],
        totals[1],
        totals[2],
        totals[3],
        totals[4],
    )


def solution(mesh):
    placed = (
        P(None, "lat", "lon", None),
        P("lat", None, None),
        P("lat", None, None),
        P(None, None, "lon"),
        P(),
        P(),
        P(),
        P(),
        P(),
        P(),
        P(),
        P(),
        P(),
        P(None, "lat", "lon", None),
    )
    return jax.shard_map(
        per_device,
        mesh=mesh,
        in_specs=placed,
        out_specs=(
            P(None, "lat", "lon", None),
            P(None, "lat", "lon", None),
            P(None, None, "lon"),
            P(),
            P(),
            P(),
            P(),
            P(),
            P(),
            P(),
            P(),
            P(),
        ),
        check_vma=False,
    )
```

profile of v0, /device:TPU:0, one launch (start us, length us, event | category | flops | bytes accessed | tf_op | source)
XLA Modules:
  0.0 1328.2 jit_solution(23835003871361064)
XLA Ops:
  43.7 93.2 %all-to-all-done = bf16[16,8,90,256]{2,1,0,3:T(8,128)(2,1)} async-done(((bf16[16,8,90,256]{2,1,0,3:T(8,128)(2,1)}), bf16[16,8,90,256]{2,1,0,3:T(8,128)(2,1)}, u32[]{:S(2)}, u32[]{:S(2)}) %all-to-all-start) | async-done | bytes 5898272 | tf_op jit(solution)/shard_map/all_to_all | solution.py:85
  149.1 13.7 %all_to_all.93 = bf16[16,8,360,64]{2,3,1,0:T(8,128)(2,1)} reshape(bf16[16,8,4,90,64]{3,2,4,1,0:T(4,128)(2,1)} %copy.67) | data formatting | bytes 11796480 | tf_op jit(solution)/shard_map/all_to_all | solution.py:85
  177.4 13.2 copy.68
  207.3 69.6 %all-to-all-done.1 = bf16[8,2,98304]{2,1,0:T(2,128)(2,1)S(1)} async-done(((bf16[8,2,98304]{2,1,0:T(2,128)(2,1)}), bf16[8,2,98304]{2,1,0:T(2,128)(2,1)S(1)}, u32[]{:S(2)}, u32[]{:S(2)}) %all-to-all-start.1) | async-done | bytes 3145760 | tf_op jit(solution)/shard_map/all_to_all | solution.py:92
  299.9 16.9 %copy.167 = bf16[16,64,64,2,12]{2,3,0,4,1:T(2,128)(2,1)} copy(bf16[16,64,64,2,12]{2,1,3,0,4:T(8,128)(2,1)S(1)} %convert_bitcast_fusion.1) | data formatting | bytes 6291456 | tf_op jit(solution)/shard_map/convert_element_type | solution.py:99
  331.1 69.5 %all-to-all-done.2 = bf16[8,2,98304]{2,1,0:T(2,128)(2,1)S(1)} async-done(((bf16[8,2,98304]{2,1,0:T(2,128)(2,1)}), bf16[8,2,98304]{2,1,0:T(2,128)(2,1)S(1)}, u32[]{:S(2)}, u32[]{:S(2)}) %all-to-all-start.2) | async-done | bytes 3145760 | tf_op jit(solution)/shard_map/all_to_all | solution.py:100
  419.2 18.3 %copy.75 = bf16[16,8,360,64]{3,1,0,2:T(8,128)(2,1)} copy(bf16[16,8,360,64]{2,3,1,0:T(8,128)(2,1)} %fusion.22) | data formatting | bytes 11796480 | tf_op jit(solution)/shard_map/convert_element_type | solution.py:103
  449.6 73.2 %all_to_all.123 = bf16[4,2,368640]{2,1,0:T(2,128)(2,1)} all-to-all(bf16[4,2,368640]{2,1,0:T(2,128)(2,1)} %reshape.272), channel_id=1, replica_groups=mesh['lat'=8,'lon'=4] {'lon'}, dimensions={0} | all-to-all | bytes 11796480 | tf_op jit(solution)/shard_map/all_to_all | solution.py:104
  534.9 18.4 %copy.76 = f32[16,8,4,90,64]{3,4,2,1,0:T(8,128)} copy(bf16[16,8,4,90,64]{4,1,0,3,2:T(8,128)(2,1)} %bitcast.182) | data formatting | bytes 17694720 | tf_op jit(solution)/shard_map/convert_element_type | solution.py:105
  553.3 16.5 %copy.77 = f32[16,8,90,256]{3,2,1,0:T(8,128)} copy(f32[16,8,90,256]{2,3,1,0:T(8,128)} %bitcast.180) | data formatting | bytes 23592960 | tf_op jit(solution)/shard_map/convert_element_type | solution.py:105
  569.8 13.7 %fusion.107 = (f32[16,8,90]{2,1,0:T(8,128)S(1)}, f32[16,8,90,256]{3,2,1,0:T(8,128)S(1)}) fusion(f32[16,8,90,256]{3,2,1,0:T(8,128)} %copy.77, bf16[256,256]{1,0:T(8,128)(2,1)S(1)} %copy-done.45, f32[256]{0:T(256)S(1)} %copy-done.41, f32[256]{0:T(256)S(1)} %copy-done.37, f32[16,8,90]{2,1,0:T(8,128)S(1)} %copy-done.16, ...), kind=kOutput, calls=%fused_computation.146 | convolution fusion | flops 1539429120 | bytes 29762560 | tf_op jit(solution)/shard_map/bjnc,cd->bjnd/dot_general | solution.py:105
  587.9 17.8 %multiply_convert_fusion = (bf16[16,8,90,512]{3,2,1,0:T(8,128)(2,1)}, f32[16,8,90,512]{3,2,1,0:T(8,128)}) fusion(f32[512]{0:T(512)S(1)} %copy-done.47, bf16[256,512]{1,0:T(8,128)(2,1)S(1)} %copy-done, f32[16,8,90,256]{3,2,1,0:T(8,128)S(1)} %get-tuple-element.78, f32[256]{0:T(256)S(1)} %copy-done.48, f32[256]{0:T(256)S(1)} %copy-done.39, ...), kind=kOutput, calls=%fused_computation.10 | convolution fusion | flops 3093626880 | bytes 47544320 | tf_op jit(solution)/shard_map/bjnc,ch->bjnh/dot_general | solution.py:112
  605.7 27.7 %convert_reduce_fusion = (f32[512]{0:T(512)}, bf16[16,8,90,512]{3,2,1,0:T(8,128)(2,1)}) fusion(f32[16,8,90,512]{3,2,1,0:T(8,128)} %get-tuple-element.80, f32[512]{0:T(512)S(1)} %copy-done.47, bf16[512,256]{1,0:T(8,128)(2,1)S(1)} %copy-done.30, bf16[16,8,90,256]{3,1,2,0:T(8,128)(2,1)} %param.27), kind=kOutput, calls=%fused_computation.9 | convolution fusion | flops 3155557888 | bytes 41553920 | tf_op jit(solution)/shard_map/bjnc,hc->bjnh/dot_general | solution.py:125
  633.4 12.5 multiply_reduce_fusion
  671.9 97.6 %all_to_all.124 = bf16[16,8,90,256]{2,1,0,3:T(8,128)(2,1)S(1)} all-to-all(bf16[16,8,90,256]{2,1,0,3:T(8,128)(2,1)} %copy.80), channel_id=1, replica_groups=mesh['lat'=8,'lon'=4] {'lon'}, dimensions={3} | all-to-all | bytes 11796480 | tf_op jit(solution)/shard_map/all_to_all | solution.py:144
  776.8 13.7 %reshape.263 = bf16[16,8,360,64,1]{2,3,1,0,4:T(8,128)(2,1)} reshape(bf16[16,8,4,90,64]{3,2,4,1,0:T(4,128)(2,1)} %copy.82) | data formatting | bytes 11796480 | tf_op jit(solution)/shard_map/all_to_all | solution.py:144
  797.7 15.8 %copy.83 = bf16[16,8,64,2,96]{2,3,1,0,4:T(2,128)(2,1)} copy(bf16[16,8,64,2,96]{4,2,3,1,0:T(8,128)(2,1)} %fusion.61) | data formatting | bytes 6291456 | tf_op jit(solution)/shard_map/convert_element_type | solution.py:147
  821.2 74.0 %all_to_all.125 = bf16[8,2,98304]{2,1,0:T(2,128)(2,1)} all-to-all(bf16[8,2,98304]{2,1,0:T(2,128)(2,1)S(1)} %reshape.274), channel_id=1, replica_groups=mesh['lat'=8,'lon'=4] {'lat'}, dimensions={0} | all-to-all | bytes 6291456 | tf_op jit(solution)/shard_map/all_to_all | solution.py:148
  927.7 16.9 %copy.166 = bf16[16,64,64,2,12]{2,3,0,4,1:T(2,128)(2,1)} copy(bf16[16,64,64,2,12]{2,1,3,0,4:T(8,128)(2,1)S(1)} %convert_bitcast_fusion) | data formatting | bytes 6291456 | tf_op jit(solution)/shard_map/convert_element_type | solution.py:164
  952.3 73.9 %all_to_all.126 = bf16[8,2,98304]{2,1,0:T(2,128)(2,1)} all-to-all(bf16[8,2,98304]{2,1,0:T(2,128)(2,1)S(1)} %reshape.276), channel_id=1, replica_groups=mesh['lat'=8,'lon'=4] {'lat'}, dimensions={0} | all-to-all | bytes 6291456 | tf_op jit(solution)/shard_map/all_to_all | solution.py:165
  1047.3 18.3 %copy.90 = bf16[16,8,360,64]{3,1,0,2:T(8,128)(2,1)} copy(bf16[16,8,360,64]{2,3,1,0:T(8,128)(2,1)} %fusion.21) | data formatting | bytes 11796480 | tf_op jit(solution)/shard_map/convert_element_type | solution.py:170
  1065.5 12.2 reshape.278
  1083.6 14.4 %add_convert_fusion = bf16[16,8,90,256]{3,2,1,0:T(8,128)(2,1)} fusion(f32[16,8,90,256]{3,2,1,0:T(8,128)} %copy-done.2, f32[256]{0:T(256)S(1)} %copy-done.36, bf16[16,8,90,512]{3,2,1,0:T(8,128)(2,1)} %get-tuple-element.79, bf16[512,256]{1,0:T(8,128)(2,1)S(1)} %copy-done.31), kind=kOutput, calls=%fused_computation.34 | convolution fusion | flops 3028746240 | bytes 29754368 | tf_op jit(solution)/shard_map/bjnh,hc->bjnc/dot_general | solution.py:118
  1107.7 13.5 %convolution_bitcast_fusion.1 = f32[256,256]{1,0:T(8,128)} fusion(bf16[16,8,90,256]{3,2,1,0:T(8,128)(2,1)} %fusion.104, f32[256]{0:T(256)S(1)} %copy-done.42, f32[256]{0:T(256)S(1)} %copy-done.38, f32[16,8,90]{2,1,0:T(8,128)S(1)} %copy-done.17, f32[16,8,90]{2,1,0:T(8,128)S(1)} %copy-done.7, bf16[16,8,90,256]{3,1,2,0:T(8,128)(2,1)S(1)} %bitcast.177), kind=kOutput, calls=%fused_computation.81 | convolution fusion | flops 1527644160 | bytes 12152832 | tf_op jit(solution)/shard_map/bjnc,bjnd->cd/dot_general | solution.py:138
  1128.7 14.7 %convolution_bitcast_fusion = f32[256,512]{1,0:T(8,128)} fusion(bf16[16,8,90,512]{3,2,1,0:T(8,128)(2,1)} %get-tuple-element.84, f32[16,8,90,256]{3,2,1,0:T(8,128)S(1)} %bitcast.173, f32[256]{0:T(256)S(1)} %copy-done.49, f32[256]{0:T(256)S(1)} %copy-done.39, f32[16,8,90]{2,1,0:T(8,128)S(1)} %add_rsqrt_fusion, f32[16,8,90]{2,1,0:T(8,128)S(1)} %broadcast_multiply_fusion.4), kind=kOutput, calls=%fused_computation.80 | convolution fusion | flops 3034644480 | bytes 24211456 | tf_op jit(solution)/shard_map/bjnc,bjnh->ch/dot_general | solution.py:128
  1143.5 36.5 %psum.70 = f32[2,96,64]{1,2,0:T(8,128)} all-reduce(f32[2,96,64]{1,2,0:T(8,128)S(1)} %pad_maximum_fusion), channel_id=1, replica_groups=mesh['lat'=8,'lon'=4] {'lat'}, use_global_device_ids=true, to_apply=%region_10.11 | all-reduce | flops 12288 | bytes 98304 | tf_op jit(solution)/shard_map/psum | solution.py:158
  1192.0 18.5 %copy.91 = f32[16,8,4,90,64]{3,4,2,1,0:T(8,128)} copy(bf16[16,8,4,90,64]{4,1,0,3,2:T(8,128)(2,1)} %bitcast.183) | data formatting | bytes 17694720 | tf_op jit(solution)/shard_map/convert_element_type | solution.py:172
  1210.5 16.5 %copy.92 = f32[16,8,90,256]{3,2,1,0:T(8,128)} copy(f32[16,8,90,256]{2,3,1,0:T(8,128)} %bitcast.181) | data formatting | bytes 23592960 | tf_op jit(solution)/shard_map/convert_element_type | solution.py:172
  1227.1 13.6 %fusion.19 = (f32[256]{0:T(256)S(1)}, f32[16,8,90]{2,1,0:T(8,128)S(1)}, f32[16,8,90]{2,1,0:T(8,128)S(1)}, f32[256]{0:T(256)S(1)}, f32[16,8,90,256]{3,2,1,0:T(8,128)S(1)}) fusion(f32[16,8,90]{2,1,0:T(8,128)S(1)} %copy-done.17, f32[16,8,90]{2,1,0:T(8,128)S(1)} %copy-done.7, bf16[16,8,90,256]{3,1,2,0:T(8,128)(2,1)} %param.14, f32[256]{0:T(256)S(1)} %copy-done.38, ...), kind=kOutput, calls=%fused_computation.28 | convolution fusion | flops 1542366208 | bytes 35707904 | tf_op jit(solution)/shard_map/bjnd,cd->bjnc/dot_general | solution.py:141
  1240.7 19.4 %convert_reduce_fusion.2 = (f32[256]{0:T(256)S(1)}, f32[16,8,90,256]{3,2,1,0:T(8,128)}) fusion(bf16[16,8,90,256]{3,1,2,0:T(8,128)(2,1)} %param.27, f32[16,8,90]{2,1,0:T(8,128)S(1)} %broadcast_multiply_fusion, f32[16,8,90]{2,1,0:T(8,128)S(1)} %copy-done.7, bf16[16,8,90,256]{3,1,2,0:T(8,128)(2,1)S(1)} %bitcast.179, ...), kind=kLoop, calls=%fused_computation.14 | loop fusion | flops 56033024 | bytes 59354112 | tf_op jit(solution)/shard_map/reduce_sum | solution.py:124
  1260.1 18.5 %copy.95 = f32[16,8,90,256]{3,1,2,0:T(8,128)} copy(f32[16,8,90,256]{3,2,1,0:T(8,128)} %get-tuple-element.74) | data formatting | bytes 23592960
  1278.7 37.1 %all-reduce = (f32[256]{0:T(256)}, f32[256]{0:T(256)}, f32[256]{0:T(256)}, f32[256]{0:T(256)}, f32[512]{0:T(512)}, /*index=5*/f32[256]{0:T(256)}) all-reduce(f32[256]{0:T(256)S(1)} %get-tuple-element.52, f32[256]{0:T(256)S(1)} %get-tuple-element.57, f32[256]{0:T(256)S(1)} %copy-done.43, ...), channel_id=1, replica_groups=mesh['lat'=8,'lon'=4] {'lat','lon'}, use_global_device_ids=true, to_apply=%region_13.14 | all-reduce | flops 1792 | bytes 14336 | tf_op jit(solution)/shard_map/psum | solution.py:177
  (192 shorter events, 313.8 us)
Async XLA Ops:
  7.2 580.7 %copy-start = (bf16[256,512]{1,0:T(8,128)(2,1)S(1)}, bf16[256,512]{1,0:T(8,128)(2,1)}, u32[]{:S(2)}) copy-start(bf16[256,512]{1,0:T(8,128)(2,1)} %param.23) | copy-start | bytes 786436
  12.3 557.5 %copy-start.6 = (f32[16,8,90]{2,1,0:T(8,128)}, f32[16,8,90]{2,1,0:T(8,128)S(1)}, u32[]{:S(2)}) copy-start(f32[16,8,90]{2,1,0:T(8,128)S(1)} %broadcast_multiply_fusion.5) | copy-start | bytes 138244
  37.4 99.5 %all-to-all-start = ((bf16[16,8,90,256]{2,1,0,3:T(8,128)(2,1)}), bf16[16,8,90,256]{2,1,0,3:T(8,128)(2,1)}, u32[]{:S(2)}, u32[]{:S(2)}) async-start(bf16[16,8,90,256]{2,1,0,3:T(8,128)(2,1)} %copy.65), calls=%async_computation | async-start | bytes 16777216 | tf_op jit(solution)/shard_map/all_to_all | solution.py:85
  43.7 119.1 %copy-start.22 = (bf16[96,360]{1,0:T(8,128)(2,1)}, bf16[96,360]{1,0:T(8,128)(2,1)S(1)}, u32[]{:S(2)}) copy-start(bf16[96,360]{1,0:T(8,128)(2,1)S(1)} %get-tuple-element.85) | copy-start | bytes 207364
  43.7 119.1 %copy-start.24 = (bf16[96,360]{1,0:T(8,128)(2,1)}, bf16[96,360]{1,0:T(8,128)(2,1)S(1)}, u32[]{:S(2)}) copy-start(bf16[96,360]{1,0:T(8,128)(2,1)S(1)} %get-tuple-element.86) | copy-start | bytes 207364
  199.6 77.3 %all-to-all-start.1 = ((bf16[8,2,98304]{2,1,0:T(2,128)(2,1)}), bf16[8,2,98304]{2,1,0:T(2,128)(2,1)S(1)}, u32[]{:S(2)}, u32[]{:S(2)}) async-start(bf16[8,2,98304]{2,1,0:T(2,128)(2,1)} %reshape.268), calls=%async_computation.1 | async-start | bytes 6291456 | tf_op jit(solution)/shard_map/all_to_all | solution.py:92
  206.5 87.1 %copy-start.34 = (pred[12,96]{1,0:T(8,128)(4,1)}, pred[12,96]{1,0:T(8,128)(4,1)S(1)}, u32[]{:S(2)}) copy-start(pred[12,96]{1,0:T(8,128)(4,1)S(1)} %iota_compare_fusion) | copy-start | bytes 3460
  207.3 80.0 %copy-start.26 = (f32[64,96]{1,0:T(8,128)}, f32[64,96]{1,0:T(8,128)S(1)}, u32[]{:S(2)}) copy-start(f32[64,96]{1,0:T(8,128)S(1)} %get-tuple-element.75) | copy-start | bytes 73732
  207.3 80.0 %copy-start.28 = (f32[64,96]{1,0:T(8,128)}, f32[64,96]{1,0:T(8,128)S(1)}, u32[]{:S(2)}) copy-start(f32[64,96]{1,0:T(8,128)S(1)} %get-tuple-element.76) | copy-start | bytes 73732
  325.7 74.9 %all-to-all-start.2 = ((bf16[8,2,98304]{2,1,0:T(2,128)(2,1)}), bf16[8,2,98304]{2,1,0:T(2,128)(2,1)S(1)}, u32[]{:S(2)}, u32[]{:S(2)}) async-start(bf16[8,2,98304]{2,1,0:T(2,128)(2,1)} %reshape.270), calls=%async_computation.2 | async-start | bytes 6291456 | tf_op jit(solution)/shard_map/all_to_all | solution.py:100
  331.1 88.1 %copy-start.11 = (bf16[1,96,360]{2,1,0:T(8,128)(2,1)}, bf16[1,96,360]{2,1,0:T(8,128)(2,1)S(1)}, u32[]{:S(2)}) copy-start(bf16[1,96,360]{2,1,0:T(8,128)(2,1)S(1)} %get-tuple-element.87) | copy-start | bytes 207364
  583.5 62.5 %copy-start.2 = (f32[16,8,90,256]{3,2,1,0:T(8,128)}, f32[16,8,90,256]{3,2,1,0:T(8,128)S(1)}, u32[]{:S(2)}) copy-start(f32[16,8,90,256]{3,2,1,0:T(8,128)S(1)} %get-tuple-element.78) | copy-start | bytes 35389444
  769.5 21.0 %copy-start.12 = (bf16[1,96,360]{2,1,0:T(8,128)(2,1)S(1)}, bf16[1,96,360]{2,1,0:T(8,128)(2,1)}, u32[]{:S(2)}) copy-start(bf16[1,96,360]{2,1,0:T(8,128)(2,1)} %copy-done.11) | copy-start | bytes 207364
  769.5 21.0 %copy-start.14 = (bf16[1,96,360]{2,1,0:T(8,128)(2,1)S(1)}, bf16[1,96,360]{2,1,0:T(8,128)(2,1)}, u32[]{:S(2)}) copy-start(bf16[1,96,360]{2,1,0:T(8,128)(2,1)} %get-tuple-element.88) | copy-start | bytes 207364
  1065.5 18.0 %copy-start.31 = (bf16[512,256]{1,0:T(8,128)(2,1)S(1)}, bf16[512,256]{1,0:T(8,128)(2,1)}, u32[]{:S(2)}) copy-start(bf16[512,256]{1,0:T(8,128)(2,1)} %param.25) | copy-start | bytes 786436
  1065.5 18.0 %copy-start.36 = (f32[256]{0:T(256)S(1)}, f32[256]{0:T(256)}, u32[]{:S(2)}) copy-start(f32[256]{0:T(256)} %param.26) | copy-start | bytes 3076
  1077.8 29.9 %slice-start.6 = ((s8[5898240]{0:T(1024)(128)(4,1)}), s8[1703936]{0:T(1024)(128)(4,1)S(1)}, s32[]{:S(2)}) async-start(s8[5898240]{0:T(1024)(128)(4,1)} %bitcast.176), calls=%async_computation.15 | async-start | bytes 3407872
  1077.8 102.2 %all-to-all-start.7 = ((bf16[4,2,368640]{2,1,0:T(2,128)(2,1)}), bf16[4,2,368640]{2,1,0:T(2,128)(2,1)}, u32[]{:S(2)}, u32[]{:S(2)}) async-start(bf16[4,2,368640]{2,1,0:T(2,128)(2,1)} %reshape.278), calls=%async_computation.7 | async-start | bytes 11796480 | tf_op jit(solution)/shard_map/all_to_all | solution.py:171
  1083.1 232.7 %all-reduce.4.cloned.1.call-start = ((), (), s32[]{:S(2)}) async-start(), calls=%async_computation.8 | async-start | bytes 2621440 | tf_op jit(solution)/shard_map/psum | solution.py:177
  1083.6 24.1 %slice-start.7 = ((s8[5898240]{0:T(1024)(128)(4,1)}), s8[4194304]{0:T(1024)(128)(4,1)S(1)}, s32[]{:S(2)}) async-start(s8[5898240]{0:T(1024)(128)(4,1)} %bitcast.176), calls=%async_computation.16 | async-start | bytes 8388608
  1083.6 24.1 %copy-start.7 = (f32[16,8,90]{2,1,0:T(8,128)S(1)}, f32[16,8,90]{2,1,0:T(8,128)}, u32[]{:S(2)}) copy-start(f32[16,8,90]{2,1,0:T(8,128)} %copy-done.6) | copy-start | bytes 138244
  1083.6 24.1 %copy-start.17 = (f32[16,8,90]{2,1,0:T(8,128)S(1)}, f32[16,8,90]{2,1,0:T(8,128)}, u32[]{:S(2)}) copy-start(f32[16,8,90]{2,1,0:T(8,128)} %copy-done.15) | copy-start | bytes 138244
  1083.6 24.1 %copy-start.38 = (f32[256]{0:T(256)S(1)}, f32[256]{0:T(256)}, u32[]{:S(2)}) copy-start(f32[256]{0:T(256)} %param.19) | copy-start | bytes 3076
  1083.6 24.1 %copy-start.42 = (f32[256]{0:T(256)S(1)}, f32[256]{0:T(256)}, u32[]{:S(2)}) copy-start(f32[256]{0:T(256)} %param.20) | copy-start | bytes 3076
  1098.1 23.1 %slice-start.10 = ((s8[5898240]{0:T(1024)(128)(4,1)}), s8[4194304]{0:T(1024)(128)(4,1)S(1)}, s32[]{:S(2)}) async-start(s8[5898240]{0:T(1024)(128)(4,1)} %bitcast.197), calls=%async_computation.19 | async-start | bytes 8388608
  1107.7 21.0 %slice-start = ((s8[12582912]{0:T(1024)(128)(4,1)}), s8[4194304]{0:T(1024)(128)(4,1)S(1)}, s32[]{:S(2)}) async-start(s8[12582912]{0:T(1024)(128)(4,1)} %bitcast.172), calls=%async_computation.9 | async-start | bytes 8388608
  1107.7 20.9 %slice-start.1 = ((s8[12582912]{0:T(1024)(128)(4,1)}), s8[4194304]{0:T(1024)(128)(4,1)S(1)}, s32[]{:S(2)}) async-start(s8[12582912]{0:T(1024)(128)(4,1)} %bitcast.172), calls=%async_computation.10 | async-start | bytes 8388608
  1210.5 30.2 %slice-start.8 = ((s8[5898240]{0:T(1024)(128)(4,1)}), s8[1703936]{0:T(1024)(128)(4,1)S(1)}, s32[]{:S(2)}) async-start(s8[5898240]{0:T(1024)(128)(4,1)} %bitcast.178), calls=%async_computation.17 | async-start | bytes 3407872
  1260.1 18.6 %copy-start.40 = (f32[512]{0:T(512)S(1)}, f32[512]{0:T(512)}, u32[]{:S(2)}) copy-start(f32[512]{0:T(512)} %get-tuple-element.83) | copy-start | bytes 6148
  1260.1 18.5 %copy-start.43 = (f32[256]{0:T(256)S(1)}, f32[256]{0:T(256)}, u32[]{:S(2)}) copy-start(f32[256]{0:T(256)} %get-tuple-element.48) | copy-start | bytes 3076
  1260.1 18.5 %copy-start.44 = (f32[256]{0:T(256)S(1)}, f32[256]{0:T(256)}, u32[]{:S(2)}) copy-start(f32[256]{0:T(256)} %get-tuple-element.56) | copy-start | bytes 3076
  1260.1 61.1 %copy-start.1 = (bf16[256,512]{1,0:T(8,128)(2,1)S(1)}, bf16[256,512]{1,0:T(8,128)(2,1)}, u32[]{:S(2)}) copy-start(bf16[256,512]{1,0:T(8,128)(2,1)} %param.23) | copy-start | bytes 786436
  (35 other events, 378.2 us)
Sparse Core Ops, SparseCore 0:
  1143.5 131.9 all-reduce.3
where the time goes:
time: 1340 us; the launch traced here: 1330 us
  local copies, waits for them, and re-layouts  421 us (31%)
  blocking collectives  392 us (29%)
  waiting for transfers between devices  232 us (17%)
  matrix products  183 us (14%)
  other arithmetic  62.6 us (5%)
  starting transfers between devices  22.3 us (2%)
  between operations  15.1 us (1%)
    unnamed x141, local copies, waits for them, and re-layouts  155 us
    all_to_all x1, blocking collectives, per_device(): lax.all_to_all(grad_mixed, 'lon', split_axis=3, concat_axis=2, tiled=True)  97.6 us
    all_to_all x1, waiting for transfers between devices, per_device(): lax.all_to_all(normed_low, 'lon', split_axis=3, concat_axis=2, tiled=True)  93.2 us
    all_to_all x1, blocking collectives, per_device(): lax.all_to_all(grad_synth, 'lat', split_axis=4, concat_axis=1, tiled=True)  74 us
    all_to_all x1, blocking collectives, per_device(): lax.all_to_all(grad_spectrum, 'lat', split_axis=1, concat_axis=4, tiled=T...  73.9 us
    all_to_all x1, blocking collectives, per_device(): lax.all_to_all(spatial, 'lon', split_axis=2, concat_axis=3, tiled=True)  73.2 us
    all_to_all x1, waiting for transfers between devices, per_device(): lax.all_to_all(spectrum, 'lat', split_axis=4, concat_axis=1, tiled=True)  69.6 us
    all_to_all x1, waiting for transfers between devices, per_device(): lax.all_to_all(synth, 'lat', split_axis=1, concat_axis=4, tiled=True)  69.5 us
  transfers between devices with their start and end apart: 5, of which 3 were waited for; matrix products, arithmetic and copies ran while one was open for 12% of the time, Pallas kernels for 0%

commit v1 on v0

v1 whole, which is shorter than its diff:
```python
import functools
import math

import jax
import jax.numpy as jnp
import ml_dtypes
import numpy as np
from jax import lax
from jax.experimental import pallas as pl
from jax.experimental.pallas import tpu as pltpu
from jax.sharding import PartitionSpec as P

epsilon = 1e-05
LANES = 128
MESH = pl.DeviceIdType.MESH
root = math.sqrt(2.0 / math.pi)
cubic = 0.044715

OFFSET = {1: 0, 2: 1, 3: 2, 4: 3, 5: 4, 6: 4, 7: 5, 8: 6, 9: 6}
ORDER = (8, 5, 7, 1, 4, 2, 9, 6, 3)


def fourier_tables(points, lat):
    def build(orders):
        waves = np.arange(orders)
        phase = (waves[:, None] * np.arange(points)[None, :] % points).astype(np.float32)
        phase = phase * np.float32(2.0 * math.pi / points)
        cosine, sine = np.cos(phase), np.sin(phase)
        factor = np.where(waves == 0, 1.0, 2.0).astype(np.float32)[:, None]
        slab = orders // lat

        def arrange(parts):
            stacked = np.stack(parts).reshape(2, lat, slab, points).transpose(1, 0, 2, 3)
            return stacked.reshape(2 * orders, points).astype(ml_dtypes.bfloat16)

        forward = arrange([cosine, -sine])
        inverse = arrange([factor * cosine, -factor * sine])
        return forward, inverse

    return build


def row_tile(rows, most):
    fits = [t for t in range(16, most + 1, 16) if rows % t == 0]
    return fits[-1] if fits else rows


def norm_parts(values):
    center = values - jnp.mean(values, axis=-1, keepdims=True)
    spread = jnp.mean(center * center, axis=-1, keepdims=True)
    scaled = lax.rsqrt(spread + epsilon)
    return center * scaled, scaled


def norm_back(grad_out, normal, scaled, gain):
    grad_norm = grad_out * gain
    inner = jnp.mean(grad_norm, axis=-1, keepdims=True)
    cross = jnp.mean(grad_norm * normal, axis=-1, keepdims=True)
    return scaled * (grad_norm - inner - normal * cross)


def fold(values):
    rows, width = values.shape
    return jnp.sum(values.reshape(rows // 8, 8, width), axis=0)


def dot(a, b):
    return jnp.dot(a, b, preferred_element_type=jnp.float32)


def dot_t(a, b):
    return lax.dot_general(a, b, (((1,), (1,)), ((), ())), preferred_element_type=jnp.float32)


def t_dot(a, b):
    return lax.dot_general(a, b, (((0,), (0,)), ((), ())), preferred_element_type=jnp.float32)


def block_kernel(
    lat,
    lon,
    x_hbm,
    g_hbm,
    fwd_t,
    inv_t,
    inv,
    fwd,
    ana,
    ana_t,
    syn,
    syn_t,
    w_real,
    w_imag,
    skip,
    mlp_in,
    mlp_out,
    gain_one,
    bias_one,
    gain_two,
    bias_two,
    bias_in,
    bias_out,
    out_hbm,
    gin_hbm,
    grad_skip,
    grad_in,
    grad_out_t,
    sums_in,
    sums,
    grad_spec,
    x_all,
    normed,
    mixed,
    lon_a,
    lon_b,
    lat_a,
    lat_b,
    coeffs,
    send_2,
    send_3,
    send_4,
    send_6,
    send_7,
    send_8,
    wide,
    slim,
    g_buf,
    o_buf,
    i_buf,
    recv_sem,
    send_sem,
    x_sem,
    g_sem,
    o_sem,
    i_sem,
):
    batch, rows, width = x_hbm.shape
    halves = width // LANES
    group = lon // halves
    chunks = batch // group
    points = fwd_t.shape[1]
    slab, degrees, lats = ana.shape
    band = lats // lat
    block = 2 * slab * band
    waves = 2 * slab * lat
    my_lat, my_lon = lax.axis_index("lat"), lax.axis_index("lon")
    half_tile = row_tile(rows, 144)
    full_tile = row_tile(rows, 240)

    def lon_copy(stage, chunk, src, dst, peer):
        return pltpu.make_async_remote_copy(
            src_ref=src,
            dst_ref=dst,
            send_sem=send_sem.at[stage - 1],
            recv_sem=recv_sem.at[stage - 1, chunk],
            device_id={"lon": peer},
            device_id_type=MESH,
        )

    def lat_copy(stage, chunk, src, dst, peer):
        return pltpu.make_async_remote_copy(
            src_ref=src,
            dst_ref=dst,
            send_sem=send_sem.at[stage - 1],
            recv_sem=recv_sem.at[stage - 1, chunk],
            device_id={"lat": peer},
            device_id_type=MESH,
        )

    def own_copy(stage, chunk, src, dst):
        return pltpu.make_async_copy(src, dst, recv_sem.at[stage - 1, chunk])

    def landed(stage, chunk, whole):
        pltpu.make_async_copy(whole, whole, recv_sem.at[stage - 1, chunk]).wait()

    def sent(stage, part):
        lon_copy(stage, 0, part, part, my_lon).wait_send()

    def x_load(sample):
        return pltpu.make_async_copy(x_hbm.at[sample], x_all.at[sample], x_sem.at[sample])

    def g_load(sample, slot):
        return pltpu.make_async_copy(g_hbm.at[sample], g_buf.at[slot], g_sem.at[slot])

    def o_store(sample, slot):
        return pltpu.make_async_copy(o_buf.at[slot], out_hbm.at[sample], o_sem.at[slot])

    def i_store(sample, slot):
        return pltpu.make_async_copy(i_buf.at[slot], gin_hbm.at[sample], i_sem.at[slot])

    def spread_rows(stage, chunk, held):
        for step in range(1, lon):
            peer = lax.rem(my_lon + step, lon)
            src = held.at[chunk * group + peer // halves, lax.rem(peer, halves)]
            lon_copy(stage, chunk, src, lon_a.at[chunk, my_lon], peer).start()
        src = held.at[chunk * group + my_lon // halves, lax.rem(my_lon, halves)]
        own_copy(stage, chunk, src, lon_a.at[chunk, my_lon]).start()

    def spread_bands(stage, chunk, buffer, target):
        for step in range(1, lat):
            peer = lax.rem(my_lat + step, lat)
            lat_copy(stage, chunk, buffer.at[peer], target.at[chunk, my_lat], peer).start()

    def pair(values, factor):
        return jnp.concatenate([values(0), values(1)], axis=1).astype(jnp.bfloat16)

    def to_waves(stage, chunk, table, scale, buffer):
        landed(stage - 1, chunk, lon_a.at[chunk])
        for source in range(lon):
            wide[pl.ds(source * rows, rows), :] = lon_a[chunk, source, pl.ds(0, rows), :].astype(jnp.float32)
        for first in range(0, band, 2):
            rhs = jnp.concatenate(
                [wide[pl.ds(first + k, points, stride=band), :] for k in range(2)], axis=1
            ).astype(jnp.bfloat16)
            got = dot(table[...], rhs)
            if scale is not None:
                got = got * scale
            for k in range(2):
                slim[pl.ds(first + k, waves, stride=band), :] = got[:, k * LANES : (k + 1) * LANES]

        @pl.when(chunk > 0)
        def _():
            sent(stage, buffer.at[pl.ds(0, lat - 1)])

        for target in range(lat):
            buffer[target] = slim[pl.ds(target * block, block), :].astype(jnp.bfloat16)
        spread_bands(stage, chunk, buffer, lat_a)
        own = pl.ds(pl.multiple_of(my_lat * block, 8), block)
        lat_a[chunk, my_lat] = slim[own, :].astype(jnp.bfloat16)

    def to_points(stage, chunk, table, scale, buffer):
        landed(stage - 1, chunk, lat_b.at[chunk, pl.ds(0, lat - 1)])
        for source in range(lat):
            slim[pl.ds(source * block, block), :] = lat_b[chunk, source].astype(jnp.float32)
        for first in range(0, band, 2):
            rhs = jnp.concatenate(
                [slim[pl.ds(first + k, waves, stride=band), :] for k in range(2)], axis=1
            ).astype(jnp.bfloat16)
            got = dot(table[...], rhs)
            if scale is not None:
                got = got * scale
            for k in range(2):
                wide[pl.ds(first + k, points, stride=band), :] = got[:, k * LANES : (k + 1) * LANES]

        @pl.when(chunk > 0)
        def _():
            sent(stage, buffer.at[pl.ds(0, lon - 1)])

        for target in range(lon):
            buffer[target, pl.ds(0, rows), :] = wide[pl.ds(target * rows, rows), :].astype(jnp.bfloat16)
        sample, half = chunk * group + my_lon // halves, lax.rem(my_lon, halves)
        for step in range(1, lon):
            peer = lax.rem(my_lon + step, lon)
            lon_copy(stage, chunk, buffer.at[peer], lon_b.at[sample, half], peer).start()
        own = pl.ds(pl.multiple_of(my_lon * rows, 8), rows)
        lon_b[sample, half, pl.ds(0, rows), :] = wide[own, :].astype(jnp.bfloat16)

    def slab_step(stage, chunk, first_table, second_table, between, buffer):
        landed(stage - 1, chunk, lat_a.at[chunk, pl.ds(0, lat - 1)])
        for source in range(lat):
            slim[pl.ds(source * block, block), :] = lat_a[chunk, source].astype(jnp.float32)
        for m in range(slab):
            parts = []
            for r in range(2):
                at = (r * slab + m) * band
                parts.append(
                    jnp.concatenate([slim[pl.ds(s * block + at, band), :] for s in range(lat)], axis=0)
                )
            rhs = jnp.concatenate(parts, axis=1).astype(jnp.bfloat16)
            real, imag = between(m, dot(first_table[m], rhs))
            low = jnp.concatenate([real, imag], axis=1).astype(jnp.bfloat16)
            got = dot(second_table[m], low)
            for r in range(2):
                at = (r * slab + m) * band
                for t in range(lat):
                    wide[pl.ds(t * block + at, band), :] = got[
                        t * band : (t + 1) * band, r * LANES : (r + 1) * LANES
                    ]

        @pl.when(chunk > 0)
        def _():
            sent(stage, buffer.at[pl.ds(0, lat - 1)])

        for target in range(lat):
            buffer[target] = wide[pl.ds(target * block, block), :].astype(jnp.bfloat16)
        spread_bands(stage, chunk, buffer, lat_b)
        own = pl.ds(pl.multiple_of(my_lat * block, 8), block)
        lat_b[chunk, my_lat] = wide[own, :].astype(jnp.bfloat16)

    def both(held, sample, where):
        return jnp.concatenate([held[sample, h, where, :] for h in range(halves)], axis=1)

    def stage_1(chunk):
        @pl.when(chunk > 0)
        def _():
            sent(1, lon_a.at[chunk, pl.ds(0, lon - 1)])

        for k in range(group):
            sample = chunk * group + k
            x_load(sample).wait()

            @pl.loop(0, rows // half_tile)
            def _(i):
                where = pl.ds(pl.multiple_of(i * half_tile, 8), half_tile)
                normal, _ = norm_parts(x_all[sample, where, :].astype(jnp.float32))
                low = (normal * gain_one[...] + bias_one[...]).astype(jnp.bfloat16)
                for h in range(halves):
                    normed[sample, h, where, :] = low[:, h * LANES : (h + 1) * LANES]

        spread_rows(1, chunk, normed)

    def stage_2(chunk):
        to_waves(2, chunk, fwd_t, 1.0 / points, send_2)

    def stage_3(chunk):
        def between(m, got):
            coeffs[chunk, m] = got
            real, imag = got[:, :LANES], got[:, LANES:]
            return (
                w_real[...] * real - w_imag[...] * imag,
                w_real[...] * imag + w_imag[...] * real,
            )

        slab_step(3, chunk, ana, syn, between, send_3)

    def stage_4(chunk):
        to_points(4, chunk, inv, None, send_4)

    def stage_5(chunk):
        landed(4, chunk, lon_a.at[chunk, pl.ds(0, lon - 1)])

        @pl.when(chunk > 0)
        def _():
            sent(5, lon_a.at[chunk, pl.ds(0, lon - 1)])

        for k in range(group):
            sample = chunk * group + k
            g_load(sample, k).wait()

            @pl.when(chunk > 0)
            def _():
                o_store(sample, k).wait()

            @pl.loop(0, rows // full_tile)
            def _(i):
                where = pl.ds(pl.multiple_of(i * full_tile, 8), full_tile)
                low_one = both(normed, sample, where)
                spatial = both(lon_b, sample, where).astype(jnp.float32)
                resid = x_all[sample, where, :].astype(jnp.float32) + (spatial + dot(low_one, skip[...]))
                normal, scaled = norm_parts(resid)
                low_two = (normal * gain_two[...] + bias_two[...]).astype(jnp.bfloat16)
                pre = dot(low_two, mlp_in[...]) + bias_in[...]
                square = pre * pre
                curve = jnp.tanh(root * pre * (1.0 + cubic * square))
                lifted = 0.5 + 0.5 * curve
                act = (pre * lifted).astype(jnp.bfloat16)
                slope = lifted + (0.5 * root) * pre * (1.0 - curve * curve) * (1.0 + (3.0 * cubic) * square)
                o_buf[k, where, :] = (resid + dot(act, mlp_out[...]) + bias_out[...]).astype(jnp.bfloat16)
                g_low = g_buf[k, where, :]
                grad_out_t[...] += t_dot(g_low, act)
                grad_pre = (dot_t(g_low, mlp_out[...]) * slope).astype(jnp.bfloat16)
                grad_in[...] += t_dot(low_two, grad_pre)
                sums_in[...] += fold(grad_pre.astype(jnp.float32))
                grad_second = dot_t(grad_pre, mlp_in[...])
                g_full = g_low.astype(jnp.float32)
                sums[0] += fold(g_full)
                sums[3] += fold(grad_second * normal)
                sums[4] += fold(grad_second)
                grad_mixed = (g_full + norm_back(grad_second, normal, scaled, gain_two[...])).astype(jnp.bfloat16)
                grad_skip[...] += t_dot(low_one, grad_mixed)
                for h in range(halves):
                    mixed[sample, h, where, :] = grad_mixed[:, h * LANES : (h + 1) * LANES]

            o_store(sample, k).start()

            @pl.when(chunk < chunks - 1)
            def _():
                g_load(sample + group, k).start()

        spread_rows(5, chunk, mixed)

    def stage_6(chunk):
        to_waves(6, chunk, inv_t, None, send_6)

    def stage_7(chunk):
        def between(m, got):
            dr, di = got[:, :LANES], got[:, LANES:]
            held = coeffs[chunk, m]
            ar, ai = held[:, :LANES], held[:, LANES:]
            grad_spec[0] += dr * ar + di * ai
            grad_spec[1] += di * ar - dr * ai
            return (
                w_real[...] * dr + w_imag[...] * di,
                w_real[...] * di - w_imag[...] * dr,
            )

        slab_step(7, chunk, syn_t, ana_t, between, send_7)

    def stage_8(chunk):
        to_points(8, chunk, fwd, 1.0 / points, send_8)

    def stage_9(chunk):
        landed(8, chunk, lon_a.at[chunk, pl.ds(0, lon - 1)])
        for k in range(group):
            sample = chunk * group + k

            @pl.when(chunk > 0)
            def _():
                i_store(sample, k).wait()

            @pl.loop(0, rows // half_tile)
            def _(i):
                where = pl.ds(pl.multiple_of(i * half_tile, 8), half_tile)
                normal, scaled = norm_parts(x_all[sample, where, :].astype(jnp.float32))
                low = both(mixed, sample, where)
                grad_normed = dot_t(low, skip[...]) + both(lon_b, sample, where).astype(jnp.float32)
                sums[1] += fold(grad_normed * normal)
                sums[2] += fold(grad_normed)
                i_buf[k, where, :] = low.astype(jnp.float32) + norm_back(
                    grad_normed, normal, scaled, gain_one[...]
                )

            i_store(sample, k).start()

    stages = (stage_1, stage_2, stage_3, stage_4, stage_5, stage_6, stage_7, stage_8, stage_9)

    for sample in range(batch):
        x_load(sample).start()
    for k in range(group):
        g_load(k, k).start()

    barrier = pltpu.get_barrier_semaphore()
    for step in range(1, lon):
        pl.semaphore_signal(
            barrier, inc=1, device_id={"lon": lax.rem(my_lon + step, lon)}, device_id_type=MESH
        )
    for step in range(1, lat):
        pl.semaphore_signal(
            barrier, inc=1, device_id={"lat": lax.rem(my_lat + step, lat)}, device_id_type=MESH
        )
    pl.semaphore_wait(barrier, lon - 1 + lat - 1)

    grad_skip[...] = jnp.zeros_like(grad_skip)
    grad_in[...] = jnp.zeros_like(grad_in)
    grad_out_t[...] = jnp.zeros_like(grad_out_t)
    sums_in[...] = jnp.zeros_like(sums_in)
    sums[...] = jnp.zeros_like(sums)
    grad_spec[...] = jnp.zeros_like(grad_spec)
    padded = lon_a.shape[2]
    if padded > rows:
        for held in (normed, mixed):
            held[:, :, rows:, :] = jnp.zeros_like(held[:, :, rows:, :])
        for held in (send_4, send_8):
            held[:, rows:, :] = jnp.zeros_like(held[:, rows:, :])

    def tick(now, carry):
        for stage in ORDER:
            chunk = now - OFFSET[stage]

            @pl.when(jnp.logical_and(chunk >= 0, chunk < chunks))
            def _(stage=stage, chunk=chunk):
                stages[stage - 1](chunk)

        return carry

    lax.fori_loop(0, chunks + max(OFFSET.values()), tick, 0)

    last = chunks - 1
    for stage in (1, 5):
        sent(stage, lon_a.at[last, pl.ds(0, lon - 1)])
    for stage, buffer, count in (
        (2, send_2, lat - 1),
        (3, send_3, lat - 1),
        (4, send_4, lon - 1),
        (6, send_6, lat - 1),
        (7, send_7, lat - 1),
        (8, send_8, lon - 1),
    ):
        sent(stage, buffer.at[pl.ds(0, count)])
    for k in range(group):
        o_store(last * group + k, k).wait()
        i_store(last * group + k, k).wait()


def per_device(
    tables,
    lat,
    lon,
    inputs,
    legendre_forward,
    legendre_inverse,
    spectral_weight,
    skip_weight,
    gain_first,
    bias_first,
    gain_second,
    bias_second,
    mlp_in,
    mlp_in_bias,
    mlp_out,
    mlp_out_bias,
    cotangent,
):
    batch, band, columns, width = inputs.shape
    points = columns * lon
    slab, degrees, lats = legendre_forward.shape
    orders = slab * lat
    hidden = mlp_in.shape[1]
    rows = columns * band
    padded = -(-rows // 16) * 16
    halves = width // LANES
    group = lon // halves
    chunks = batch // group
    block = 2 * slab * band
    waves = 2 * orders

    forward, inverse = tables(points, lat)(orders)
    order_index = lax.axis_index("lat") * slab + jnp.arange(slab, dtype=jnp.int32)
    degree_index = jnp.arange(degrees, dtype=jnp.int32)
    zero_low = jnp.zeros((), jnp.bfloat16)
    analysis = jnp.where(
        degree_index[None, :, None] >= order_index[:, None, None], legendre_forward, zero_low
    )
    synthesis = jnp.where(
        degree_index[None, None, :] >= order_index[:, None, None], legendre_inverse, zero_low
    )
    my_lon = lax.axis_index("lon")
    my_half = lax.rem(my_lon, halves)
    weight = lax.all_gather(spectral_weight, "lon", axis=2, tiled=True)
    weight = lax.dynamic_slice_in_dim(weight, my_half * LANES, LANES, axis=2)

    def flat(values):
        return values.transpose(0, 2, 1, 3).reshape(batch, rows, width)

    def row(values):
        return values.reshape(1, -1)

    vmem = pl.BlockSpec(memory_space=pltpu.VMEM)
    hbm = pl.BlockSpec(memory_space=pl.ANY)
    low, full = jnp.bfloat16, jnp.float32
    results = pl.pallas_call(
        functools.partial(block_kernel, lat, lon),
        out_shape=(
            jax.ShapeDtypeStruct((batch, rows, width), low),
            jax.ShapeDtypeStruct((batch, rows, width), full),
            jax.ShapeDtypeStruct((width, width), full),
            jax.ShapeDtypeStruct((width, hidden), full),
            jax.ShapeDtypeStruct((width, hidden), full),
            jax.ShapeDtypeStruct((8, hidden), full),
            jax.ShapeDtypeStruct((5, 8, width), full),
            jax.ShapeDtypeStruct((2, degrees, LANES), full),
        ),
        in_specs=[hbm, hbm] + [vmem] * 19,
        out_specs=(hbm, hbm) + (vmem,) * 6,
        scratch_shapes=[
            pltpu.VMEM((batch, rows, width), low),
            pltpu.VMEM((batch, halves, padded, LANES), low),
            pltpu.VMEM((batch, halves, padded, LANES), low),
            pltpu.VMEM((chunks, lon, padded, LANES), low),
            pltpu.VMEM((batch, halves, padded, LANES), low),
            pltpu.VMEM((chunks, lat, block, LANES), low),
            pltpu.VMEM((chunks, lat, block, LANES), low),
            pltpu.VMEM((chunks, slab, degrees, 2 * LANES), full),
            pltpu.VMEM((lat, block, LANES), low),
            pltpu.VMEM((lat, block, LANES), low),
            pltpu.VMEM((lon, padded, LANES), low),
            pltpu.VMEM((lat, block, LANES), low),
            pltpu.VMEM((lat, block, LANES), low),
            pltpu.VMEM((lon, padded, LANES), low),
            pltpu.VMEM((max(points, waves) * band, LANES), full),
            pltpu.VMEM((waves * band, LANES), full),
            pltpu.VMEM((group, rows, width), low),
            pltpu.VMEM((group, rows, width), low),
            pltpu.VMEM((group, rows, width), full),
            pltpu.SemaphoreType.DMA((8, chunks)),
            pltpu.SemaphoreType.DMA((8,)),
            pltpu.SemaphoreType.DMA((batch,)),
            pltpu.SemaphoreType.DMA((group,)),
            pltpu.SemaphoreType.DMA((group,)),
            pltpu.SemaphoreType.DMA((group,)),
        ],
        compiler_params=pltpu.CompilerParams(
            collective_id=0, has_side_effects=True, vmem_limit_bytes=63 * 2**20
        ),
    )(
        flat(inputs),
        flat(cotangent),
        jnp.asarray(forward),
        jnp.asarray(inverse),
        jnp.asarray(inverse.T),
        jnp.asarray(forward.T),
        analysis,
        analysis.transpose(0, 2, 1),
        synthesis,
        synthesis.transpose(0, 2, 1),
        weight[0],
        weight[1],
        skip_weight,
        mlp_in,
        mlp_out,
        row(gain_first),
        row(bias_first),
        row(gain_second),
        row(bias_second),
        row(mlp_in_bias),
        row(mlp_out_bias),
    )
    output, grad_inputs, grad_skip, grad_in, grad_out_t, sums_in, sums, grad_spec = results

    def unflat(values):
        return values.reshape(batch, columns, band, width).transpose(0, 2, 1, 3)

    spread = jnp.zeros((2, degrees, width), full)
    spread = lax.dynamic_update_slice_in_dim(spread, grad_spec, my_half * LANES, axis=2)
    sums = jnp.sum(sums, axis=1)
    grad_skip, grad_in, grad_out, in_bias, sums, spread = lax.psum(
        (grad_skip, grad_in, grad_out_t.T, jnp.sum(sums_in, axis=0), sums, spread), ("lat", "lon")
    )
    narrow = width // lon
    grad_spec = lax.dynamic_slice_in_dim(spread, my_lon * narrow, narrow, axis=2)
    return (
        unflat(output),
        unflat(grad_inputs),
        grad_spec,
        grad_skip,
        sums[1],
        sums[2],
        sums[3],
        sums[4],
        grad_in,
        in_bias,
        grad_out,
        sums[0],
    )


def solution(mesh):
    lat, lon = mesh.shape["lat"], mesh.shape["lon"]
    grid = P(None, "lat", "lon", None)
    table = P("lat", None, None)
    channel = P(None, None, "lon")
    return jax.shard_map(
        functools.partial(per_device, fourier_tables, lat, lon),
        mesh=mesh,
        in_specs=(grid, table, table, channel) + (P(),) * 9 + (grid,),
        out_specs=(grid, grid, channel) + (P(),) * 9,
        check_vma=False,
    )
```

time: 1340 us -> 518 us (0.39)
  local copies, waits for them, and re-layouts: 421 us -> 27.9 us
  blocking collectives: 392 us -> 50 us
  Pallas kernels: 0 us -> 326 us
  matrix products: 183 us -> 0 us
  waiting for transfers between devices: 232 us -> 94 us
  other arithmetic: 62.6 us -> 5.34 us
  starting transfers between devices: 22.3 us -> 0.04 us
    pallas_call x0 -> x1, Pallas kernels: none -> 326 us  [per_device(): pl.pallas_call(functools.partial(block_kernel, lat, lon), out_shape=(jax....]
    all_to_all x4 -> x0, blocking collectives: 319 us -> none  [the longest x1 97.6 us: per_device(): lax.all_to_all(grad_mixed, 'lon', split_axis=3, concat_axis=2, tiled=True)]
    all_to_all x4 -> x0, waiting for transfers between devices: 232 us -> none  [the longest x1 93.2 us: per_device(): lax.all_to_all(normed_low, 'lon', split_axis=3, concat_axis=2, tiled=True)]
    dot_general x17 -> x0, matrix products: 183 us -> none  [the longest x1 27.7 us: per_device(): jnp.einsum('bjnc,hc->bjnh', cotangent, mlp_out, preferred_element_type=jn...]
    convert_element_type x11 -> x0, local copies, waits for them, and re-layouts: 179 us -> none  [the longest x2 35.1 us: per_device(): grad_normed = grad_normed + grad_grid.astype(jnp.float32)]
    unnamed x141 -> x15, local copies, waits for them, and re-layouts: 155 us -> 23.1 us
    psum x1, waiting for transfers between devices: 0.01 us -> 94 us  [per_device(): lax.psum((grad_skip, grad_in, grad_out_t.T, jnp.sum(sums_in, axis=0), sum...]
    all_to_all x7 -> x0, local copies, waits for them, and re-layouts: 65 us -> none  [the longest x2 25.9 us: per_device(): lax.all_to_all(normed_low, 'lon', split_axis=3, concat_axis=2, tiled=True)]
  transfers between devices with their start and end apart: 5 -> 1, of which waited for: 3 -> 1; matrix products, arithmetic and copies ran while one was open for 12% -> 0% of each run, Pallas kernels for 0% -> 0%
where the time goes in v1:
time: 518 us
  Pallas kernels  326 us (63%)
  waiting for transfers between devices  94 us (18%)
  blocking collectives  50 us (10%)
  local copies, waits for them, and re-layouts  27.9 us (5%)
  between operations  14.1 us (3%)
  other arithmetic  5.34 us (1%)
    pallas_call x1, Pallas kernels, per_device(): pl.pallas_call(functools.partial(block_kernel, lat, lon), out_shape=(jax....  326 us
    psum x1, waiting for transfers between devices, per_device(): lax.psum((grad_skip, grad_in, grad_out_t.T, jnp.sum(sums_in, axis=0), sum...  94 us
    psum x1, blocking collectives, per_device(): lax.psum((grad_skip, grad_in, grad_out_t.T, jnp.sum(sums_in, axis=0), sum...  42.8 us
    unnamed x15, local copies, waits for them, and re-layouts  23.1 us
  transfers between devices with their start and end apart: 1, of which 1 were waited for; matrix products, arithmetic and copies ran while one was open for 0% of the time, Pallas kernels for 0%

profile of v1, /device:TPU:0, one launch (start us, length us, event | category | flops | bytes accessed | tf_op | source)
XLA Modules:
  0.0 517.7 jit_solution(5047700159348250047)
XLA Ops:
  7.2 0.0 all-reduce.4.cloned.1.call-start
  7.2 0.1 iota_compare_fusion
  7.3 1.1 copy.36
  8.4 0.2 broadcast_select_fusion
  8.6 0.9 fusion.1.syn_t
  9.6 0.9 broadcast_select_fusion.1
  10.5 1.6 fusion.2.ana_t
  12.2 0.9 copy.37
  13.1 7.2 %all_gather.3 = f32[2,96,256]{1,0,2:T(2,128)S(1)} all-gather(f32[2,96,64]{1,0,2:T(2,128)S(1)} %copy.37), channel_id=1, replica_groups=mesh['lat'=8,'lon'=4] {'lon'}, dimensions={2}, use_global_device_ids=true | all-gather | bytes 245760 | tf_op jit(solution)/shard_map/all_gather | solution.py:529
  20.3 0.1 constant_dynamic-slice_fusion.2
  20.4 0.7 copy.44
  21.1 0.7 copy.45
  21.8 0.8 copy.40.syn
  22.6 0.9 copy.39.ana
  23.5 326.3 %shard_map.265 = (bf16[16,720,256]{2,1,0:T(8,128)(2,1)}, f32[16,720,256]{2,1,0:T(8,128)}, f32[256,256]{1,0:T(8,128)}, f32[256,512]{1,0:T(8,128)}, f32[256,512]{1...) custom-call(bf16[16,720,256]{2,1,0:T(8,128)(2,1)} %bitcast.31, ...), custom_call_target="tpu_custom_call" | custom-call | tf_op jit(solution)/shard_map/pallas_call | solution.py:541
  349.8 1.0 copy.41
  350.8 0.0 copy-start
  350.9 0.7 copy-done
  351.6 0.0 all-reduce.4.cloned.1.call-update
  351.6 0.8 reduce_sum.18
  352.4 0.7 reduce_sum.19
  353.1 42.8 %all-reduce = (f32[5,256]{1,0:T(8,128)S(1)}, f32[512]{0:T(512)}) all-reduce(f32[5,256]{1,0:T(8,128)S(1)} %reduce_sum.18, f32[512]{0:T(512)S(1)} %reduce_sum.19), channel_id=1, replica_groups=mesh['lat'=8,'lon'=4] {'lat','lon'}, use_global_device_ids=true, to_apply=%region_3.4 | all-reduce | flops 1792 | bytes 14336 | tf_op jit(solution)/shard_map/psum | solution.py:616
  395.9 0.6 fusion
  396.5 94.0 %all-reduce.4.cloned.1.call-done = (f32[2,96,256]{1,2,0:T(8,128)}, f32[256,256]{1,0:T(8,128)}, f32[256,512]{1,0:T(8,128)}, f32[512,256]{0,1:T(8,128)}) async-done(((f32[2,96,256]{1,2,0:T(8,128)}, f32[256,256]{1,0:T(8,128)}, f32[256,512]{1,0:T(8,128)}, f32[512,256]{0,1:T(8,128)}), (f32[2,96,256]{1,2,0:T(8,128)}, f32[256,256]{1,0:T(8,128)}, f32[256,512]{1,0:T(8,128)}, ...) | async-done | bytes 1507344 | tf_op jit(solution)/shard_map/psum | solution.py:616
  490.4 2.0 copy.42
  492.5 1.5 constant_dynamic-slice_fusion.1
  494.0 5.6 %copy.55 = bf16[16,8,90,256]{3,1,2,0:T(8,128)(2,1)} copy(bf16[16,8,90,256]{3,1,2,0:T(8,128)(2,1)} %bitcast.33) | data formatting | bytes 11796480
  499.6 9.8 %copy.56 = f32[16,8,90,256]{3,1,2,0:T(8,128)} copy(f32[16,8,90,256]{3,1,2,0:T(8,128)} %bitcast.30) | data formatting | bytes 23592960
  509.4 0.0 copy-done.2
  509.4 0.7 copy.57
  510.1 0.0 copy-done.1
  510.1 0.8 copy.58
  (5 shorter events, 0.0 us)
Async XLA Ops:
  7.2 483.3 %all-reduce.4.cloned.1.call-start = ((), (), s32[]{:S(2)}) async-start(), calls=%async_computation | async-start | bytes 3145728 | tf_op jit(solution)/shard_map/psum | solution.py:616
  350.8 0.7 copy-start
  499.6 9.8 %copy-start.2 = (f32[256,256]{1,0:T(8,128)S(1)}, f32[256,256]{1,0:T(8,128)}, u32[]{:S(2)}) copy-start(f32[256,256]{1,0:T(8,128)} %get-tuple-element.80) | copy-start | bytes 786436
  499.6 10.5 %copy-start.1 = (f32[256,512]{1,0:T(8,128)S(1)}, f32[256,512]{1,0:T(8,128)}, u32[]{:S(2)}) copy-start(f32[256,512]{1,0:T(8,128)} %get-tuple-element.85) | copy-start | bytes 1572868
Sparse Core Ops, SparseCore 0:
  351.7 138.7 all-reduce.3

commit v2 on v1

--- a/solution.py
+++ b/solution.py
@@ -85,12 +85,9 @@
     inv_t,
     inv,
     fwd,
-    ana,
-    ana_t,
-    syn,
-    syn_t,
-    w_real,
-    w_imag,
+    raw_ana,
+    raw_syn,
+    weight,
     skip,
     mlp_in,
     mlp_out,
@@ -102,12 +99,9 @@
     bias_out,
     out_hbm,
     gin_hbm,
-    grad_skip,
-    grad_in,
-    grad_out_t,
-    sums_in,
-    sums,
-    grad_spec,
+    total_hbm,
+    total_spec,
+    total_norm,
     x_all,
     normed,
     mixed,
@@ -133,13 +127,43 @@
     g_sem,
     o_sem,
     i_sem,
+    ana,
+    ana_t,
+    syn,
+    syn_t,
+    w_parts,
+    w_real,
+    w_imag,
+    acc,
+    part_core,
+    part_chip,
+    part_lat,
+    spec,
+    spec_lat,
+    spec_lon,
+    spec_sum,
+    norm_sums,
+    norm_own,
+    norm_lon,
+    norm_lat,
+    w_sem,
+    fold_recv,
+    fold_send,
+    spec_recv,
+    spec_send,
+    spec_pair,
+    norm_recv,
+    norm_send,
+    own_sem,
 ):
     batch, rows, width = x_hbm.shape
     halves = width // LANES
     group = lon // halves
     chunks = batch // group
     points = fwd_t.shape[1]
-    slab, degrees, lats = ana.shape
+    slab, lats, degrees = raw_ana.shape
+    narrow = width // lon
+    hidden = mlp_in.shape[1]
     band = lats // lat
     block = 2 * slab * band
     waves = 2 * slab * lat
@@ -287,6 +311,14 @@
         own = pl.ds(pl.multiple_of(my_lat * block, 8), block)
         lat_b[chunk, my_lat] = wide[own, :].astype(jnp.bfloat16)
 
+    hidden_rows = width * hidden // LANES
+    vector_rows = 2 * hidden_rows + width * width // LANES
+
+    def gather_rows(base, values):
+        count = values.shape[0]
+        for q in range(values.shape[1] // LANES):
+            acc[pl.ds(base + q * count, count), :] += values[:, q * LANES : (q + 1) * LANES]
+
     def both(held, sample, where):
         return jnp.concatenate([held[sample, h, where, :] for h in range(halves)], axis=1)
 
@@ -314,7 +346,7 @@
 
     def stage_3(chunk):
         def between(m, got):
-            coeffs[chunk, m] = got
+            coeffs[chunk, m] = got.astype(jnp.bfloat16)
             real, imag = got[:, :LANES], got[:, LANES:]
             return (
                 w_real[...] * real - w_imag[...] * imag,
@@ -357,17 +389,16 @@
                 slope = lifted + (0.5 * root) * pre * (1.0 - curve * curve) * (1.0 + (3.0 * cubic) * square)
                 o_buf[k, where, :] = (resid + dot(act, mlp_out[...]) + bias_out[...]).astype(jnp.bfloat16)
                 g_low = g_buf[k, where, :]
-                grad_out_t[...] += t_dot(g_low, act)
+                gather_rows(hidden_rows, t_dot(g_low, act))
                 grad_pre = (dot_t(g_low, mlp_out[...]) * slope).astype(jnp.bfloat16)
-                grad_in[...] += t_dot(low_two, grad_pre)
-                sums_in[...] += fold(grad_pre.astype(jnp.float32))
+                gather_rows(0, t_dot(low_two, grad_pre))
+                gather_rows(vector_rows, fold(grad_pre.astype(jnp.float32)))
                 grad_second = dot_t(grad_pre, mlp_in[...])
                 g_full = g_low.astype(jnp.float32)
-                sums[0] += fold(g_full)
-                sums[3] += fold(grad_second * normal)
-                sums[4] += fold(grad_second)
+                for at, values in enumerate((g_full, grad_second * normal, grad_second)):
+                    gather_rows(vector_rows + 8 * (hidden + at * width) // LANES, fold(values))
                 grad_mixed = (g_full + norm_back(grad_second, normal, scaled, gain_two[...])).astype(jnp.bfloat16)
-                grad_skip[...] += t_dot(low_one, grad_mixed)
+                gather_rows(2 * hidden_rows, t_dot(low_one, grad_mixed))
                 for h in range(halves):
                     mixed[sample, h, where, :] = grad_mixed[:, h * LANES : (h + 1) * LANES]
 
@@ -385,10 +416,10 @@
     def stage_7(chunk):
         def between(m, got):
             dr, di = got[:, :LANES], got[:, LANES:]
-            held = coeffs[chunk, m]
+            held = coeffs[chunk, m].astype(jnp.float32)
             ar, ai = held[:, :LANES], held[:, LANES:]
-            grad_spec[0] += dr * ar + di * ai
-            grad_spec[1] += di * ar - dr * ai
+            spec[pl.ds(0, degrees), :] += dr * ar + di * ai
+            spec[pl.ds(degrees, degrees), :] += di * ar - dr * ai
             return (
                 w_real[...] * dr + w_imag[...] * di,
                 w_real[...] * di - w_imag[...] * dr,
@@ -414,13 +445,266 @@
                 normal, scaled = norm_parts(x_all[sample, where, :].astype(jnp.float32))
                 low = both(mixed, sample, where)
                 grad_normed = dot_t(low, skip[...]) + both(lon_b, sample, where).astype(jnp.float32)
-                sums[1] += fold(grad_normed * normal)
-                sums[2] += fold(grad_normed)
+                norm_sums[0] += fold(grad_normed * normal)
+                norm_sums[1] += fold(grad_normed)
                 i_buf[k, where, :] = low.astype(jnp.float32) + norm_back(
                     grad_normed, normal, scaled, gain_one[...]
                 )
 
             i_store(sample, k).start()
+
+    def weight_copies(start):
+        place = lax.rem(my_lon, group)
+        held = w_parts.at[:, pl.ds(pl.multiple_of(place * narrow, 8), narrow), :]
+        for q in range(group):
+            peer = my_lon // group + halves * q
+
+            @pl.when(peer != my_lon)
+            def _(peer=peer, q=q):
+                copy = pltpu.make_async_remote_copy(
+                    src_ref=weight,
+                    dst_ref=held,
+                    send_sem=w_sem.at[1, q],
+                    recv_sem=w_sem.at[0, place],
+                    device_id={"lon": peer},
+                    device_id_type=MESH,
+                )
+                if start:
+                    copy.start()
+                else:
+                    copy.wait_send()
+
+            if start:
+
+                @pl.when(peer == my_lon)
+                def _():
+                    pltpu.make_async_copy(weight, held, w_sem.at[0, place]).start()
+
+    def build():
+        acc[...] = jnp.zeros_like(acc)
+        spec[...] = jnp.zeros_like(spec)
+        norm_sums[...] = jnp.zeros_like(norm_sums)
+        norm_own[...] = jnp.zeros_like(norm_own)
+        degree = lax.broadcasted_iota(jnp.int32, (lats, degrees), 1)
+
+        @pl.loop(0, slab)
+        def _(m):
+            kept = degree >= my_lat * slab + m
+            for raw, plain, turned in ((raw_ana, ana_t, ana), (raw_syn, syn, syn_t)):
+                values = jnp.where(kept, raw[m].astype(jnp.float32), 0.0)
+                plain[m] = values.astype(jnp.bfloat16)
+                turned[m] = values.T.astype(jnp.bfloat16)
+
+        for q in range(group):
+            part = w_parts.at[:, pl.ds(q * narrow, narrow), :]
+            pltpu.make_async_copy(part, part, w_sem.at[0, q]).wait()
+        w_real[...] = w_parts[0].T
+        w_imag[...] = w_parts[1].T
+
+    total_rows = acc.shape[0]
+    place_core, place_chip = lax.rem(my_lon, 2), my_lon // 2
+    levels = (
+        (2, place_core, part_core, lambda p: {"lon": 2 * place_chip + p}),
+        (lon // 2, place_chip, part_chip, lambda p: {"lon": 2 * p + place_core}),
+        (lat, my_lat, part_lat, lambda p: {"lat": p}),
+    )
+    bases, sizes = [0], [total_rows]
+    for count, place, _, _ in levels:
+        sizes.append(sizes[-1] // count)
+        bases.append(bases[-1] + place * sizes[-1])
+
+    def row_part(at, count):
+        return pl.ds(pl.multiple_of(at, 8), count)
+
+    def fold_start(k):
+        count, place, parts, device = levels[k]
+        for step in range(1, count):
+            peer = lax.rem(place + step, count)
+            pltpu.make_async_remote_copy(
+                src_ref=acc.at[row_part(bases[k] + peer * sizes[k + 1], sizes[k + 1]), :],
+                dst_ref=parts.at[step - 1],
+                send_sem=fold_send.at[0, k],
+                recv_sem=fold_recv.at[0, k],
+                device_id=device(peer),
+                device_id_type=MESH,
+            ).start()
+
+    def fold_end(k):
+        count, _, parts, _ = levels[k]
+        pltpu.make_async_copy(parts, parts, fold_recv.at[0, k]).wait()
+        got = parts[0]
+        for step in range(2, count):
+            got = got + parts[step - 1]
+        acc[row_part(bases[k + 1], sizes[k + 1]), :] += got
+
+    def spread_start(k):
+        count, place, _, device = levels[k]
+        own = row_part(bases[k + 1], sizes[k + 1])
+        src = acc if k == len(levels) - 1 else total_hbm
+        for step in range(1, count):
+            pltpu.make_async_remote_copy(
+                src_ref=src.at[own, :],
+                dst_ref=total_hbm.at[own, :],
+                send_sem=fold_send.at[1, k],
+                recv_sem=fold_recv.at[1, k],
+                device_id=device(lax.rem(place + step, count)),
+                device_id_type=MESH,
+            ).start()
+        if src is acc:
+            pltpu.make_async_copy(acc.at[own, :], total_hbm.at[own, :], own_sem).start()
+
+    def spread_end(k):
+        count = levels[k][0]
+        all_parts = total_hbm.at[pl.ds(0, (count - 1) * sizes[k + 1]), :]
+        pltpu.make_async_copy(all_parts, all_parts, fold_recv.at[1, k]).wait()
+        if k == len(levels) - 1:
+            own = row_part(bases[k + 1], sizes[k + 1])
+            pltpu.make_async_copy(acc.at[own, :], total_hbm.at[own, :], own_sem).wait()
+
+    def fold_sent():
+        for k, (count, _, _, _) in enumerate(levels):
+            for way in range(2):
+                part = total_hbm if way and k < len(levels) - 1 else acc
+                part = part.at[pl.ds(0, (count - 1) * sizes[k + 1]), :]
+                pltpu.make_async_remote_copy(
+                    src_ref=part,
+                    dst_ref=part,
+                    send_sem=fold_send.at[way, k],
+                    recv_sem=fold_recv.at[way, k],
+                    device_id={"lon": my_lon},
+                    device_id_type=MESH,
+                ).wait_send()
+
+    spec_rows = spec_sum.shape[0]
+
+    def spec_lat_copies(way, src, dst):
+        for step in range(1, lat):
+            peer = lax.rem(my_lat + step, lat)
+            pltpu.make_async_remote_copy(
+                src_ref=src(peer),
+                dst_ref=dst(step),
+                send_sem=spec_send.at[way],
+                recv_sem=spec_recv.at[way],
+                device_id={"lat": peer},
+                device_id_type=MESH,
+            ).start()
+
+    def spec_start():
+        spec_lat_copies(
+            0, lambda p: spec.at[row_part(p * spec_rows, spec_rows), :], lambda s: spec_lat.at[s - 1]
+        )
+
+    def spec_pairs(action):
+        half = lax.rem(my_lon, halves)
+        for q in range(group):
+            target = half * group + q
+
+            @pl.when(target != my_lon)
+            def _(target=target, q=q):
+                copy = pltpu.make_async_remote_copy(
+                    src_ref=spec_sum,
+                    dst_ref=spec_lon.at[my_lon // halves],
+                    send_sem=spec_pair.at[1, q],
+                    recv_sem=spec_pair.at[0, my_lon // halves],
+                    device_id={"lon": target},
+                    device_id_type=MESH,
+                )
+                if action == "start":
+                    copy.start()
+                else:
+                    copy.wait_send()
+
+            if action == "start":
+
+                @pl.when(target == my_lon)
+                def _():
+                    pltpu.make_async_copy(
+                        spec_sum, spec_lon.at[my_lon // halves], spec_pair.at[0, my_lon // halves]
+                    ).start()
+
+    def spec_middle():
+        pltpu.make_async_copy(spec_lat, spec_lat, spec_recv.at[0]).wait()
+        got = spec[row_part(my_lat * spec_rows, spec_rows), :]
+        for step in range(1, lat):
+            got = got + spec_lat[step - 1]
+        spec_sum[...] = got
+        spec_pairs("start")
+
+    def spec_back():
+        for q in range(group):
+            pltpu.make_async_copy(spec_lon.at[q], spec_lon.at[q], spec_pair.at[0, q]).wait()
+        got = spec_lon[0]
+        for q in range(1, group):
+            got = got + spec_lon[q]
+        own = row_part(my_lat * spec_rows, spec_rows)
+        total_spec[own, :] = got
+        spec_lat_copies(1, lambda p: total_spec.at[own, :], lambda s: total_spec.at[own, :])
+
+    def spec_end():
+        part = total_spec.at[pl.ds(0, (lat - 1) * spec_rows), :]
+        pltpu.make_async_copy(part, part, spec_recv.at[1]).wait()
+        for way in range(2):
+            pltpu.make_async_remote_copy(
+                src_ref=part,
+                dst_ref=part,
+                send_sem=spec_send.at[way],
+                recv_sem=spec_recv.at[way],
+                device_id={"lat": my_lat},
+                device_id_type=MESH,
+            ).wait_send()
+        spec_pairs("end")
+
+    def norm_copies(way, axis, count, place, src, parts, action):
+        for step in range(1, count):
+            copy = pltpu.make_async_remote_copy(
+                src_ref=src,
+                dst_ref=parts.at[step - 1],
+                send_sem=norm_send.at[way, step - 1],
+                recv_sem=norm_recv.at[way],
+                device_id={axis: lax.rem(place + step, count)},
+                device_id_type=MESH,
+            )
+            if action == "start":
+                copy.start()
+            else:
+                copy.wait_send()
+
+    def norm_fold(way, axis, count, place, src, parts, out):
+        norm_copies(way, axis, count, place, src, parts, "start")
+        pltpu.make_async_copy(parts, parts, norm_recv.at[way]).wait()
+        got = src[...]
+        for step in range(1, count):
+            got = got + parts[step - 1]
+        out[...] = got
+
+    def norm_all():
+        for which in range(2):
+            line = jnp.sum(norm_sums[which], axis=0, keepdims=True)
+            for h in range(halves):
+                norm_own[0, pl.ds(which * halves + h, 1), :] = line[:, h * LANES : (h + 1) * LANES]
+        norm_fold(0, "lon", lon, my_lon, norm_own.at[0], norm_lon, norm_own.at[1])
+        norm_fold(1, "lat", lat, my_lat, norm_own.at[1], norm_lat, total_norm)
+        norm_copies(0, "lon", lon, my_lon, norm_own.at[0], norm_lon, "end")
+        norm_copies(1, "lat", lat, my_lat, norm_own.at[1], norm_lat, "end")
+
+    def run(*steps):
+        def go():
+            for step, k in steps:
+                step() if k is None else step(k)
+
+        return go
+
+    aside = {
+        (0, 1): build,
+        (chunks + 3, 5): run((fold_start, 0)),
+        (chunks + 3, 7): run((fold_end, 0), (fold_start, 1)),
+        (chunks + 3, 6): run((fold_end, 1), (fold_start, 2)),
+        (chunks + 4, 8): run((fold_end, 2), (spread_start, 2)),
+        (chunks + 4, 7): run((spec_start, None)),
+        (chunks + 4, 9): run((spread_end, 2), (spread_start, 1)),
+        (chunks + 5, 8): run((spread_end, 1), (spread_start, 0), (spec_middle, None)),
+        (chunks + 5, 7): run((spec_back, None)),
+    }
 
     stages = (stage_1, stage_2, stage_3, stage_4, stage_5, stage_6, stage_7, stage_8, stage_9)
 
@@ -440,12 +724,7 @@
         )
     pl.semaphore_wait(barrier, lon - 1 + lat - 1)
 
-    grad_skip[...] = jnp.zeros_like(grad_skip)
-    grad_in[...] = jnp.zeros_like(grad_in)
-    grad_out_t[...] = jnp.zeros_like(grad_out_t)
-    sums_in[...] = jnp.zeros_like(sums_in)
-    sums[...] = jnp.zeros_like(sums)
-    grad_spec[...] = jnp.zeros_like(grad_spec)
+    weight_copies(True)
     padded = lon_a.shape[2]
     if padded > rows:
         for held in (normed, mixed):
@@ -461,10 +740,19 @@
             def _(stage=stage, chunk=chunk):
                 stages[stage - 1](chunk)
 
+            for (when, after), action in aside.items():
+                if after == stage:
+                    pl.when(now == when)(action)
+
         return carry
 
     lax.fori_loop(0, chunks + max(OFFSET.values()), tick, 0)
 
+    norm_all()
+    spread_end(0)
+    spec_end()
+    fold_sent()
+    weight_copies(False)
     last = chunks - 1
     for stage in (1, 5):
         sent(stage, lon_a.at[last, pl.ds(0, lon - 1)])
@@ -515,19 +803,12 @@
     waves = 2 * orders
 
     forward, inverse = tables(points, lat)(orders)
-    order_index = lax.axis_index("lat") * slab + jnp.arange(slab, dtype=jnp.int32)
-    degree_index = jnp.arange(degrees, dtype=jnp.int32)
-    zero_low = jnp.zeros((), jnp.bfloat16)
-    analysis = jnp.where(
-        degree_index[None, :, None] >= order_index[:, None, None], legendre_forward, zero_low
-    )
-    synthesis = jnp.where(
-        degree_index[None, None, :] >= order_index[:, None, None], legendre_inverse, zero_low
-    )
     my_lon = lax.axis_index("lon")
-    my_half = lax.rem(my_lon, halves)
-    weight = lax.all_gather(spectral_weight, "lon", axis=2, tiled=True)
-    weight = lax.dynamic_slice_in_dim(weight, my_half * LANES, LANES, axis=2)
+    hidden = mlp_in.shape[1]
+    flat_rows = (2 * hidden + width) * width // LANES + 8 * (hidden + 3 * width) // LANES
+    share = -(-flat_rows // (8 * lat * lon)) * 8
+    total_rows = share * lat * lon
+    spec_rows = -(-2 * degrees // (8 * lat)) * 8
 
     def flat(values):
         return values.transpose(0, 2, 1, 3).reshape(batch, rows, width)
@@ -543,15 +824,12 @@
         out_shape=(
             jax.ShapeDtypeStruct((batch, rows, width), low),
             jax.ShapeDtypeStruct((batch, rows, width), full),
-            jax.ShapeDtypeStruct((width, width), full),
-            jax.ShapeDtypeStruct((width, hidden), full),
-            jax.ShapeDtypeStruct((width, hidden), full),
-            jax.ShapeDtypeStruct((8, hidden), full),
-            jax.ShapeDtypeStruct((5, 8, width), full),
-            jax.ShapeDtypeStruct((2, degrees, LANES), full),
+            jax.ShapeDtypeStruct((total_rows, LANES), full),
+            jax.ShapeDtypeStruct((lat * spec_rows, LANES), full),
+            jax.ShapeDtypeStruct((8, LANES), full),
         ),
-        in_specs=[hbm, hbm] + [vmem] * 19,
-        out_specs=(hbm, hbm) + (vmem,) * 6,
+        in_specs=[hbm, hbm] + [vmem] * 16,
+        out_specs=(hbm, hbm, hbm, vmem, vmem),
         scratch_shapes=[
             pltpu.VMEM((batch, rows, width), low),
             pltpu.VMEM((batch, halves, padded, LANES), low),
@@ -560,7 +838,7 @@
             pltpu.VMEM((batch, halves, padded, LANES), low),
             pltpu.VMEM((chunks, lat, block, LANES), low),
             pltpu.VMEM((chunks, lat, block, LANES), low),
-            pltpu.VMEM((chunks, slab, degrees, 2 * LANES), full),
+            pltpu.VMEM((chunks, slab, degrees, 2 * LANES), low),
             pltpu.VMEM((lat, block, LANES), low),
             pltpu.VMEM((lat, block, LANES), low),
             pltpu.VMEM((lon, padded, LANES), low),
@@ -578,6 +856,34 @@
             pltpu.SemaphoreType.DMA((group,)),
             pltpu.SemaphoreType.DMA((group,)),
             pltpu.SemaphoreType.DMA((group,)),
+            pltpu.VMEM((slab, degrees, lats), low),
+            pltpu.VMEM((slab, lats, degrees), low),
+            pltpu.VMEM((slab, lats, degrees), low),
+            pltpu.VMEM((slab, degrees, lats), low),
+            pltpu.VMEM((2, LANES, degrees), full),
+            pltpu.VMEM((degrees, LANES), full),
+            pltpu.VMEM((degrees, LANES), full),
+            pltpu.VMEM((total_rows, LANES), full),
+            pltpu.VMEM((1, total_rows // 2, LANES), full),
+            pltpu.VMEM((lon // 2 - 1, total_rows // lon, LANES), full),
+            pltpu.VMEM((lat - 1, share, LANES), full),
+            pltpu.VMEM((lat * spec_rows, LANES), full),
+            pltpu.VMEM((lat - 1, spec_rows, LANES), full),
+            pltpu.VMEM((group, spec_rows, LANES), full),
+            pltpu.VMEM((spec_rows, LANES), full),
+            pltpu.VMEM((2, 8, width), full),
+            pltpu.VMEM((2, 8, LANES), full),
+            pltpu.VMEM((lon - 1, 8, LANES), full),
+            pltpu.VMEM((lat - 1, 8, LANES), full),
+            pltpu.SemaphoreType.DMA((2, group)),
+            pltpu.SemaphoreType.DMA((2, 3)),
+            pltpu.SemaphoreType.DMA((2, 3)),
+            pltpu.SemaphoreType.DMA((2,)),
+            pltpu.SemaphoreType.DMA((2,)),
+            pltpu.SemaphoreType.DMA((2, group)),
+            pltpu.SemaphoreType.DMA((2,)),
+            pltpu.SemaphoreType.DMA((2, max(lat, lon) - 1)),
+            pltpu.SemaphoreType.DMA,
         ],
         compiler_params=pltpu.CompilerParams(
             collective_id=0, has_side_effects=True, vmem_limit_bytes=63 * 2**20
@@ -589,12 +895,9 @@
         jnp.asarray(inverse),
         jnp.asarray(inverse.T),
         jnp.asarray(forward.T),
-        analysis,
-        analysis.transpose(0, 2, 1),
-        synthesis,
-        synthesis.transpose(0, 2, 1),
-        weight[0],
-        weight[1],
+        legendre_forward.transpose(0, 2, 1),
+        legendre_inverse,
+        spectral_weight.transpose(0, 2, 1),
         skip_weight,
         mlp_in,
         mlp_out,
@@ -605,32 +908,35 @@
         row(mlp_in_bias),
         row(mlp_out_bias),
     )
-    output, grad_inputs, grad_skip, grad_in, grad_out_t, sums_in, sums, grad_spec = results
+    output, grad_inputs, total, spec, norm = results
 
     def unflat(values):
         return values.reshape(batch, columns, band, width).transpose(0, 2, 1, 3)
 
-    spread = jnp.zeros((2, degrees, width), full)
-    spread = lax.dynamic_update_slice_in_dim(spread, grad_spec, my_half * LANES, axis=2)
-    sums = jnp.sum(sums, axis=1)
-    grad_skip, grad_in, grad_out, in_bias, sums, spread = lax.psum(
-        (grad_skip, grad_in, grad_out_t.T, jnp.sum(sums_in, axis=0), sums, spread), ("lat", "lon")
-    )
+    def wide_part(base, height, across):
+        part = total[base : base + height * across // LANES]
+        return part.reshape(across // LANES, height, LANES).transpose(1, 0, 2).reshape(height, across)
+
+    hidden_rows = width * hidden // LANES
+    vector_rows = 2 * hidden_rows + width * width // LANES
+    vectors = total[vector_rows:flat_rows].reshape(-1, 8, LANES).sum(axis=1).reshape(-1)
+    spec = spec[: 2 * degrees].reshape(2, degrees, LANES)
     narrow = width // lon
-    grad_spec = lax.dynamic_slice_in_dim(spread, my_lon * narrow, narrow, axis=2)
+    grad_spec = lax.dynamic_slice_in_dim(spec, lax.rem(my_lon, group) * narrow, narrow, axis=2)
+    norm = norm[: 2 * halves].reshape(2, width)
     return (
         unflat(output),
         unflat(grad_inputs),
         grad_spec,
-        grad_skip,
-        sums[1],
-        sums[2],
-        sums[3],
-        sums[4],
-        grad_in,
-        in_bias,
-        grad_out,
-        sums[0],
+        wide_part(2 * hidden_rows, width, width),
+        norm[0],
+        norm[1],
+        vectors[hidden + width : hidden + 2 * width],
+        vectors[hidden + 2 * width :],
+        wide_part(0, width, hidden),
+        vectors[:hidden],
+        wide_part(hidden_rows, width, hidden).T,
+        vectors[hidden : hidden + width],
     )
 
 

time: 518 us -> 383 us (0.74)
  waiting for transfers between devices: 94 us -> 0 us
  blocking collectives: 50 us -> 0 us
  Pallas kernels: 326 us -> 357 us
  between operations: 14.1 us -> 0.69 us
    psum x1 -> x0, waiting for transfers between devices: 94 us -> none  [per_device(): lax.psum((grad_skip, grad_in, grad_out_t.T, jnp.sum(sums_in, axis=0), sum...]
    psum x1 -> x0, blocking collectives: 42.8 us -> none  [per_device(): lax.psum((grad_skip, grad_in, grad_out_t.T, jnp.sum(sums_in, axis=0), sum...]
    pallas_call x1, Pallas kernels: 326 us -> 357 us  [per_device(): pl.pallas_call(functools.partial(block_kernel, lat, lon), out_shape=(jax....]
    all_gather x1 -> x0, blocking collectives: 7.22 us -> none  [per_device(): weight = lax.all_gather(spectral_weight, 'lon', axis=2, tiled=True)]
    unnamed x15 -> x3, local copies, waits for them, and re-layouts: 23.1 us -> 16.1 us
  transfers between devices with their start and end apart: 1 -> 0, of which waited for: 1 -> 0; matrix products, arithmetic and copies ran while one was open for 0% -> 0% of each run, Pallas kernels for 0% -> 0%
where the time goes in v2:
time: 383 us; the launch traced here: 382 us
  Pallas kernels  357 us (93%)
  local copies, waits for them, and re-layouts  23.8 us (6%)
    pallas_call x1, Pallas kernels, per_device(): pl.pallas_call(functools.partial(block_kernel, lat, lon), out_shape=(jax....  357 us
    unnamed x3, local copies, waits for them, and re-layouts  16.1 us

profile of v2, /device:TPU:0, one launch (start us, length us, event | category | flops | bytes accessed | tf_op | source)
XLA Modules:
  0.0 382.2 jit_solution(3899501404538430246)
XLA Ops:
  0.7 356.9 %shard_map.265 = (bf16[16,720,256]{2,1,0:T(8,128)(2,1)}, f32[16,720,256]{2,1,0:T(8,128)}, f32[2816,128]{1,0:T(8,128)}, f32[192,128]{1,0:T(8,128)}, f32[8,128]{1,0:T(8,128)}) custom-call(bf16[16,720,256]{2,1,0:T(8,128)(2,1)} %bitcast.56, bf16[16,720,256]{2,1,0:T(8,128)(2,1)} %bitcast.57, bf16[192,360]{1,0:T(8,128)(2,1)} %constant.24.clone.fwd_t, ...), custom_call_target="tpu_custom_call" | custom-call | tf_op jit(solution)/shard_map/pallas_call | solution.py:822
  357.6 1.0 constant_dynamic-slice_fusion
  358.6 0.7 copy.34
  359.3 0.8 bitcast_reduce_fusion
  360.1 1.3 slice_bitcast_fusion.1
  361.4 1.3 fusion
  362.7 1.0 copy.33
  363.7 0.9 copy.39
  364.5 0.6 slice_bitcast_fusion
  365.1 1.0 slice.47
  366.1 0.7 copy.40
  366.8 5.6 %copy.43 = bf16[16,8,90,256]{3,1,2,0:T(8,128)(2,1)} copy(bf16[16,8,90,256]{3,1,2,0:T(8,128)(2,1)} %bitcast.58) | data formatting | bytes 11796480
  372.4 9.7 %copy.44 = f32[16,8,90,256]{3,1,2,0:T(8,128)} copy(f32[16,8,90,256]{3,1,2,0:T(8,128)} %bitcast.55) | data formatting | bytes 23592960

commit v3 on v2

--- a/solution.py
+++ b/solution.py
@@ -16,8 +16,8 @@
 root = math.sqrt(2.0 / math.pi)
 cubic = 0.044715
 
-OFFSET = {1: 0, 2: 1, 3: 2, 4: 3, 5: 4, 6: 4, 7: 5, 8: 6, 9: 6}
-ORDER = (8, 5, 7, 1, 4, 2, 9, 6, 3)
+OFFSET = {"1": 0, "2": 1, "3": 2, "4": 3, "5a": 4, "5b": 5, "6": 6, "7": 7, "8": 8, "9": 9}
+ORDER = ("6", "5b", "1", "2", "7", "3", "8", "9", "5a", "4")
 
 
 def fourier_tables(points, lat):
@@ -212,13 +212,18 @@
     def i_store(sample, slot):
         return pltpu.make_async_copy(i_buf.at[slot], gin_hbm.at[sample], i_sem.at[slot])
 
-    def spread_rows(stage, chunk, held):
-        for step in range(1, lon):
-            peer = lax.rem(my_lon + step, lon)
-            src = held.at[chunk * group + peer // halves, lax.rem(peer, halves)]
-            lon_copy(stage, chunk, src, lon_a.at[chunk, my_lon], peer).start()
-        src = held.at[chunk * group + my_lon // halves, lax.rem(my_lon, halves)]
-        own_copy(stage, chunk, src, lon_a.at[chunk, my_lon]).start()
+    def spread_rows(stage, chunk, held, sample):
+        src = chunk * group + sample
+        for half in range(halves):
+            peer = sample * halves + half
+
+            @pl.when(peer != my_lon)
+            def _(peer=peer, half=half):
+                lon_copy(stage, chunk, held.at[src, half], lon_a.at[chunk, my_lon], peer).start()
+
+            @pl.when(peer == my_lon)
+            def _(half=half):
+                own_copy(stage, chunk, held.at[src, half], lon_a.at[chunk, my_lon]).start()
 
     def spread_bands(stage, chunk, buffer, target):
         for step in range(1, lat):
@@ -322,24 +327,29 @@
     def both(held, sample, where):
         return jnp.concatenate([held[sample, h, where, :] for h in range(halves)], axis=1)
 
+    def normalize(sample):
+        x_load(sample).wait()
+
+        @pl.loop(0, rows // half_tile)
+        def _(i):
+            where = pl.ds(pl.multiple_of(i * half_tile, 8), half_tile)
+            normal, _ = norm_parts(x_all[sample, where, :].astype(jnp.float32))
+            low = (normal * gain_one[...] + bias_one[...]).astype(jnp.bfloat16)
+            for h in range(halves):
+                normed[sample, h, where, :] = low[:, h * LANES : (h + 1) * LANES]
+
     def stage_1(chunk):
         @pl.when(chunk > 0)
         def _():
             sent(1, lon_a.at[chunk, pl.ds(0, lon - 1)])
 
         for k in range(group):
-            sample = chunk * group + k
-            x_load(sample).wait()
-
-            @pl.loop(0, rows // half_tile)
-            def _(i):
-                where = pl.ds(pl.multiple_of(i * half_tile, 8), half_tile)
-                normal, _ = norm_parts(x_all[sample, where, :].astype(jnp.float32))
-                low = (normal * gain_one[...] + bias_one[...]).astype(jnp.bfloat16)
-                for h in range(halves):
-                    normed[sample, h, where, :] = low[:, h * LANES : (h + 1) * LANES]
-
-        spread_rows(1, chunk, normed)
+
+            @pl.when(chunk > 0)
+            def _():
+                normalize(chunk * group + k)
+
+            spread_rows(1, chunk, normed, k)
 
     def stage_2(chunk):
         to_waves(2, chunk, fwd_t, 1.0 / points, send_2)
@@ -358,14 +368,20 @@
     def stage_4(chunk):
         to_points(4, chunk, inv, None, send_4)
 
-    def stage_5(chunk):
+    def stage_5a(chunk):
         landed(4, chunk, lon_a.at[chunk, pl.ds(0, lon - 1)])
 
         @pl.when(chunk > 0)
         def _():
             sent(5, lon_a.at[chunk, pl.ds(0, lon - 1)])
 
-        for k in range(group):
+        feed_forward(chunk, range(group // 2))
+
+    def stage_5b(chunk):
+        feed_forward(chunk, range(group // 2, group))
+
+    def feed_forward(chunk, members):
+        for k in members:
             sample = chunk * group + k
             g_load(sample, k).wait()
 
@@ -408,7 +424,7 @@
             def _():
                 g_load(sample + group, k).start()
 
-        spread_rows(5, chunk, mixed)
+            spread_rows(5, chunk, mixed, k)
 
     def stage_6(chunk):
         to_waves(6, chunk, inv_t, None, send_6)
@@ -694,25 +710,44 @@
 
         return go
 
+    end = chunks - 1
     aside = {
-        (0, 1): build,
-        (chunks + 3, 5): run((fold_start, 0)),
-        (chunks + 3, 7): run((fold_end, 0), (fold_start, 1)),
-        (chunks + 3, 6): run((fold_end, 1), (fold_start, 2)),
-        (chunks + 4, 8): run((fold_end, 2), (spread_start, 2)),
-        (chunks + 4, 7): run((spec_start, None)),
-        (chunks + 4, 9): run((spread_end, 2), (spread_start, 1)),
-        (chunks + 5, 8): run((spread_end, 1), (spread_start, 0), (spec_middle, None)),
-        (chunks + 5, 7): run((spec_back, None)),
+        (0, "1"): build,
+        (end + OFFSET["5b"], "5b"): run((fold_start, 0)),
+        (end + OFFSET["5b"], "9"): run((fold_end, 0), (fold_start, 1)),
+        (end + OFFSET["6"], "8"): run((fold_end, 1), (fold_start, 2)),
+        (end + OFFSET["7"], "7"): run((spec_start, None)),
+        (end + OFFSET["7"], "8"): run((fold_end, 2), (spread_start, 2)),
+        (end + OFFSET["7"], "9"): run((spec_middle, None)),
+        (end + OFFSET["8"], "8"): run((spread_end, 2), (spread_start, 1)),
+        (end + OFFSET["8"], "9"): run((spec_back, None)),
+        (end + OFFSET["9"], "8"): run((spread_end, 1), (spread_start, 0)),
     }
 
-    stages = (stage_1, stage_2, stage_3, stage_4, stage_5, stage_6, stage_7, stage_8, stage_9)
+    stages = {
+        "1": stage_1,
+        "2": stage_2,
+        "3": stage_3,
+        "4": stage_4,
+        "5a": stage_5a,
+        "5b": stage_5b,
+        "6": stage_6,
+        "7": stage_7,
+        "8": stage_8,
+        "9": stage_9,
+    }
 
     for sample in range(batch):
         x_load(sample).start()
     for k in range(group):
         g_load(k, k).start()
 
+    padded = lon_a.shape[2]
+    if padded > rows:
+        for held in (normed, mixed):
+            held[:, :, rows:, :] = jnp.zeros_like(held[:, :, rows:, :])
+        for held in (send_4, send_8):
+            held[:, rows:, :] = jnp.zeros_like(held[:, rows:, :])
     barrier = pltpu.get_barrier_semaphore()
     for step in range(1, lon):
         pl.semaphore_signal(
@@ -722,15 +757,11 @@
         pl.semaphore_signal(
             barrier, inc=1, device_id={"lat": lax.rem(my_lat + step, lat)}, device_id_type=MESH
         )
+    for k in range(group):
+        normalize(k)
     pl.semaphore_wait(barrier, lon - 1 + lat - 1)
 
     weight_copies(True)
-    padded = lon_a.shape[2]
-    if padded > rows:
-        for held in (normed, mixed):
-            held[:, :, rows:, :] = jnp.zeros_like(held[:, :, rows:, :])
-        for held in (send_4, send_8):
-            held[:, rows:, :] = jnp.zeros_like(held[:, rows:, :])
 
     def tick(now, carry):
         for stage in ORDER:
@@ -738,7 +769,7 @@
 
             @pl.when(jnp.logical_and(chunk >= 0, chunk < chunks))
             def _(stage=stage, chunk=chunk):
-                stages[stage - 1](chunk)
+                stages[stage](chunk)
 
             for (when, after), action in aside.items():
                 if after == stage:

time: 383 us -> 369 us (0.963)
  Pallas kernels: 357 us -> 343 us
    pallas_call x1, Pallas kernels: 357 us -> 343 us  [per_device(): pl.pallas_call(functools.partial(block_kernel, lat, lon), out_shape=(jax....]
where the time goes in v3:
time: 369 us
  Pallas kernels  343 us (93%)
  local copies, waits for them, and re-layouts  23.8 us (6%)
    pallas_call x1, Pallas kernels, per_device(): pl.pallas_call(functools.partial(block_kernel, lat, lon), out_shape=(jax....  343 us
    unnamed x3, local copies, waits for them, and re-layouts  16.1 us

profile of v3, /device:TPU:0, one launch (start us, length us, event | category | flops | bytes accessed | tf_op | source)
XLA Modules:
  0.0 368.7 jit_solution(13800770870971926041)
XLA Ops:
  0.7 343.5 %shard_map.265 = (bf16[16,720,256]{2,1,0:T(8,128)(2,1)}, f32[16,720,256]{2,1,0:T(8,128)}, f32[2816,128]{1,0:T(8,128)}, f32[192,128]{1,0:T(8,128)}, f32[8,128]{1,0:T(8,128)}) custom-call(bf16[16,720,256]{2,1,0:T(8,128)(2,1)} %bitcast.56, bf16[16,720,256]{2,1,0:T(8,128)(2,1)} %bitcast.57, bf16[192,360]{1,0:T(8,128)(2,1)} %constant.24.clone.fwd_t, ...), custom_call_target="tpu_custom_call" | custom-call | tf_op jit(solution)/shard_map/pallas_call | solution.py:853
  344.1 1.0 constant_dynamic-slice_fusion
  345.1 0.7 copy.34
  345.8 0.8 bitcast_reduce_fusion
  346.6 1.3 slice_bitcast_fusion.1
  348.0 1.3 fusion
  349.2 1.0 copy.33
  350.2 0.9 copy.39
  351.1 0.6 slice_bitcast_fusion
  351.7 1.0 slice.47
  352.7 0.7 copy.40
  353.4 5.6 %copy.43 = bf16[16,8,90,256]{3,1,2,0:T(8,128)(2,1)} copy(bf16[16,8,90,256]{3,1,2,0:T(8,128)(2,1)} %bitcast.58) | data formatting | bytes 11796480
  359.0 9.7 %copy.44 = f32[16,8,90,256]{3,1,2,0:T(8,128)} copy(f32[16,8,90,256]{3,1,2,0:T(8,128)} %bitcast.55) | data formatting | bytes 23592960

commit v4 on v3

--- a/solution.py
+++ b/solution.py
@@ -16,8 +16,8 @@
 root = math.sqrt(2.0 / math.pi)
 cubic = 0.044715
 
-OFFSET = {"1": 0, "2": 1, "3": 2, "4": 3, "5a": 4, "5b": 5, "6": 6, "7": 7, "8": 8, "9": 9}
-ORDER = ("6", "5b", "1", "2", "7", "3", "8", "9", "5a", "4")
+OFFSET = {"1": 0, "2": 1, "3": 3, "4": 4, "5a": 5, "5b": 5, "6": 7, "7": 9, "8": 10, "9": 11}
+ORDER = ("1", "3", "7", "4", "5a", "6", "2", "5b", "8", "9")
 
 
 def fourier_tables(points, lat):
@@ -100,8 +100,6 @@
     out_hbm,
     gin_hbm,
     total_hbm,
-    total_spec,
-    total_norm,
     x_all,
     normed,
     mixed,
@@ -136,12 +134,14 @@
     w_imag,
     acc,
     part_core,
+    part_near,
     part_chip,
-    part_lat,
+    part_far,
     spec,
     spec_lat,
     spec_lon,
     spec_sum,
+    spec_own,
     norm_sums,
     norm_own,
     norm_lon,
@@ -171,12 +171,12 @@
     half_tile = row_tile(rows, 144)
     full_tile = row_tile(rows, 240)
 
-    def lon_copy(stage, chunk, src, dst, peer):
+    def lon_copy(stage, chunk, src, dst, peer, member=0):
         return pltpu.make_async_remote_copy(
             src_ref=src,
             dst_ref=dst,
             send_sem=send_sem.at[stage - 1],
-            recv_sem=recv_sem.at[stage - 1, chunk],
+            recv_sem=recv_sem.at[stage - 1, chunk, member],
             device_id={"lon": peer},
             device_id_type=MESH,
         )
@@ -186,16 +186,23 @@
             src_ref=src,
             dst_ref=dst,
             send_sem=send_sem.at[stage - 1],
-            recv_sem=recv_sem.at[stage - 1, chunk],
+            recv_sem=recv_sem.at[stage - 1, chunk, 0],
             device_id={"lat": peer},
             device_id_type=MESH,
         )
 
     def own_copy(stage, chunk, src, dst):
-        return pltpu.make_async_copy(src, dst, recv_sem.at[stage - 1, chunk])
-
-    def landed(stage, chunk, whole):
-        pltpu.make_async_copy(whole, whole, recv_sem.at[stage - 1, chunk]).wait()
+        return pltpu.make_async_copy(src, dst, recv_sem.at[stage - 1, chunk, 0])
+
+    def landed(stage, chunk, whole, member=0):
+        pltpu.make_async_copy(whole, whole, recv_sem.at[stage - 1, chunk, member]).wait()
+
+    def member_at(step):
+        return lax.rem(my_lon // halves + step, group)
+
+    def member_landed(stage, chunk, step):
+        count = halves if step else halves - 1
+        landed(stage, chunk, lon_a.at[chunk, pl.ds(0, count)], member_at(step))
 
     def sent(stage, part):
         lon_copy(stage, 0, part, part, my_lon).wait_send()
@@ -280,7 +287,7 @@
         sample, half = chunk * group + my_lon // halves, lax.rem(my_lon, halves)
         for step in range(1, lon):
             peer = lax.rem(my_lon + step, lon)
-            lon_copy(stage, chunk, buffer.at[peer], lon_b.at[sample, half], peer).start()
+            lon_copy(stage, chunk, buffer.at[peer], lon_b.at[sample, half], peer, my_lon // halves).start()
         own = pl.ds(pl.multiple_of(my_lon * rows, 8), rows)
         lon_b[sample, half, pl.ds(0, rows), :] = wide[own, :].astype(jnp.bfloat16)
 
@@ -343,10 +350,11 @@
         def _():
             sent(1, lon_a.at[chunk, pl.ds(0, lon - 1)])
 
-        for k in range(group):
+        for step in reversed(range(group)):
+            k = member_at(step)
 
             @pl.when(chunk > 0)
-            def _():
+            def _(k=k):
                 normalize(chunk * group + k)
 
             spread_rows(1, chunk, normed, k)
@@ -369,8 +377,6 @@
         to_points(4, chunk, inv, None, send_4)
 
     def stage_5a(chunk):
-        landed(4, chunk, lon_a.at[chunk, pl.ds(0, lon - 1)])
-
         @pl.when(chunk > 0)
         def _():
             sent(5, lon_a.at[chunk, pl.ds(0, lon - 1)])
@@ -380,13 +386,15 @@
     def stage_5b(chunk):
         feed_forward(chunk, range(group // 2, group))
 
-    def feed_forward(chunk, members):
-        for k in members:
+    def feed_forward(chunk, steps):
+        for step in steps:
+            member_landed(4, chunk, step)
+            k = member_at(step)
             sample = chunk * group + k
             g_load(sample, k).wait()
 
             @pl.when(chunk > 0)
-            def _():
+            def _(sample=sample, k=k):
                 o_store(sample, k).wait()
 
             @pl.loop(0, rows // full_tile)
@@ -421,7 +429,7 @@
             o_store(sample, k).start()
 
             @pl.when(chunk < chunks - 1)
-            def _():
+            def _(sample=sample, k=k):
                 g_load(sample + group, k).start()
 
             spread_rows(5, chunk, mixed, k)
@@ -447,12 +455,13 @@
         to_points(8, chunk, fwd, 1.0 / points, send_8)
 
     def stage_9(chunk):
-        landed(8, chunk, lon_a.at[chunk, pl.ds(0, lon - 1)])
-        for k in range(group):
+        for step in range(group):
+            member_landed(8, chunk, step)
+            k = member_at(step)
             sample = chunk * group + k
 
             @pl.when(chunk > 0)
-            def _():
+            def _(sample=sample, k=k):
                 i_store(sample, k).wait()
 
             @pl.loop(0, rows // half_tile)
@@ -519,10 +528,12 @@
 
     total_rows = acc.shape[0]
     place_core, place_chip = lax.rem(my_lon, 2), my_lon // 2
+    place_near, place_far = lax.rem(my_lat, 2), my_lat // 2
     levels = (
         (2, place_core, part_core, lambda p: {"lon": 2 * place_chip + p}),
+        (2, place_near, part_near, lambda p: {"lat": 2 * place_far + p}),
         (lon // 2, place_chip, part_chip, lambda p: {"lon": 2 * p + place_core}),
-        (lat, my_lat, part_lat, lambda p: {"lat": p}),
+        (lat // 2, place_far, part_far, lambda p: {"lat": 2 * p + place_near}),
     )
     bases, sizes = [0], [total_rows]
     for count, place, _, _ in levels:
@@ -547,6 +558,8 @@
 
     def fold_end(k):
         count, _, parts, _ = levels[k]
+        if count == 1:
+            return
         pltpu.make_async_copy(parts, parts, fold_recv.at[0, k]).wait()
         got = parts[0]
         for step in range(2, count):
@@ -567,19 +580,20 @@
                 device_id_type=MESH,
             ).start()
         if src is acc:
-            pltpu.make_async_copy(acc.at[own, :], total_hbm.at[own, :], own_sem).start()
+            pltpu.make_async_copy(acc.at[own, :], total_hbm.at[own, :], own_sem.at[0]).start()
 
     def spread_end(k):
         count = levels[k][0]
-        all_parts = total_hbm.at[pl.ds(0, (count - 1) * sizes[k + 1]), :]
-        pltpu.make_async_copy(all_parts, all_parts, fold_recv.at[1, k]).wait()
+        if count > 1:
+            all_parts = total_hbm.at[pl.ds(0, (count - 1) * sizes[k + 1]), :]
+            pltpu.make_async_copy(all_parts, all_parts, fold_recv.at[1, k]).wait()
         if k == len(levels) - 1:
             own = row_part(bases[k + 1], sizes[k + 1])
-            pltpu.make_async_copy(acc.at[own, :], total_hbm.at[own, :], own_sem).wait()
+            pltpu.make_async_copy(acc.at[own, :], total_hbm.at[own, :], own_sem.at[0]).wait()
 
     def fold_sent():
         for k, (count, _, _, _) in enumerate(levels):
-            for way in range(2):
+            for way in range(2 if count > 1 else 0):
                 part = total_hbm if way and k < len(levels) - 1 else acc
                 part = part.at[pl.ds(0, (count - 1) * sizes[k + 1]), :]
                 pltpu.make_async_remote_copy(
@@ -652,12 +666,15 @@
         got = spec_lon[0]
         for q in range(1, group):
             got = got + spec_lon[q]
-        own = row_part(my_lat * spec_rows, spec_rows)
-        total_spec[own, :] = got
-        spec_lat_copies(1, lambda p: total_spec.at[own, :], lambda s: total_spec.at[own, :])
+        spec_own[...] = got
+        own = row_part(total_rows + my_lat * spec_rows, spec_rows)
+        spec_lat_copies(1, lambda p: spec_own, lambda s: total_hbm.at[own, :])
+        pltpu.make_async_copy(spec_own, total_hbm.at[own, :], own_sem.at[1]).start()
 
     def spec_end():
-        part = total_spec.at[pl.ds(0, (lat - 1) * spec_rows), :]
+        own = row_part(total_rows + my_lat * spec_rows, spec_rows)
+        pltpu.make_async_copy(spec_own, total_hbm.at[own, :], own_sem.at[1]).wait()
+        part = spec.at[pl.ds(0, (lat - 1) * spec_rows), :]
         pltpu.make_async_copy(part, part, spec_recv.at[1]).wait()
         for way in range(2):
             pltpu.make_async_remote_copy(
@@ -699,7 +716,11 @@
             for h in range(halves):
                 norm_own[0, pl.ds(which * halves + h, 1), :] = line[:, h * LANES : (h + 1) * LANES]
         norm_fold(0, "lon", lon, my_lon, norm_own.at[0], norm_lon, norm_own.at[1])
-        norm_fold(1, "lat", lat, my_lat, norm_own.at[1], norm_lat, total_norm)
+        norm_fold(1, "lat", lat, my_lat, norm_own.at[1], norm_lat, norm_own.at[2])
+        where = pl.ds(total_rows + lat * spec_rows, 8)
+        copy = pltpu.make_async_copy(norm_own.at[2], total_hbm.at[where, :], own_sem.at[2])
+        copy.start()
+        copy.wait()
         norm_copies(0, "lon", lon, my_lon, norm_own.at[0], norm_lon, "end")
         norm_copies(1, "lat", lat, my_lat, norm_own.at[1], norm_lat, "end")
 
@@ -713,15 +734,16 @@
     end = chunks - 1
     aside = {
         (0, "1"): build,
-        (end + OFFSET["5b"], "5b"): run((fold_start, 0)),
-        (end + OFFSET["5b"], "9"): run((fold_end, 0), (fold_start, 1)),
-        (end + OFFSET["6"], "8"): run((fold_end, 1), (fold_start, 2)),
-        (end + OFFSET["7"], "7"): run((spec_start, None)),
-        (end + OFFSET["7"], "8"): run((fold_end, 2), (spread_start, 2)),
-        (end + OFFSET["7"], "9"): run((spec_middle, None)),
-        (end + OFFSET["8"], "8"): run((spread_end, 2), (spread_start, 1)),
-        (end + OFFSET["8"], "9"): run((spec_back, None)),
-        (end + OFFSET["9"], "8"): run((spread_end, 1), (spread_start, 0)),
+        (end + 5, "5b"): run((fold_start, 0)),
+        (end + 5, "9"): run((fold_end, 0), (fold_start, 1)),
+        (end + 6, "8"): run((fold_end, 1), (fold_start, 2)),
+        (end + 7, "7"): run((fold_end, 2), (fold_start, 3)),
+        (end + 7, "9"): run((fold_end, 3), (spread_start, 3)),
+        (end + 8, "9"): run((spread_end, 3), (spread_start, 2)),
+        (end + 9, "9"): run((spread_end, 2), (spread_start, 1), (spec_middle, None)),
+        (end + 10, "9"): run((spread_end, 1), (spread_start, 0)),
+        (end + 9, "7"): run((spec_start, None)),
+        (end + 10, "8"): run((spec_back, None)),
     }
 
     stages = {
@@ -737,10 +759,8 @@
         "9": stage_9,
     }
 
-    for sample in range(batch):
+    for sample in range(group):
         x_load(sample).start()
-    for k in range(group):
-        g_load(k, k).start()
 
     padded = lon_a.shape[2]
     if padded > rows:
@@ -759,6 +779,10 @@
         )
     for k in range(group):
         normalize(k)
+    for sample in range(group, batch):
+        x_load(sample).start()
+    for k in range(group):
+        g_load(k, k).start()
     pl.semaphore_wait(barrier, lon - 1 + lat - 1)
 
     weight_copies(True)
@@ -799,6 +823,83 @@
     for k in range(group):
         o_store(last * group + k, k).wait()
         i_store(last * group + k, k).wait()
+
+
+def result_kernel(
+    group,
+    narrow,
+    spec_at,
+    norm_at,
+    out_from,
+    gin_from,
+    total,
+    out_to,
+    gin_to,
+    grad_spec,
+    grad_skip,
+    grad_in,
+    grad_out,
+    in_bias,
+    vectors,
+    gin_held,
+    out_held,
+    sems,
+):
+    batch = out_from.shape[0]
+    width, hidden = grad_in.shape
+    halves = width // LANES
+    degrees = grad_spec.shape[2]
+
+    def reads(sample):
+        return (
+            pltpu.make_async_copy(gin_from.at[sample], gin_held.at[sample], sems.at[0, sample]),
+            pltpu.make_async_copy(out_from.at[sample], out_held.at[sample], sems.at[1, sample]),
+        )
+
+    def writes(sample):
+        return (
+            pltpu.make_async_copy(gin_held.at[sample], gin_to.at[sample], sems.at[2, sample]),
+            pltpu.make_async_copy(out_held.at[sample], out_to.at[sample], sems.at[3, sample]),
+        )
+
+    for sample in range(batch):
+        for copy in reads(sample):
+            copy.start()
+    for sample in range(batch):
+        for read, write in zip(reads(sample), writes(sample)):
+            read.wait()
+            write.start()
+
+    def tile(base, height, q):
+        return total[pl.ds(base + q * height, height), :]
+
+    hidden_rows = width * hidden // LANES
+    vector_rows = 2 * hidden_rows + width * width // LANES
+    for q in range(hidden // LANES):
+        where = pl.ds(q * LANES, LANES)
+        grad_in[:, where] = tile(0, width, q)
+        grad_out[where, :] = tile(hidden_rows, width, q).T
+        in_bias[:, where] = jnp.sum(tile(vector_rows, 8, q), axis=0, keepdims=True)
+    for q in range(halves):
+        where = pl.ds(q * LANES, LANES)
+        grad_skip[:, where] = tile(2 * hidden_rows, width, q)
+        for which in range(3):
+            at = vector_rows + 8 * (hidden + which * width) // LANES
+            vectors[which, :, where] = jnp.sum(tile(at, 8, q), axis=0, keepdims=True)
+        for which in range(2):
+            vectors[3 + which, :, where] = total[pl.ds(norm_at + which * halves + q, 1), :]
+    place = lax.rem(lax.axis_index("lon"), group)
+    for which in range(2):
+        turned = total[pl.ds(spec_at + which * degrees, degrees), :].T
+        for q in range(group):
+
+            @pl.when(place == q)
+            def _(q=q, which=which, turned=turned):
+                grad_spec[which] = turned[q * narrow : (q + 1) * narrow, :]
+
+    for sample in range(batch):
+        for write in writes(sample):
+            write.wait()
 
 
 def per_device(
@@ -849,18 +950,17 @@
 
     vmem = pl.BlockSpec(memory_space=pltpu.VMEM)
     hbm = pl.BlockSpec(memory_space=pl.ANY)
+    fixed = pl.BlockSpec(memory_space=pltpu.HBM)
     low, full = jnp.bfloat16, jnp.float32
     results = pl.pallas_call(
         functools.partial(block_kernel, lat, lon),
         out_shape=(
             jax.ShapeDtypeStruct((batch, rows, width), low),
             jax.ShapeDtypeStruct((batch, rows, width), full),
-            jax.ShapeDtypeStruct((total_rows, LANES), full),
-            jax.ShapeDtypeStruct((lat * spec_rows, LANES), full),
-            jax.ShapeDtypeStruct((8, LANES), full),
+            jax.ShapeDtypeStruct((total_rows + lat * spec_rows + 8, LANES), full),
         ),
         in_specs=[hbm, hbm] + [vmem] * 16,
-        out_specs=(hbm, hbm, hbm, vmem, vmem),
+        out_specs=(hbm, hbm, hbm),
         scratch_shapes=[
             pltpu.VMEM((batch, rows, width), low),
             pltpu.VMEM((batch, halves, padded, LANES), low),
@@ -881,7 +981,7 @@
             pltpu.VMEM((group, rows, width), low),
             pltpu.VMEM((group, rows, width), low),
             pltpu.VMEM((group, rows, width), full),
-            pltpu.SemaphoreType.DMA((8, chunks)),
+            pltpu.SemaphoreType.DMA((8, chunks, group)),
             pltpu.SemaphoreType.DMA((8,)),
             pltpu.SemaphoreType.DMA((batch,)),
             pltpu.SemaphoreType.DMA((group,)),
@@ -896,25 +996,27 @@
             pltpu.VMEM((degrees, LANES), full),
             pltpu.VMEM((total_rows, LANES), full),
             pltpu.VMEM((1, total_rows // 2, LANES), full),
-            pltpu.VMEM((lon // 2 - 1, total_rows // lon, LANES), full),
-            pltpu.VMEM((lat - 1, share, LANES), full),
+            pltpu.VMEM((1, total_rows // 4, LANES), full),
+            pltpu.VMEM((max(lon // 2 - 1, 1), total_rows // (2 * lon), LANES), full),
+            pltpu.VMEM((max(lat // 2 - 1, 1), share, LANES), full),
             pltpu.VMEM((lat * spec_rows, LANES), full),
             pltpu.VMEM((lat - 1, spec_rows, LANES), full),
             pltpu.VMEM((group, spec_rows, LANES), full),
             pltpu.VMEM((spec_rows, LANES), full),
+            pltpu.VMEM((spec_rows, LANES), full),
             pltpu.VMEM((2, 8, width), full),
-            pltpu.VMEM((2, 8, LANES), full),
+            pltpu.VMEM((3, 8, LANES), full),
             pltpu.VMEM((lon - 1, 8, LANES), full),
             pltpu.VMEM((lat - 1, 8, LANES), full),
             pltpu.SemaphoreType.DMA((2, group)),
-            pltpu.SemaphoreType.DMA((2, 3)),
-            pltpu.SemaphoreType.DMA((2, 3)),
+            pltpu.SemaphoreType.DMA((2, 4)),
+            pltpu.SemaphoreType.DMA((2, 4)),
             pltpu.SemaphoreType.DMA((2,)),
             pltpu.SemaphoreType.DMA((2,)),
             pltpu.SemaphoreType.DMA((2, group)),
             pltpu.SemaphoreType.DMA((2,)),
             pltpu.SemaphoreType.DMA((2, max(lat, lon) - 1)),
-            pltpu.SemaphoreType.DMA,
+            pltpu.SemaphoreType.DMA((3,)),
         ],
         compiler_params=pltpu.CompilerParams(
             collective_id=0, has_side_effects=True, vmem_limit_bytes=63 * 2**20
@@ -939,35 +1041,45 @@
         row(mlp_in_bias),
         row(mlp_out_bias),
     )
-    output, grad_inputs, total, spec, norm = results
+    shapes = (
+        ((batch, rows, width), low),
+        ((batch, rows, width), full),
+        ((2, width // lon, degrees), full),
+        ((width, width), full),
+        ((width, hidden), full),
+        ((hidden, width), full),
+        ((1, hidden), full),
+        ((5, 1, width), full),
+    )
+    output, grad_inputs, grad_spec, grad_skip, grad_in, grad_out, in_bias, vectors = pl.pallas_call(
+        functools.partial(result_kernel, group, width // lon, total_rows, total_rows + lat * spec_rows),
+        out_shape=tuple(jax.ShapeDtypeStruct(*shape) for shape in shapes),
+        in_specs=[fixed, fixed, vmem],
+        out_specs=(fixed, fixed) + (vmem,) * 6,
+        scratch_shapes=[
+            pltpu.VMEM((batch, rows, width), full),
+            pltpu.VMEM((batch, rows, width), low),
+            pltpu.SemaphoreType.DMA((4, batch)),
+        ],
+        compiler_params=pltpu.CompilerParams(vmem_limit_bytes=48 * 2**20),
+    )(*results)
 
     def unflat(values):
         return values.reshape(batch, columns, band, width).transpose(0, 2, 1, 3)
 
-    def wide_part(base, height, across):
-        part = total[base : base + height * across // LANES]
-        return part.reshape(across // LANES, height, LANES).transpose(1, 0, 2).reshape(height, across)
-
-    hidden_rows = width * hidden // LANES
-    vector_rows = 2 * hidden_rows + width * width // LANES
-    vectors = total[vector_rows:flat_rows].reshape(-1, 8, LANES).sum(axis=1).reshape(-1)
-    spec = spec[: 2 * degrees].reshape(2, degrees, LANES)
-    narrow = width // lon
-    grad_spec = lax.dynamic_slice_in_dim(spec, lax.rem(my_lon, group) * narrow, narrow, axis=2)
-    norm = norm[: 2 * halves].reshape(2, width)
     return (
         unflat(output),
         unflat(grad_inputs),
-        grad_spec,
-        wide_part(2 * hidden_rows, width, width),
-        norm[0],
-        norm[1],
-        vectors[hidden + width : hidden + 2 * width],
-        vectors[hidden + 2 * width :],
-        wide_part(0, width, hidden),
-        vectors[:hidden],
-        wide_part(hidden_rows, width, hidden).T,
-        vectors[hidden : hidden + width],
+        grad_spec.transpose(0, 2, 1),
+        grad_skip,
+        vectors[3, 0],
+        vectors[4, 0],
+        vectors[1, 0],
+        vectors[2, 0],
+        grad_in,
+        in_bias[0],
+        grad_out,
+        vectors[0, 0],
     )
 
 

time: 369 us -> 344 us (0.932)
  local copies, waits for them, and re-layouts: 23.8 us -> 1.97 us
    pallas_call x1, Pallas kernels: 343 us -> 327 us  [per_device(): pl.pallas_call(functools.partial(block_kernel, lat, lon), out_shape=(jax....]
    unnamed x3 -> x2, local copies, waits for them, and re-layouts: 16.1 us -> 1.39 us
    pallas_call x0 -> x1, Pallas kernels: none -> 13.8 us  [per_device(): pl.pallas_call(functools.partial(result_kernel, group, width // lon, tota...]
where the time goes in v4:
time: 344 us
  Pallas kernels  341 us (99%)
    pallas_call x1, Pallas kernels, per_device(): pl.pallas_call(functools.partial(block_kernel, lat, lon), out_shape=(jax....  327 us
    pallas_call x1, Pallas kernels, per_device(): pl.pallas_call(functools.partial(result_kernel, group, width // lon, tota...  13.8 us

profile of v4, /device:TPU:0, one launch (start us, length us, event | category | flops | bytes accessed | tf_op | source)
XLA Modules:
  0.0 343.7 jit_solution(15400086060879091782)
XLA Ops:
  0.6 327.3 %shard_map.265 = (bf16[16,720,256]{2,1,0:T(8,128)(2,1)}, f32[16,720,256]{2,1,0:T(8,128)}, f32[3016,128]{1,0:T(8,128)}) custom-call(bf16[16,720,256]{2,1,0:T(8,128)(2,1)} %bitcast.27, bf16[16,720,256]{2,1,0:T(8,128)(2,1)} %bitcast.28, bf16[192,360]{1,0:T(8,128)(2,1)} %constant.8.clone.fwd_t, bf16[192,360]{1,0:T(8,128)(2,1)} %constant.9.clone.inv_t, ...), custom_call_target="tpu_custom_call" | custom-call | tf_op jit(solution)/shard_map/pallas_call | solution.py:955
  327.9 0.0 copy-start
  327.9 1.4 copy-done
  329.3 13.8 %shard_map.266 = (bf16[16,720,256]{2,1,0:T(8,128)(2,1)}, f32[16,720,256]{2,1,0:T(8,128)}, f32[2,64,96]{2,1,0:T(8,128)}, f32[256,256]{1,0:T(8,128)}, f32[256,512]...) custom-call(bf16[16,720,256]{2,1,0:T(8,128)(2,1)} %get-tuple-element.23.out_from, ...), custom_call_target="tpu_custom_call" | custom-call | tf_op jit(solution)/shard_map/pallas_call | solution.py:1054
  343.1 0.6 fusion
Async XLA Ops:
  327.9 1.4 copy-start

commit v5 on v4

--- a/solution.py
+++ b/solution.py
@@ -57,6 +57,12 @@
     inner = jnp.mean(grad_norm, axis=-1, keepdims=True)
     cross = jnp.mean(grad_norm * normal, axis=-1, keepdims=True)
     return scaled * (grad_norm - inner - normal * cross)
+
+
+def norm_step(values, mixed, sent, skip, gain):
+    normal, scaled = norm_parts(values.astype(jnp.float32))
+    grad_normed = dot_t(mixed, skip) + sent.astype(jnp.float32)
+    return mixed.astype(jnp.float32) + norm_back(grad_normed, normal, scaled, gain)
 
 
 def fold(values):
@@ -100,10 +106,14 @@
     out_hbm,
     gin_hbm,
     total_hbm,
+    small_hbm,
+    last_mixed,
+    last_grid,
     x_all,
     normed,
     mixed,
     lon_a,
+    lon_c,
     lon_b,
     lat_a,
     lat_b,
@@ -137,12 +147,16 @@
     part_near,
     part_chip,
     part_far,
+    wire_chip,
+    wire_far,
+    share,
     spec,
     spec_lat,
     spec_lon,
     spec_sum,
     spec_own,
     norm_sums,
+    mixed_sums,
     norm_own,
     norm_lon,
     norm_lat,
@@ -219,18 +233,18 @@
     def i_store(sample, slot):
         return pltpu.make_async_copy(i_buf.at[slot], gin_hbm.at[sample], i_sem.at[slot])
 
-    def spread_rows(stage, chunk, held, sample):
+    def spread_rows(stage, chunk, held, sample, landing):
         src = chunk * group + sample
         for half in range(halves):
             peer = sample * halves + half
 
             @pl.when(peer != my_lon)
             def _(peer=peer, half=half):
-                lon_copy(stage, chunk, held.at[src, half], lon_a.at[chunk, my_lon], peer).start()
+                lon_copy(stage, chunk, held.at[src, half], landing.at[chunk, my_lon], peer).start()
 
             @pl.when(peer == my_lon)
             def _(half=half):
-                own_copy(stage, chunk, held.at[src, half], lon_a.at[chunk, my_lon]).start()
+                own_copy(stage, chunk, held.at[src, half], landing.at[chunk, my_lon]).start()
 
     def spread_bands(stage, chunk, buffer, target):
         for step in range(1, lat):
@@ -240,10 +254,10 @@
     def pair(values, factor):
         return jnp.concatenate([values(0), values(1)], axis=1).astype(jnp.bfloat16)
 
-    def to_waves(stage, chunk, table, scale, buffer):
-        landed(stage - 1, chunk, lon_a.at[chunk])
+    def to_waves(stage, chunk, table, scale, buffer, landing):
+        landed(stage - 1, chunk, landing.at[chunk])
         for source in range(lon):
-            wide[pl.ds(source * rows, rows), :] = lon_a[chunk, source, pl.ds(0, rows), :].astype(jnp.float32)
+            wide[pl.ds(source * rows, rows), :] = landing[chunk, source, pl.ds(0, rows), :].astype(jnp.float32)
         for first in range(0, band, 2):
             rhs = jnp.concatenate(
                 [wide[pl.ds(first + k, points, stride=band), :] for k in range(2)], axis=1
@@ -283,13 +297,42 @@
             sent(stage, buffer.at[pl.ds(0, lon - 1)])
 
         for target in range(lon):
-            buffer[target, pl.ds(0, rows), :] = wide[pl.ds(target * rows, rows), :].astype(jnp.bfloat16)
-        sample, half = chunk * group + my_lon // halves, lax.rem(my_lon, halves)
-        for step in range(1, lon):
-            peer = lax.rem(my_lon + step, lon)
-            lon_copy(stage, chunk, buffer.at[peer], lon_b.at[sample, half], peer, my_lon // halves).start()
-        own = pl.ds(pl.multiple_of(my_lon * rows, 8), rows)
-        lon_b[sample, half, pl.ds(0, rows), :] = wide[own, :].astype(jnp.bfloat16)
+            grid = wide[pl.ds(target * rows, rows), :]
+            buffer[target, pl.ds(0, rows), :] = grid.astype(jnp.bfloat16)
+            if stage == 8:
+                before = lon_a[chunk, target, pl.ds(0, rows), :].astype(jnp.float32)
+                norm_sums[0] += fold(grid * before)
+                norm_sums[1] += fold(grid)
+        member, half = my_lon // halves, lax.rem(my_lon, halves)
+
+        def send(landing):
+            for step in range(1, lon):
+                peer = lax.rem(my_lon + step, lon)
+                lon_copy(stage, chunk, buffer.at[peer], landing, peer, member).start()
+
+        def send_here():
+            send(lon_b.at[chunk * group + member, half])
+            own = pl.ds(pl.multiple_of(my_lon * rows, 8), rows)
+            lon_b[chunk * group + member, half, pl.ds(0, rows), :] = wide[own, :].astype(jnp.bfloat16)
+
+        if stage == 4:
+            send_here()
+        else:
+            pl.when(chunk < chunks - 1)(send_here)
+
+            @pl.when(chunk == chunks - 1)
+            def _():
+                norm_start()
+                send(last_grid.at[member, half])
+                last_own().start()
+
+    def last_own():
+        held = last_grid.at[my_lon // halves, lax.rem(my_lon, halves)]
+        return pltpu.make_async_copy(send_8.at[my_lon], held, own_sem.at[3])
+
+    def last_mixed_copy():
+        part = mixed.at[pl.ds((chunks - 1) * group, group)]
+        return pltpu.make_async_copy(part, last_mixed, own_sem.at[4])
 
     def slab_step(stage, chunk, first_table, second_table, between, buffer):
         landed(stage - 1, chunk, lat_a.at[chunk, pl.ds(0, lat - 1)])
@@ -357,10 +400,10 @@
             def _(k=k):
                 normalize(chunk * group + k)
 
-            spread_rows(1, chunk, normed, k)
+            spread_rows(1, chunk, normed, k, lon_a)
 
     def stage_2(chunk):
-        to_waves(2, chunk, fwd_t, 1.0 / points, send_2)
+        to_waves(2, chunk, fwd_t, 1.0 / points, send_2, lon_a)
 
     def stage_3(chunk):
         def between(m, got):
@@ -423,6 +466,7 @@
                     gather_rows(vector_rows + 8 * (hidden + at * width) // LANES, fold(values))
                 grad_mixed = (g_full + norm_back(grad_second, normal, scaled, gain_two[...])).astype(jnp.bfloat16)
                 gather_rows(2 * hidden_rows, t_dot(low_one, grad_mixed))
+                mixed_sums[...] += fold(grad_mixed.astype(jnp.float32))
                 for h in range(halves):
                     mixed[sample, h, where, :] = grad_mixed[:, h * LANES : (h + 1) * LANES]
 
@@ -432,10 +476,10 @@
             def _(sample=sample, k=k):
                 g_load(sample + group, k).start()
 
-            spread_rows(5, chunk, mixed, k)
+            spread_rows(5, chunk, mixed, k, lon_c)
 
     def stage_6(chunk):
-        to_waves(6, chunk, inv_t, None, send_6)
+        to_waves(6, chunk, inv_t, None, send_6, lon_c)
 
     def stage_7(chunk):
         def between(m, got):
@@ -467,13 +511,12 @@
             @pl.loop(0, rows // half_tile)
             def _(i):
                 where = pl.ds(pl.multiple_of(i * half_tile, 8), half_tile)
-                normal, scaled = norm_parts(x_all[sample, where, :].astype(jnp.float32))
-                low = both(mixed, sample, where)
-                grad_normed = dot_t(low, skip[...]) + both(lon_b, sample, where).astype(jnp.float32)
-                norm_sums[0] += fold(grad_normed * normal)
-                norm_sums[1] += fold(grad_normed)
-                i_buf[k, where, :] = low.astype(jnp.float32) + norm_back(
-                    grad_normed, normal, scaled, gain_one[...]
+                i_buf[k, where, :] = norm_step(
+                    x_all[sample, where, :],
+                    both(mixed, sample, where),
+                    both(lon_b, sample, where),
+                    skip[...],
+                    gain_one[...],
                 )
 
             i_store(sample, k).start()
@@ -509,6 +552,7 @@
         acc[...] = jnp.zeros_like(acc)
         spec[...] = jnp.zeros_like(spec)
         norm_sums[...] = jnp.zeros_like(norm_sums)
+        mixed_sums[...] = jnp.zeros_like(mixed_sums)
         norm_own[...] = jnp.zeros_like(norm_own)
         degree = lax.broadcasted_iota(jnp.int32, (lats, degrees), 1)
 
@@ -530,25 +574,31 @@
     place_core, place_chip = lax.rem(my_lon, 2), my_lon // 2
     place_near, place_far = lax.rem(my_lat, 2), my_lat // 2
     levels = (
-        (2, place_core, part_core, lambda p: {"lon": 2 * place_chip + p}),
-        (2, place_near, part_near, lambda p: {"lat": 2 * place_far + p}),
-        (lon // 2, place_chip, part_chip, lambda p: {"lon": 2 * p + place_core}),
-        (lat // 2, place_far, part_far, lambda p: {"lat": 2 * p + place_near}),
+        (2, place_core, part_core, None, lambda p: {"lon": 2 * place_chip + p}),
+        (2, place_near, part_near, None, lambda p: {"lat": 2 * place_far + p}),
+        (lon // 2, place_chip, part_chip, wire_chip, lambda p: {"lon": 2 * p + place_core}),
+        (lat // 2, place_far, part_far, wire_far, lambda p: {"lat": 2 * p + place_near}),
     )
     bases, sizes = [0], [total_rows]
-    for count, place, _, _ in levels:
+    for count, place, _, _, _ in levels:
         sizes.append(sizes[-1] // count)
         bases.append(bases[-1] + place * sizes[-1])
 
     def row_part(at, count):
-        return pl.ds(pl.multiple_of(at, 8), count)
+        return pl.ds(pl.multiple_of(at, 16), count)
 
     def fold_start(k):
-        count, place, parts, device = levels[k]
+        count, place, parts, wire, device = levels[k]
+        if wire is not None:
+            wire[...] = acc[row_part(bases[k], sizes[k]), :].astype(jnp.bfloat16)
         for step in range(1, count):
             peer = lax.rem(place + step, count)
+            if wire is None:
+                src = acc.at[row_part(bases[k] + peer * sizes[k + 1], sizes[k + 1]), :]
+            else:
+                src = wire.at[row_part(peer * sizes[k + 1], sizes[k + 1]), :]
             pltpu.make_async_remote_copy(
-                src_ref=acc.at[row_part(bases[k] + peer * sizes[k + 1], sizes[k + 1]), :],
+                src_ref=src,
                 dst_ref=parts.at[step - 1],
                 send_sem=fold_send.at[0, k],
                 recv_sem=fold_recv.at[0, k],
@@ -557,30 +607,32 @@
             ).start()
 
     def fold_end(k):
-        count, _, parts, _ = levels[k]
+        count, _, parts, _, _ = levels[k]
         if count == 1:
             return
         pltpu.make_async_copy(parts, parts, fold_recv.at[0, k]).wait()
-        got = parts[0]
+        got = parts[0].astype(jnp.float32)
         for step in range(2, count):
-            got = got + parts[step - 1]
+            got = got + parts[step - 1].astype(jnp.float32)
         acc[row_part(bases[k + 1], sizes[k + 1]), :] += got
 
     def spread_start(k):
-        count, place, _, device = levels[k]
+        count, place, _, _, device = levels[k]
         own = row_part(bases[k + 1], sizes[k + 1])
-        src = acc if k == len(levels) - 1 else total_hbm
+        src = total_hbm.at[own, :]
+        if k == len(levels) - 1:
+            share[...] = acc[own, :].astype(jnp.bfloat16)
+            src = share
+            pltpu.make_async_copy(share, total_hbm.at[own, :], own_sem.at[0]).start()
         for step in range(1, count):
             pltpu.make_async_remote_copy(
-                src_ref=src.at[own, :],
+                src_ref=src,
                 dst_ref=total_hbm.at[own, :],
                 send_sem=fold_send.at[1, k],
                 recv_sem=fold_recv.at[1, k],
                 device_id=device(lax.rem(place + step, count)),
                 device_id_type=MESH,
             ).start()
-        if src is acc:
-            pltpu.make_async_copy(acc.at[own, :], total_hbm.at[own, :], own_sem.at[0]).start()
 
     def spread_end(k):
         count = levels[k][0]
@@ -589,13 +641,14 @@
             pltpu.make_async_copy(all_parts, all_parts, fold_recv.at[1, k]).wait()
         if k == len(levels) - 1:
             own = row_part(bases[k + 1], sizes[k + 1])
-            pltpu.make_async_copy(acc.at[own, :], total_hbm.at[own, :], own_sem.at[0]).wait()
+            pltpu.make_async_copy(share, total_hbm.at[own, :], own_sem.at[0]).wait()
 
     def fold_sent():
-        for k, (count, _, _, _) in enumerate(levels):
-            for way in range(2 if count > 1 else 0):
-                part = total_hbm if way and k < len(levels) - 1 else acc
-                part = part.at[pl.ds(0, (count - 1) * sizes[k + 1]), :]
+        for k, (count, _, _, wire, _) in enumerate(levels):
+            for way, held in ((0, acc if wire is None else wire), (1, total_hbm)):
+                if count == 1:
+                    continue
+                part = held.at[pl.ds(0, (count - 1) * sizes[k + 1]), :]
                 pltpu.make_async_remote_copy(
                     src_ref=part,
                     dst_ref=part,
@@ -606,6 +659,9 @@
                 ).wait_send()
 
     spec_rows = spec_sum.shape[0]
+
+    def spec_part(at):
+        return pl.ds(pl.multiple_of(at * spec_rows, 8), spec_rows)
 
     def spec_lat_copies(way, src, dst):
         for step in range(1, lat):
@@ -621,7 +677,7 @@
 
     def spec_start():
         spec_lat_copies(
-            0, lambda p: spec.at[row_part(p * spec_rows, spec_rows), :], lambda s: spec_lat.at[s - 1]
+            0, lambda p: spec.at[spec_part(p), :], lambda s: spec_lat.at[s - 1]
         )
 
     def spec_pairs(action):
@@ -654,7 +710,7 @@
 
     def spec_middle():
         pltpu.make_async_copy(spec_lat, spec_lat, spec_recv.at[0]).wait()
-        got = spec[row_part(my_lat * spec_rows, spec_rows), :]
+        got = spec[spec_part(my_lat), :]
         for step in range(1, lat):
             got = got + spec_lat[step - 1]
         spec_sum[...] = got
@@ -667,13 +723,12 @@
         for q in range(1, group):
             got = got + spec_lon[q]
         spec_own[...] = got
-        own = row_part(total_rows + my_lat * spec_rows, spec_rows)
-        spec_lat_copies(1, lambda p: spec_own, lambda s: total_hbm.at[own, :])
-        pltpu.make_async_copy(spec_own, total_hbm.at[own, :], own_sem.at[1]).start()
+        own = spec_part(my_lat)
+        spec_lat_copies(1, lambda p: spec_own, lambda s: small_hbm.at[own, :])
+        pltpu.make_async_copy(spec_own, small_hbm.at[own, :], own_sem.at[1]).start()
 
     def spec_end():
-        own = row_part(total_rows + my_lat * spec_rows, spec_rows)
-        pltpu.make_async_copy(spec_own, total_hbm.at[own, :], own_sem.at[1]).wait()
+        pltpu.make_async_copy(spec_own, small_hbm.at[spec_part(my_lat), :], own_sem.at[1]).wait()
         part = spec.at[pl.ds(0, (lat - 1) * spec_rows), :]
         pltpu.make_async_copy(part, part, spec_recv.at[1]).wait()
         for way in range(2):
@@ -702,27 +757,54 @@
             else:
                 copy.wait_send()
 
-    def norm_fold(way, axis, count, place, src, parts, out):
-        norm_copies(way, axis, count, place, src, parts, "start")
+    def norm_end(way, parts, count):
         pltpu.make_async_copy(parts, parts, norm_recv.at[way]).wait()
-        got = src[...]
+        got = norm_own[way]
         for step in range(1, count):
             got = got + parts[step - 1]
-        out[...] = got
-
-    def norm_all():
+        norm_own[way + 1] = got
+
+    def norm_skip():
+        lines = [jnp.zeros((1, width), jnp.float32) for _ in range(2)]
+        all_mixed = jnp.sum(mixed_sums[...], axis=0, keepdims=True)
+        for q in range(halves):
+            lanes = slice(q * LANES, (q + 1) * LANES)
+            part = skip[:, lanes].astype(jnp.float32)
+            held = acc[pl.ds(2 * hidden_rows + q * width, width), :]
+            for which, values in enumerate((held, all_mixed[:, lanes])):
+                lines[which] += jnp.sum((part * values).T, axis=0, keepdims=True)
         for which in range(2):
-            line = jnp.sum(norm_sums[which], axis=0, keepdims=True)
-            for h in range(halves):
-                norm_own[0, pl.ds(which * halves + h, 1), :] = line[:, h * LANES : (h + 1) * LANES]
-        norm_fold(0, "lon", lon, my_lon, norm_own.at[0], norm_lon, norm_own.at[1])
-        norm_fold(1, "lat", lat, my_lat, norm_own.at[1], norm_lat, norm_own.at[2])
-        where = pl.ds(total_rows + lat * spec_rows, 8)
-        copy = pltpu.make_async_copy(norm_own.at[2], total_hbm.at[where, :], own_sem.at[2])
+            for half in range(halves):
+                norm_own[0, pl.ds(which * halves + half, 1), :] = lines[which][
+                    :, half * LANES : (half + 1) * LANES
+                ]
+
+    def norm_start():
+        for half in range(halves):
+
+            @pl.when(lax.rem(my_lon, halves) == half)
+            def _(half=half):
+                for which in range(2):
+                    line = jnp.sum(norm_sums[which], axis=0, keepdims=True)
+                    norm_own[0, pl.ds(which * halves + half, 1), :] += line
+
+        norm_copies(0, "lon", lon, my_lon, norm_own.at[0], norm_lon, "start")
+
+    def norm_middle():
+        norm_end(0, norm_lon, lon)
+        norm_copies(1, "lat", lat, my_lat, norm_own.at[1], norm_lat, "start")
+
+    def norm_finish():
+        norm_end(1, norm_lat, lat)
+        where = pl.ds(lat * spec_rows, 8)
+        copy = pltpu.make_async_copy(norm_own.at[2], small_hbm.at[where, :], own_sem.at[2])
         copy.start()
-        copy.wait()
         norm_copies(0, "lon", lon, my_lon, norm_own.at[0], norm_lon, "end")
         norm_copies(1, "lat", lat, my_lat, norm_own.at[1], norm_lat, "end")
+        copy.wait()
+
+    def last_mixed_start():
+        last_mixed_copy().start()
 
     def run(*steps):
         def go():
@@ -734,16 +816,16 @@
     end = chunks - 1
     aside = {
         (0, "1"): build,
-        (end + 5, "5b"): run((fold_start, 0)),
+        (end + 5, "5b"): run((last_mixed_start, None), (norm_skip, None), (fold_start, 0)),
         (end + 5, "9"): run((fold_end, 0), (fold_start, 1)),
         (end + 6, "8"): run((fold_end, 1), (fold_start, 2)),
         (end + 7, "7"): run((fold_end, 2), (fold_start, 3)),
         (end + 7, "9"): run((fold_end, 3), (spread_start, 3)),
         (end + 8, "9"): run((spread_end, 3), (spread_start, 2)),
-        (end + 9, "9"): run((spread_end, 2), (spread_start, 1), (spec_middle, None)),
-        (end + 10, "9"): run((spread_end, 1), (spread_start, 0)),
+        (end + 9, "8"): run((spread_end, 2), (spread_start, 1)),
+        (end + 9, "9"): run((spread_end, 1), (spread_start, 0), (spec_middle, None)),
         (end + 9, "7"): run((spec_start, None)),
-        (end + 10, "8"): run((spec_back, None)),
+        (end + 10, "8"): run((norm_middle, None), (spec_back, None)),
     }
 
     stages = {
@@ -791,7 +873,7 @@
         for stage in ORDER:
             chunk = now - OFFSET[stage]
 
-            @pl.when(jnp.logical_and(chunk >= 0, chunk < chunks))
+            @pl.when(jnp.logical_and(chunk >= 0, chunk < (end if stage == "9" else chunks)))
             def _(stage=stage, chunk=chunk):
                 stages[stage](chunk)
 
@@ -803,10 +885,14 @@
 
     lax.fori_loop(0, chunks + max(OFFSET.values()), tick, 0)
 
-    norm_all()
     spread_end(0)
+    norm_finish()
     spec_end()
     fold_sent()
+    for step in range(group):
+        member_landed(8, end, step)
+    last_own().wait()
+    last_mixed_copy().wait()
     weight_copies(False)
     last = chunks - 1
     for stage in (1, 5):
@@ -822,17 +908,24 @@
         sent(stage, buffer.at[pl.ds(0, count)])
     for k in range(group):
         o_store(last * group + k, k).wait()
-        i_store(last * group + k, k).wait()
+        if chunks > 1:
+            i_store((last - 1) * group + k, k).wait()
 
 
 def result_kernel(
     group,
     narrow,
-    spec_at,
     norm_at,
     out_from,
     gin_from,
     total,
+    small,
+    last_mixed,
+    last_grid,
+    x_hbm,
+    skip,
+    gain,
+    bias,
     out_to,
     gin_to,
     grad_spec,
@@ -843,38 +936,72 @@
     vectors,
     gin_held,
     out_held,
+    x_held,
+    mixed_held,
+    grid_held,
     sems,
+    last_sems,
 ):
-    batch = out_from.shape[0]
-    width, hidden = grad_in.shape
+    batch, rows, width = out_from.shape
+    hidden = grad_in.shape[1]
     halves = width // LANES
     degrees = grad_spec.shape[2]
+    first = batch - group
 
     def reads(sample):
-        return (
-            pltpu.make_async_copy(gin_from.at[sample], gin_held.at[sample], sems.at[0, sample]),
-            pltpu.make_async_copy(out_from.at[sample], out_held.at[sample], sems.at[1, sample]),
+        out = pltpu.make_async_copy(out_from.at[sample], out_held.at[sample], sems.at[1, sample])
+        if sample >= first:
+            return (out,)
+        return (pltpu.make_async_copy(gin_from.at[sample], gin_held.at[sample], sems.at[0, sample]), out)
+
+    def gin_write(sample):
+        return pltpu.make_async_copy(gin_held.at[sample], gin_to.at[sample], sems.at[2, sample])
+
+    def writes(sample):
+        out = pltpu.make_async_copy(out_held.at[sample], out_to.at[sample], sems.at[3, sample])
+        return (out,) if sample >= first else (gin_write(sample), out)
+
+    last = [
+        pltpu.make_async_copy(source, held, last_sems.at[at])
+        for at, (source, held) in enumerate(
+            ((x_hbm.at[pl.ds(first, group)], x_held), (last_mixed, mixed_held), (last_grid, grid_held))
         )
-
-    def writes(sample):
-        return (
-            pltpu.make_async_copy(gin_held.at[sample], gin_to.at[sample], sems.at[2, sample]),
-            pltpu.make_async_copy(out_held.at[sample], out_to.at[sample], sems.at[3, sample]),
-        )
-
+    ]
+    for copy in last:
+        copy.start()
     for sample in range(batch):
         for copy in reads(sample):
             copy.start()
+    for copy in last:
+        copy.wait()
+
+    back_tile = row_tile(rows, 144)
+    for k in range(group):
+
+        @pl.loop(0, rows // back_tile)
+        def _(i, k=k):
+            where = pl.ds(pl.multiple_of(i * back_tile, 8), back_tile)
+            gin_held[first + k, where, :] = norm_step(
+                x_held[k, where, :],
+                jnp.concatenate([mixed_held[k, h, where, :] for h in range(halves)], axis=1),
+                jnp.concatenate([grid_held[k, h, where, :] for h in range(halves)], axis=1),
+                skip[...],
+                gain[...],
+            )
+
+        gin_write(first + k).start()
+
     for sample in range(batch):
         for read, write in zip(reads(sample), writes(sample)):
             read.wait()
             write.start()
 
     def tile(base, height, q):
-        return total[pl.ds(base + q * height, height), :]
+        return total[pl.ds(base + q * height, height), :].astype(jnp.float32)
 
     hidden_rows = width * hidden // LANES
     vector_rows = 2 * hidden_rows + width * width // LANES
+
     for q in range(hidden // LANES):
         where = pl.ds(q * LANES, LANES)
         grad_in[:, where] = tile(0, width, q)
@@ -886,11 +1013,12 @@
         for which in range(3):
             at = vector_rows + 8 * (hidden + which * width) // LANES
             vectors[which, :, where] = jnp.sum(tile(at, 8, q), axis=0, keepdims=True)
-        for which in range(2):
-            vectors[3 + which, :, where] = total[pl.ds(norm_at + which * halves + q, 1), :]
+        all_normed, everything = (small[pl.ds(norm_at + which * halves + q, 1), :] for which in range(2))
+        vectors[3, :, where] = (all_normed - bias[:, where] * everything) / gain[:, where]
+        vectors[4, :, where] = everything
     place = lax.rem(lax.axis_index("lon"), group)
     for which in range(2):
-        turned = total[pl.ds(spec_at + which * degrees, degrees), :].T
+        turned = small[pl.ds(which * degrees, degrees), :].T
         for q in range(group):
 
             @pl.when(place == q)
@@ -900,6 +1028,8 @@
     for sample in range(batch):
         for write in writes(sample):
             write.wait()
+    for k in range(group):
+        gin_write(first + k).wait()
 
 
 def per_device(
@@ -938,7 +1068,7 @@
     my_lon = lax.axis_index("lon")
     hidden = mlp_in.shape[1]
     flat_rows = (2 * hidden + width) * width // LANES + 8 * (hidden + 3 * width) // LANES
-    share = -(-flat_rows // (8 * lat * lon)) * 8
+    share = -(-flat_rows // (16 * lat * lon)) * 16
     total_rows = share * lat * lon
     spec_rows = -(-2 * degrees // (8 * lat)) * 8
 
@@ -956,15 +1086,19 @@
         functools.partial(block_kernel, lat, lon),
         out_shape=(
             jax.ShapeDtypeStruct((batch, rows, width), low),
-            jax.ShapeDtypeStruct((batch, rows, width), full),
-            jax.ShapeDtypeStruct((total_rows + lat * spec_rows + 8, LANES), full),
+            jax.ShapeDtypeStruct((max(batch - group, 1), rows, width), full),
+            jax.ShapeDtypeStruct((total_rows, LANES), low),
+            jax.ShapeDtypeStruct((lat * spec_rows + 8, LANES), full),
+            jax.ShapeDtypeStruct((group, halves, padded, LANES), low),
+            jax.ShapeDtypeStruct((group, halves, padded, LANES), low),
         ),
         in_specs=[hbm, hbm] + [vmem] * 16,
-        out_specs=(hbm, hbm, hbm),
+        out_specs=(hbm,) * 6,
         scratch_shapes=[
             pltpu.VMEM((batch, rows, width), low),
             pltpu.VMEM((batch, halves, padded, LANES), low),
             pltpu.VMEM((batch, halves, padded, LANES), low),
+            pltpu.VMEM((chunks, lon, padded, LANES), low),
             pltpu.VMEM((chunks, lon, padded, LANES), low),
             pltpu.VMEM((batch, halves, padded, LANES), low),
             pltpu.VMEM((chunks, lat, block, LANES), low),
@@ -997,14 +1131,18 @@
             pltpu.VMEM((total_rows, LANES), full),
             pltpu.VMEM((1, total_rows // 2, LANES), full),
             pltpu.VMEM((1, total_rows // 4, LANES), full),
-            pltpu.VMEM((max(lon // 2 - 1, 1), total_rows // (2 * lon), LANES), full),
-            pltpu.VMEM((max(lat // 2 - 1, 1), share, LANES), full),
+            pltpu.VMEM((max(lon // 2 - 1, 1), total_rows // (2 * lon), LANES), low),
+            pltpu.VMEM((max(lat // 2 - 1, 1), share, LANES), low),
+            pltpu.VMEM((total_rows // 4, LANES), low),
+            pltpu.VMEM((total_rows // (2 * lon), LANES), low),
+            pltpu.VMEM((share, LANES), low),
             pltpu.VMEM((lat * spec_rows, LANES), full),
             pltpu.VMEM((lat - 1, spec_rows, LANES), full),
             pltpu.VMEM((group, spec_rows, LANES), full),
             pltpu.VMEM((spec_rows, LANES), full),
             pltpu.VMEM((spec_rows, LANES), full),
-            pltpu.VMEM((2, 8, width), full),
+            pltpu.VMEM((2, 8, LANES), full),
+            pltpu.VMEM((8, width), full),
             pltpu.VMEM((3, 8, LANES), full),
             pltpu.VMEM((lon - 1, 8, LANES), full),
             pltpu.VMEM((lat - 1, 8, LANES), full),
@@ -1016,7 +1154,7 @@
             pltpu.SemaphoreType.DMA((2, group)),
             pltpu.SemaphoreType.DMA((2,)),
             pltpu.SemaphoreType.DMA((2, max(lat, lon) - 1)),
-            pltpu.SemaphoreType.DMA((3,)),
+            pltpu.SemaphoreType.DMA((5,)),
         ],
         compiler_params=pltpu.CompilerParams(
             collective_id=0, has_side_effects=True, vmem_limit_bytes=63 * 2**20
@@ -1052,17 +1190,21 @@
         ((5, 1, width), full),
     )
     output, grad_inputs, grad_spec, grad_skip, grad_in, grad_out, in_bias, vectors = pl.pallas_call(
-        functools.partial(result_kernel, group, width // lon, total_rows, total_rows + lat * spec_rows),
+        functools.partial(result_kernel, group, width // lon, lat * spec_rows),
         out_shape=tuple(jax.ShapeDtypeStruct(*shape) for shape in shapes),
-        in_specs=[fixed, fixed, vmem],
+        in_specs=[fixed, fixed, vmem, vmem, fixed, fixed, fixed, vmem, vmem, vmem],
         out_specs=(fixed, fixed) + (vmem,) * 6,
         scratch_shapes=[
             pltpu.VMEM((batch, rows, width), full),
             pltpu.VMEM((batch, rows, width), low),
+            pltpu.VMEM((group, rows, width), low),
+            pltpu.VMEM((group, halves, padded, LANES), low),
+            pltpu.VMEM((group, halves, padded, LANES), low),
             pltpu.SemaphoreType.DMA((4, batch)),
+            pltpu.SemaphoreType.DMA((3,)),
         ],
         compiler_params=pltpu.CompilerParams(vmem_limit_bytes=48 * 2**20),
-    )(*results)
+    )(*results, flat(inputs), skip_weight, row(gain_first), row(bias_first))
 
     def unflat(values):
         return values.reshape(batch, columns, band, width).transpose(0, 2, 1, 3)

time: 344 us -> 333 us (0.968)
  Pallas kernels: 341 us -> 327 us
    pallas_call x1, Pallas kernels: 327 us -> 315 us  [per_device(): pl.pallas_call(functools.partial(block_kernel, lat, lon), out_shape=(jax....]
where the time goes in v5:
time: 333 us
  Pallas kernels  327 us (98%)
  local copies, waits for them, and re-layouts  4.84 us (1%)
    pallas_call x1, Pallas kernels, per_device(): pl.pallas_call(functools.partial(block_kernel, lat, lon), out_shape=(jax....  315 us
    pallas_call x1, Pallas kernels, per_device(): pl.pallas_call(functools.partial(result_kernel, group, width // lon, lat...  12.8 us

profile of v5, /device:TPU:0, one launch (start us, length us, event | category | flops | bytes accessed | tf_op | source)
XLA Modules:
  0.0 333.0 jit_solution(15534698993092657258)
XLA Ops:
  0.6 0.0 copy-start.3
  0.7 0.0 copy-start.5
  0.7 0.0 copy-start.6
  0.7 314.7 %shard_map.265 = (bf16[16,720,256]{2,1,0:T(8,128)(2,1)}, f32[14,720,256]{2,1,0:T(8,128)}, bf16[3072,128]{1,0:T(8,128)(2,1)}, f32[200,128]{1,0:T(8,128)}, bf16[2,...) custom-call(bf16[16,720,256]{2,1,0:T(8,128)(2,1)} %bitcast.31, bf16[16,720,256]{2,1,0:T(8,128)(2,1)} %bitcast.33, ...), custom_call_target="tpu_custom_call" | custom-call | tf_op jit(solution)/shard_map/pallas_call | solution.py:1085
  315.4 0.0 copy-done.3
  315.4 0.0 copy-done.5
  315.4 0.0 copy-done.6
  315.4 0.0 copy-start
  315.4 1.1 copy-done
  316.6 0.0 copy-start.1
  316.6 1.1 copy-done.1
  317.7 0.0 copy-start.2
  317.7 1.1 copy-done.2
  318.8 0.0 copy-start.4
  318.8 0.9 copy-done.4
  319.7 12.8 %shard_map.266 = (bf16[16,720,256]{2,1,0:T(8,128)(2,1)}, f32[16,720,256]{2,1,0:T(8,128)}, f32[2,64,96]{2,1,0:T(8,128)}, f32[256,256]{1,0:T(8,128)}, f32[256,512]...) custom-call(bf16[16,720,256]{2,1,0:T(8,128)(2,1)} %get-tuple-element.26.out_from, ...), custom_call_target="tpu_custom_call" | custom-call | tf_op jit(solution)/shard_map/pallas_call | solution.py:1192
  332.5 0.6 fusion
Async XLA Ops:
  0.6 314.8 %copy-start.3 = (bf16[256,256]{1,0:T(8,128)(2,1)S(1)}, bf16[256,256]{1,0:T(8,128)(2,1)}, u32[]{:S(2)}) copy-start(bf16[256,256]{1,0:T(8,128)(2,1)} %skip.3) | copy-start | bytes 393220
  0.7 314.8 %copy-start.5 = (f32[256]{0:T(256)S(1)}, f32[256]{0:T(256)}, u32[]{:S(2)}) copy-start(f32[256]{0:T(256)} %param.23) | copy-start | bytes 3076
  0.7 314.8 %copy-start.6 = (f32[256]{0:T(256)S(1)}, f32[256]{0:T(256)}, u32[]{:S(2)}) copy-start(f32[256]{0:T(256)} %param.24) | copy-start | bytes 3076
  315.4 1.1 copy-start
  316.6 1.1 copy-start.1
  317.7 1.1 copy-start.2
  318.8 0.9 copy-start.4

commit v6 on v5

--- a/solution.py
+++ b/solution.py
@@ -16,28 +16,33 @@
 root = math.sqrt(2.0 / math.pi)
 cubic = 0.044715
 
-OFFSET = {"1": 0, "2": 1, "3": 3, "4": 4, "5a": 5, "5b": 5, "6": 7, "7": 9, "8": 10, "9": 11}
-ORDER = ("1", "3", "7", "4", "5a", "6", "2", "5b", "8", "9")
-
-
-def fourier_tables(points, lat):
-    def build(orders):
-        waves = np.arange(orders)
-        phase = (waves[:, None] * np.arange(points)[None, :] % points).astype(np.float32)
-        phase = phase * np.float32(2.0 * math.pi / points)
-        cosine, sine = np.cos(phase), np.sin(phase)
-        factor = np.where(waves == 0, 1.0, 2.0).astype(np.float32)[:, None]
-        slab = orders // lat
-
-        def arrange(parts):
-            stacked = np.stack(parts).reshape(2, lat, slab, points).transpose(1, 0, 2, 3)
-            return stacked.reshape(2 * orders, points).astype(ml_dtypes.bfloat16)
-
-        forward = arrange([cosine, -sine])
-        inverse = arrange([factor * cosine, -factor * sine])
-        return forward, inverse
-
-    return build
+OFFSET = {"1": 0, "2": 1, "3a": 3, "3b": 4, "4": 5, "5a": 6, "5b": 6, "6": 8, "7a": 10, "7b": 11, "8": 12, "9": 13}
+ORDER = ("1", "3b", "3a", "7b", "7a", "4", "5a", "6", "2", "5b", "8", "9")
+
+
+def split_orders(orders, lat):
+    high = 2 * orders // 3
+    each = high // lat
+    assert each * lat == high and 3 * high == 2 * orders
+    return high, each
+
+
+def fourier_tables(points, orders, lat):
+    waves = np.arange(orders)
+    phase = (waves[:, None] * np.arange(points)[None, :] % points).astype(np.float32)
+    phase = phase * np.float32(2.0 * math.pi / points)
+    cosine, sine = np.cos(phase), np.sin(phase)
+    factor = np.where(waves == 0, 1.0, 2.0).astype(np.float32)[:, None]
+    high, each = split_orders(orders, lat)
+    near = lat // 2
+    owned = [[t * each + i for i in range(each)] for t in range(lat)]
+    owned += [[high + near * i + d for i in range(each)] for d in range(near)]
+
+    def arrange(*parts):
+        stacked = [part[waves] for waves in owned for part in parts]
+        return np.concatenate(stacked).astype(ml_dtypes.bfloat16)
+
+    return arrange(cosine, -sine), arrange(factor * cosine, -factor * sine)
 
 
 def row_tile(rows, most):
@@ -111,13 +116,17 @@
     last_grid,
     x_all,
     normed,
-    mixed,
     lon_a,
     lon_c,
     lon_b,
     lat_a,
     lat_b,
     coeffs,
+    coeffs_high,
+    pack_own,
+    pack_far,
+    stack,
+    stack_held,
     send_2,
     send_3,
     send_4,
@@ -135,10 +144,17 @@
     g_sem,
     o_sem,
     i_sem,
+    tabs,
     ana,
     ana_t,
     syn,
     syn_t,
+    ana_high,
+    ana_high_t,
+    syn_high,
+    syn_high_t,
+    tab_recv,
+    tab_send,
     w_parts,
     w_real,
     w_imag,
@@ -179,9 +195,17 @@
     narrow = width // lon
     hidden = mlp_in.shape[1]
     band = lats // lat
-    block = 2 * slab * band
     waves = 2 * slab * lat
+    high, each = split_orders(slab * lat, lat)
+    near = lat // 2
+    block = 2 * each * band
+    slots = lat + near
+    low_rows = degrees - high
+    starts = [near * i // 8 * 8 for i in range(each)]
+    packs = [sum(low_rows - start for start in starts[:i]) for i in range(each)]
     my_lat, my_lon = lax.axis_index("lat"), lax.axis_index("lon")
+    mixed = normed
+    my_side, my_near = my_lat // near, lax.rem(my_lat, near)
     half_tile = row_tile(rows, 144)
     full_tile = row_tile(rows, 240)
 
@@ -195,12 +219,12 @@
             device_id_type=MESH,
         )
 
-    def lat_copy(stage, chunk, src, dst, peer):
+    def lat_copy(send_at, recv_at, chunk, src, dst, peer):
         return pltpu.make_async_remote_copy(
             src_ref=src,
             dst_ref=dst,
-            send_sem=send_sem.at[stage - 1],
-            recv_sem=recv_sem.at[stage - 1, chunk, 0],
+            send_sem=send_sem.at[send_at],
+            recv_sem=recv_sem.at[recv_at, chunk, 0],
             device_id={"lat": peer},
             device_id_type=MESH,
         )
@@ -246,13 +270,19 @@
             def _(half=half):
                 own_copy(stage, chunk, held.at[src, half], landing.at[chunk, my_lon]).start()
 
-    def spread_bands(stage, chunk, buffer, target):
+    def spread_low(send_at, recv_at, chunk, buffer, target):
         for step in range(1, lat):
             peer = lax.rem(my_lat + step, lat)
-            lat_copy(stage, chunk, buffer.at[peer], target.at[chunk, my_lat], peer).start()
-
-    def pair(values, factor):
-        return jnp.concatenate([values(0), values(1)], axis=1).astype(jnp.bfloat16)
+            lat_copy(send_at, recv_at, chunk, buffer.at[peer], target.at[chunk, my_lat], peer).start()
+
+    def spread_high(send_at, recv_at, chunk, buffer, target):
+        for step in range(1, near):
+            peer = lax.rem(my_near + step, near)
+            src, dst = buffer.at[lat + peer], target.at[chunk, lat + my_near]
+            lat_copy(send_at, recv_at, chunk, src, dst, my_side * near + peer).start()
+
+    def own_rows(at):
+        return pl.ds(pl.multiple_of(at * block, 16), block)
 
     def to_waves(stage, chunk, table, scale, buffer, landing):
         landed(stage - 1, chunk, landing.at[chunk])
@@ -270,17 +300,18 @@
 
         @pl.when(chunk > 0)
         def _():
-            sent(stage, buffer.at[pl.ds(0, lat - 1)])
-
-        for target in range(lat):
+            sent(stage, buffer.at[pl.ds(0, slots - 2)])
+
+        for target in range(slots):
             buffer[target] = slim[pl.ds(target * block, block), :].astype(jnp.bfloat16)
-        spread_bands(stage, chunk, buffer, lat_a)
-        own = pl.ds(pl.multiple_of(my_lat * block, 8), block)
-        lat_a[chunk, my_lat] = slim[own, :].astype(jnp.bfloat16)
+        spread_low(stage - 1, stage - 1, chunk, buffer, lat_a)
+        spread_high(stage - 1, stage - 1, chunk, buffer, lat_a)
+        lat_a[chunk, my_lat] = slim[own_rows(my_lat), :].astype(jnp.bfloat16)
+        lat_a[chunk, lat + my_near] = slim[own_rows(lat + my_near), :].astype(jnp.bfloat16)
 
     def to_points(stage, chunk, table, scale, buffer):
-        landed(stage - 1, chunk, lat_b.at[chunk, pl.ds(0, lat - 1)])
-        for source in range(lat):
+        landed(stage - 1, chunk, lat_b.at[chunk, pl.ds(0, slots - 2)])
+        for source in range(slots):
             slim[pl.ds(source * block, block), :] = lat_b[chunk, source].astype(jnp.float32)
         for first in range(0, band, 2):
             rhs = jnp.concatenate(
@@ -334,27 +365,45 @@
         part = mixed.at[pl.ds((chunks - 1) * group, group)]
         return pltpu.make_async_copy(part, last_mixed, own_sem.at[4])
 
-    def slab_step(stage, chunk, first_table, second_table, between, buffer):
-        landed(stage - 1, chunk, lat_a.at[chunk, pl.ds(0, lat - 1)])
-        for source in range(lat):
+    def wave_rows(first, count, i):
+        parts = []
+        for r in range(2):
+            at = (r * each + i) * band
+            held = [slim[pl.ds(s * block + at, band), :] for s in range(first, first + count)]
+            parts.append(jnp.concatenate(held, axis=0))
+        return jnp.concatenate(parts, axis=1).astype(jnp.bfloat16)
+
+    def put_rows(got, count, i):
+        for r in range(2):
+            at = (r * each + i) * band
+            for t in range(count):
+                wide[pl.ds(t * block + at, band), :] = got[
+                    t * band : (t + 1) * band, r * LANES : (r + 1) * LANES
+                ]
+
+    def pack_copy(k, chunk):
+        peer = lax.rem(my_lat + near, lat)
+        return lat_copy(10 + k, 8 + k, chunk, pack_own.at[k, chunk], pack_far.at[k, chunk], peer)
+
+    def slab_first(stage, k, chunk, tables, between, buffer):
+        first_table, second_table, high_table = tables
+        landed(stage - 1, chunk, lat_a.at[chunk, pl.ds(0, slots - 2)])
+        for source in range(slots):
             slim[pl.ds(source * block, block), :] = lat_a[chunk, source].astype(jnp.float32)
-        for m in range(slab):
-            parts = []
-            for r in range(2):
-                at = (r * slab + m) * band
-                parts.append(
-                    jnp.concatenate([slim[pl.ds(s * block + at, band), :] for s in range(lat)], axis=0)
-                )
-            rhs = jnp.concatenate(parts, axis=1).astype(jnp.bfloat16)
-            real, imag = between(m, dot(first_table[m], rhs))
+        for i in range(each):
+            got = dot(high_table[i], wave_rows(lat, near, i))
+            stack[pl.ds(packs[i], low_rows - starts[i]), :] = got[starts[i] :, :]
+
+        @pl.when(chunk > 0)
+        def _():
+            pack_copy(k, chunk).wait_send()
+
+        pack_own[k, chunk] = stack[...].astype(jnp.bfloat16)
+        pack_copy(k, chunk).start()
+        for m in range(each):
+            real, imag = between(m, dot(first_table[m], wave_rows(0, lat, m)))
             low = jnp.concatenate([real, imag], axis=1).astype(jnp.bfloat16)
-            got = dot(second_table[m], low)
-            for r in range(2):
-                at = (r * slab + m) * band
-                for t in range(lat):
-                    wide[pl.ds(t * block + at, band), :] = got[
-                        t * band : (t + 1) * band, r * LANES : (r + 1) * LANES
-                    ]
+            put_rows(dot(second_table[m], low), lat, m)
 
         @pl.when(chunk > 0)
         def _():
@@ -362,9 +411,31 @@
 
         for target in range(lat):
             buffer[target] = wide[pl.ds(target * block, block), :].astype(jnp.bfloat16)
-        spread_bands(stage, chunk, buffer, lat_b)
-        own = pl.ds(pl.multiple_of(my_lat * block, 8), block)
-        lat_b[chunk, my_lat] = wide[own, :].astype(jnp.bfloat16)
+        spread_low(stage - 1, stage - 1, chunk, buffer, lat_b)
+        lat_b[chunk, my_lat] = wide[own_rows(my_lat), :].astype(jnp.bfloat16)
+
+    def slab_second(stage, k, chunk, table, before, between, buffer):
+        landed(9 + k, chunk, pack_far.at[k, chunk])
+        stack[...] = pack_own[k, chunk].astype(jnp.float32) + pack_far[k, chunk].astype(jnp.float32)
+        before()
+        for i in range(each):
+            count = low_rows - starts[i]
+            real, imag = between(pl.ds(packs[i], count), high + starts[i], count)
+            low = jnp.concatenate([real, imag], axis=1)
+            if starts[i]:
+                low = jnp.concatenate([jnp.zeros((starts[i], 2 * LANES), jnp.float32), low], axis=0)
+            put_rows(dot(table[i], low.astype(jnp.bfloat16)), near, i)
+
+        if near > 1:
+
+            @pl.when(chunk > 0)
+            def _():
+                sent(9 + k, buffer.at[pl.ds(lat, near - 1)])
+
+        for target in range(near):
+            buffer[lat + target] = wide[pl.ds(target * block, block), :].astype(jnp.bfloat16)
+        spread_high(8 + k, stage - 1, chunk, buffer, lat_b)
+        lat_b[chunk, lat + my_near] = wide[own_rows(my_near), :].astype(jnp.bfloat16)
 
     hidden_rows = width * hidden // LANES
     vector_rows = 2 * hidden_rows + width * width // LANES
@@ -405,16 +476,26 @@
     def stage_2(chunk):
         to_waves(2, chunk, fwd_t, 1.0 / points, send_2, lon_a)
 
-    def stage_3(chunk):
+    def filtered(real, imag, rows):
+        wr, wi = w_real[rows, :], w_imag[rows, :]
+        return wr * real - wi * imag, wr * imag + wi * real
+
+    def stage_3a(chunk):
         def between(m, got):
             coeffs[chunk, m] = got.astype(jnp.bfloat16)
-            real, imag = got[:, :LANES], got[:, LANES:]
-            return (
-                w_real[...] * real - w_imag[...] * imag,
-                w_real[...] * imag + w_imag[...] * real,
-            )
-
-        slab_step(3, chunk, ana, syn, between, send_3)
+            return filtered(got[:, :LANES], got[:, LANES:], pl.ds(0, degrees))
+
+        slab_first(3, 0, chunk, (ana, syn, ana_high), between, send_3)
+
+    def stage_3b(chunk):
+        def before():
+            coeffs_high[chunk] = stack[...].astype(jnp.bfloat16)
+
+        def between(where, degree, count):
+            got = stack[where, :]
+            return filtered(got[:, :LANES], got[:, LANES:], pl.ds(degree, count))
+
+        slab_second(3, 0, chunk, syn_high, before, between, send_3)
 
     def stage_4(chunk):
         to_points(4, chunk, inv, None, send_4)
@@ -423,6 +504,10 @@
         @pl.when(chunk > 0)
         def _():
             sent(5, lon_a.at[chunk, pl.ds(0, lon - 1)])
+
+        @pl.when(chunk == chunks - 1)
+        def _():
+            sent(1, lon_a.at[chunk, pl.ds(0, lon - 1)])
 
         feed_forward(chunk, range(group // 2))
 
@@ -481,19 +566,28 @@
     def stage_6(chunk):
         to_waves(6, chunk, inv_t, None, send_6, lon_c)
 
-    def stage_7(chunk):
+    def unfiltered(got, held, degree, count, share_of):
+        dr, di = got[:, :LANES], got[:, LANES:]
+        ar, ai = held[:, :LANES], held[:, LANES:]
+        spec[pl.ds(degree, count), :] += share_of * (dr * ar + di * ai)
+        spec[pl.ds(degrees + degree, count), :] += share_of * (di * ar - dr * ai)
+        wr, wi = w_real[pl.ds(degree, count), :], w_imag[pl.ds(degree, count), :]
+        return wr * dr + wi * di, wr * di - wi * dr
+
+    def stage_7a(chunk):
         def between(m, got):
-            dr, di = got[:, :LANES], got[:, LANES:]
-            held = coeffs[chunk, m].astype(jnp.float32)
-            ar, ai = held[:, :LANES], held[:, LANES:]
-            spec[pl.ds(0, degrees), :] += dr * ar + di * ai
-            spec[pl.ds(degrees, degrees), :] += di * ar - dr * ai
-            return (
-                w_real[...] * dr + w_imag[...] * di,
-                w_real[...] * di - w_imag[...] * dr,
-            )
-
-        slab_step(7, chunk, syn_t, ana_t, between, send_7)
+            return unfiltered(got, coeffs[chunk, m].astype(jnp.float32), 0, degrees, 1.0)
+
+        slab_first(7, 1, chunk, (syn_t, ana_t, syn_high_t), between, send_7)
+
+    def stage_7b(chunk):
+        def before():
+            stack_held[...] = coeffs_high[chunk].astype(jnp.float32)
+
+        def between(where, degree, count):
+            return unfiltered(stack[where, :], stack_held[where, :], degree, count, 0.5)
+
+        slab_second(7, 1, chunk, ana_high_t, before, between, send_7)
 
     def stage_8(chunk):
         to_points(8, chunk, fwd, 1.0 / points, send_8)
@@ -548,6 +642,48 @@
                 def _():
                     pltpu.make_async_copy(weight, held, w_sem.at[0, place]).start()
 
+    def table_copies(start):
+        def one(i, carry):
+            wave = my_lat * slab + i
+
+            def give(peer, slot, way):
+                for which, raw in enumerate((raw_ana, raw_syn)):
+
+                    @pl.when(peer != my_lat)
+                    def _(which=which, raw=raw):
+                        copy = pltpu.make_async_remote_copy(
+                            src_ref=raw.at[i],
+                            dst_ref=tabs.at[which, slot],
+                            send_sem=tab_send.at[which, i, way],
+                            recv_sem=tab_recv.at[which],
+                            device_id={"lat": peer},
+                            device_id_type=MESH,
+                        )
+                        if start:
+                            copy.start()
+                        else:
+                            copy.wait_send()
+
+                    if start:
+
+                        @pl.when(peer == my_lat)
+                        def _(which=which, raw=raw):
+                            pltpu.make_async_copy(raw.at[i], tabs.at[which, slot], tab_recv.at[which]).start()
+
+            @pl.when(wave < high)
+            def _():
+                give(lax.div(wave, each), lax.rem(wave, each), 0)
+
+            @pl.when(wave >= high)
+            def _():
+                above = wave - high
+                for side in range(2):
+                    give(side * near + lax.rem(above, near), each + lax.div(above, near), side)
+
+            return carry
+
+        lax.fori_loop(0, slab, one, 0)
+
     def build():
         acc[...] = jnp.zeros_like(acc)
         spec[...] = jnp.zeros_like(spec)
@@ -555,14 +691,23 @@
         mixed_sums[...] = jnp.zeros_like(mixed_sums)
         norm_own[...] = jnp.zeros_like(norm_own)
         degree = lax.broadcasted_iota(jnp.int32, (lats, degrees), 1)
-
-        @pl.loop(0, slab)
-        def _(m):
-            kept = degree >= my_lat * slab + m
-            for raw, plain, turned in ((raw_ana, ana_t, ana), (raw_syn, syn, syn_t)):
-                values = jnp.where(kept, raw[m].astype(jnp.float32), 0.0)
-                plain[m] = values.astype(jnp.bfloat16)
-                turned[m] = values.T.astype(jnp.bfloat16)
+        for which in range(2):
+            pltpu.make_async_copy(tabs.at[which], tabs.at[which], tab_recv.at[which]).wait()
+        kinds = ((ana_t, ana, ana_high_t, ana_high), (syn, syn_t, syn_high, syn_high_t))
+
+        @pl.loop(0, each)
+        def _(i):
+            half = pl.ds(pl.multiple_of(my_side * near * band, 16), near * band)
+            for which, (plain, turned, part, part_turned) in enumerate(kinds):
+                values = tabs[which, i].astype(jnp.float32)
+                values = jnp.where(degree >= my_lat * each + i, values, 0.0)
+                plain[i] = values.astype(jnp.bfloat16)
+                turned[i] = values.T.astype(jnp.bfloat16)
+                values = tabs[which, each + i, half, :].astype(jnp.float32)
+                values = jnp.where(degree[: near * band] >= high + near * i + my_near, values, 0.0)
+                values = values.T[high:, :]
+                part_turned[i] = values.astype(jnp.bfloat16)
+                part[i] = values.T.astype(jnp.bfloat16)
 
         for q in range(group):
             part = w_parts.at[:, pl.ds(q * narrow, narrow), :]
@@ -816,27 +961,28 @@
     end = chunks - 1
     aside = {
         (0, "1"): build,
-        (end + 5, "5b"): run((last_mixed_start, None), (norm_skip, None), (fold_start, 0)),
-        (end + 5, "9"): run((fold_end, 0), (fold_start, 1)),
-        (end + 6, "8"): run((fold_end, 1), (fold_start, 2)),
-        (end + 7, "7"): run((fold_end, 2), (fold_start, 3)),
-        (end + 7, "9"): run((fold_end, 3), (spread_start, 3)),
-        (end + 8, "9"): run((spread_end, 3), (spread_start, 2)),
-        (end + 9, "8"): run((spread_end, 2), (spread_start, 1)),
-        (end + 9, "9"): run((spread_end, 1), (spread_start, 0), (spec_middle, None)),
-        (end + 9, "7"): run((spec_start, None)),
-        (end + 10, "8"): run((norm_middle, None), (spec_back, None)),
+        (end + 6, "5b"): run((last_mixed_start, None), (norm_skip, None), (fold_start, 0)),
+        (end + 7, "7b"): run((fold_end, 0), (fold_start, 1)),
+        (end + 7, "9"): run((fold_end, 1), (fold_start, 2)),
+        (end + 8, "6"): run((fold_end, 2), (fold_start, 3)),
+        (end + 9, "7a"): run((fold_end, 3), (spread_start, 3)),
+        (end + 10, "7b"): run((spread_end, 3), (spread_start, 2)),
+        (end + 11, "7b"): run((spread_end, 2), (spread_start, 1), (spec_start, None)),
+        (end + 12, "8"): run((spread_end, 1), (spread_start, 0), (norm_middle, None), (spec_back, None)),
+        (end + 11, "9"): run((spec_middle, None)),
     }
 
     stages = {
         "1": stage_1,
         "2": stage_2,
-        "3": stage_3,
+        "3a": stage_3a,
+        "3b": stage_3b,
         "4": stage_4,
         "5a": stage_5a,
         "5b": stage_5b,
         "6": stage_6,
-        "7": stage_7,
+        "7a": stage_7a,
+        "7b": stage_7b,
         "8": stage_8,
         "9": stage_9,
     }
@@ -846,8 +992,7 @@
 
     padded = lon_a.shape[2]
     if padded > rows:
-        for held in (normed, mixed):
-            held[:, :, rows:, :] = jnp.zeros_like(held[:, :, rows:, :])
+        normed[:, :, rows:, :] = jnp.zeros_like(normed[:, :, rows:, :])
         for held in (send_4, send_8):
             held[:, rows:, :] = jnp.zeros_like(held[:, rows:, :])
     barrier = pltpu.get_barrier_semaphore()
@@ -868,6 +1013,7 @@
     pl.semaphore_wait(barrier, lon - 1 + lat - 1)
 
     weight_copies(True)
+    table_copies(True)
 
     def tick(now, carry):
         for stage in ORDER:
@@ -894,18 +1040,23 @@
     last_own().wait()
     last_mixed_copy().wait()
     weight_copies(False)
+    table_copies(False)
     last = chunks - 1
-    for stage in (1, 5):
-        sent(stage, lon_a.at[last, pl.ds(0, lon - 1)])
+    sent(5, lon_a.at[last, pl.ds(0, lon - 1)])
     for stage, buffer, count in (
-        (2, send_2, lat - 1),
+        (2, send_2, slots - 2),
         (3, send_3, lat - 1),
         (4, send_4, lon - 1),
-        (6, send_6, lat - 1),
+        (6, send_6, slots - 2),
         (7, send_7, lat - 1),
         (8, send_8, lon - 1),
+        (9, send_3, near - 1),
+        (10, send_7, near - 1),
     ):
-        sent(stage, buffer.at[pl.ds(0, count)])
+        if count:
+            sent(stage, buffer.at[pl.ds(0, count)])
+    for k in range(2):
+        pack_copy(k, last).wait_send()
     for k in range(group):
         o_store(last * group + k, k).wait()
         if chunks > 1:
@@ -1033,7 +1184,6 @@
 
 
 def per_device(
-    tables,
     lat,
     lon,
     inputs,
@@ -1061,10 +1211,14 @@
     halves = width // LANES
     group = lon // halves
     chunks = batch // group
-    block = 2 * slab * band
+
+    forward, inverse = fourier_tables(points, orders, lat)
+    high, each = split_orders(orders, lat)
+    near = lat // 2
+    low_rows = degrees - high
+    block = 2 * each * band
     waves = 2 * orders
-
-    forward, inverse = tables(points, lat)(orders)
+    pack_rows = sum(low_rows - near * i // 8 * 8 for i in range(each))
     my_lon = lax.axis_index("lon")
     hidden = mlp_in.shape[1]
     flat_rows = (2 * hidden + width) * width // LANES + 8 * (hidden + 3 * width) // LANES
@@ -1097,34 +1251,45 @@
         scratch_shapes=[
             pltpu.VMEM((batch, rows, width), low),
             pltpu.VMEM((batch, halves, padded, LANES), low),
-            pltpu.VMEM((batch, halves, padded, LANES), low),
             pltpu.VMEM((chunks, lon, padded, LANES), low),
             pltpu.VMEM((chunks, lon, padded, LANES), low),
             pltpu.VMEM((batch, halves, padded, LANES), low),
-            pltpu.VMEM((chunks, lat, block, LANES), low),
-            pltpu.VMEM((chunks, lat, block, LANES), low),
-            pltpu.VMEM((chunks, slab, degrees, 2 * LANES), low),
-            pltpu.VMEM((lat, block, LANES), low),
-            pltpu.VMEM((lat, block, LANES), low),
+            pltpu.VMEM((chunks, lat + near, block, LANES), low),
+            pltpu.VMEM((chunks, lat + near, block, LANES), low),
+            pltpu.VMEM((chunks, each, degrees, 2 * LANES), low),
+            pltpu.VMEM((chunks, pack_rows, 2 * LANES), low),
+            pltpu.VMEM((2, chunks, pack_rows, 2 * LANES), low),
+            pltpu.VMEM((2, chunks, pack_rows, 2 * LANES), low),
+            pltpu.VMEM((pack_rows, 2 * LANES), full),
+            pltpu.VMEM((pack_rows, 2 * LANES), full),
+            pltpu.VMEM((lat + near, block, LANES), low),
+            pltpu.VMEM((lat + near, block, LANES), low),
             pltpu.VMEM((lon, padded, LANES), low),
-            pltpu.VMEM((lat, block, LANES), low),
-            pltpu.VMEM((lat, block, LANES), low),
+            pltpu.VMEM((lat + near, block, LANES), low),
+            pltpu.VMEM((lat + near, block, LANES), low),
             pltpu.VMEM((lon, padded, LANES), low),
             pltpu.VMEM((max(points, waves) * band, LANES), full),
             pltpu.VMEM((waves * band, LANES), full),
             pltpu.VMEM((group, rows, width), low),
             pltpu.VMEM((group, rows, width), low),
             pltpu.VMEM((group, rows, width), full),
-            pltpu.SemaphoreType.DMA((8, chunks, group)),
-            pltpu.SemaphoreType.DMA((8,)),
+            pltpu.SemaphoreType.DMA((10, chunks, group)),
+            pltpu.SemaphoreType.DMA((12,)),
             pltpu.SemaphoreType.DMA((batch,)),
             pltpu.SemaphoreType.DMA((group,)),
             pltpu.SemaphoreType.DMA((group,)),
             pltpu.SemaphoreType.DMA((group,)),
-            pltpu.VMEM((slab, degrees, lats), low),
-            pltpu.VMEM((slab, lats, degrees), low),
-            pltpu.VMEM((slab, lats, degrees), low),
-            pltpu.VMEM((slab, degrees, lats), low),
+            pltpu.VMEM((2, 2 * each, lats, degrees), low),
+            pltpu.VMEM((each, degrees, lats), low),
+            pltpu.VMEM((each, lats, degrees), low),
+            pltpu.VMEM((each, lats, degrees), low),
+            pltpu.VMEM((each, degrees, lats), low),
+            pltpu.VMEM((each, low_rows, near * band), low),
+            pltpu.VMEM((each, near * band, low_rows), low),
+            pltpu.VMEM((each, near * band, low_rows), low),
+            pltpu.VMEM((each, low_rows, near * band), low),
+            pltpu.SemaphoreType.DMA((2,)),
+            pltpu.SemaphoreType.DMA((2, slab, 2)),
             pltpu.VMEM((2, LANES, degrees), full),
             pltpu.VMEM((degrees, LANES), full),
             pltpu.VMEM((degrees, LANES), full),
@@ -1231,7 +1396,7 @@
     table = P("lat", None, None)
     channel = P(None, None, "lon")
     return jax.shard_map(
-        functools.partial(per_device, fourier_tables, lat, lon),
+        functools.partial(per_device, lat, lon),
         mesh=mesh,
         in_specs=(grid, table, table, channel) + (P(),) * 9 + (grid,),
         out_specs=(grid, grid, channel) + (P(),) * 9,

time: 333 us -> 322 us (0.967)
  Pallas kernels: 327 us -> 315 us
    pallas_call x1, Pallas kernels: 315 us -> 302 us  [per_device(): pl.pallas_call(functools.partial(block_kernel, lat, lon), out_shape=(jax....]
where the time goes in v6:
time: 322 us; the launch traced here: 320 us
  Pallas kernels  315 us (98%)
  local copies, waits for them, and re-layouts  4.84 us (2%)
    pallas_call x1, Pallas kernels, per_device(): pl.pallas_call(functools.partial(block_kernel, lat, lon), out_shape=(jax....  302 us
    pallas_call x1, Pallas kernels, per_device(): pl.pallas_call(functools.partial(result_kernel, group, width // lon, lat...  12.8 us

profile of v6, /device:TPU:0, one launch (start us, length us, event | category | flops | bytes accessed | tf_op | source)
XLA Modules:
  0.0 320.4 jit_solution(1898453985655310314)
XLA Ops:
  0.6 0.0 copy-start.3
  0.7 0.0 copy-start.5
  0.7 0.0 copy-start.6
  0.7 302.1 %shard_map.265 = (bf16[16,720,256]{2,1,0:T(8,128)(2,1)}, f32[14,720,256]{2,1,0:T(8,128)}, bf16[3072,128]{1,0:T(8,128)(2,1)}, f32[200,128]{1,0:T(8,128)}, bf16[2,...) custom-call(bf16[16,720,256]{2,1,0:T(8,128)(2,1)} %bitcast.31, bf16[16,720,256]{2,1,0:T(8,128)(2,1)} %bitcast.33, ...), custom_call_target="tpu_custom_call" | custom-call | tf_op jit(solution)/shard_map/pallas_call | solution.py:1239
  302.8 0.0 copy-done.3
  302.8 0.0 copy-done.5
  302.8 0.0 copy-done.6
  302.8 0.0 copy-start
  302.8 1.1 copy-done
  303.9 0.0 copy-start.1
  303.9 1.1 copy-done.1
  305.1 0.0 copy-start.2
  305.1 1.1 copy-done.2
  306.2 0.0 copy-start.4
  306.2 0.9 copy-done.4
  307.1 12.8 %shard_map.266 = (bf16[16,720,256]{2,1,0:T(8,128)(2,1)}, f32[16,720,256]{2,1,0:T(8,128)}, f32[2,64,96]{2,1,0:T(8,128)}, f32[256,256]{1,0:T(8,128)}, f32[256,512]...) custom-call(bf16[16,720,256]{2,1,0:T(8,128)(2,1)} %get-tuple-element.26.out_from, ...), custom_call_target="tpu_custom_call" | custom-call | tf_op jit(solution)/shard_map/pallas_call | solution.py:1357
  319.8 0.6 fusion
Async XLA Ops:
  0.6 302.1 %copy-start.3 = (bf16[256,256]{1,0:T(8,128)(2,1)S(1)}, bf16[256,256]{1,0:T(8,128)(2,1)}, u32[]{:S(2)}) copy-start(bf16[256,256]{1,0:T(8,128)(2,1)} %skip.3) | copy-start | bytes 393220
  0.7 302.1 %copy-start.5 = (f32[256]{0:T(256)S(1)}, f32[256]{0:T(256)}, u32[]{:S(2)}) copy-start(f32[256]{0:T(256)} %param.23) | copy-start | bytes 3076
  0.7 302.1 %copy-start.6 = (f32[256]{0:T(256)S(1)}, f32[256]{0:T(256)}, u32[]{:S(2)}) copy-start(f32[256]{0:T(256)} %param.24) | copy-start | bytes 3076
  302.8 1.1 copy-start
  303.9 1.1 copy-start.1
  305.1 1.1 copy-start.2
  306.2 0.9 copy-start.4

commit v7 on v6

--- a/solution.py
+++ b/solution.py
@@ -140,6 +140,7 @@
     i_buf,
     recv_sem,
     send_sem,
+    rows_sem,
     x_sem,
     g_sem,
     o_sem,
@@ -209,11 +210,14 @@
     half_tile = row_tile(rows, 144)
     full_tile = row_tile(rows, 240)
 
+    def slot_of(chunk):
+        return lax.rem(chunk, 2)
+
     def lon_copy(stage, chunk, src, dst, peer, member=0):
         return pltpu.make_async_remote_copy(
             src_ref=src,
             dst_ref=dst,
-            send_sem=send_sem.at[stage - 1],
+            send_sem=rows_sem.at[stage // 4, chunk] if stage in (1, 5) else send_sem.at[stage - 1, slot_of(chunk)],
             recv_sem=recv_sem.at[stage - 1, chunk, member],
             device_id={"lon": peer},
             device_id_type=MESH,
@@ -223,7 +227,7 @@
         return pltpu.make_async_remote_copy(
             src_ref=src,
             dst_ref=dst,
-            send_sem=send_sem.at[send_at],
+            send_sem=send_sem.at[send_at, slot_of(chunk)],
             recv_sem=recv_sem.at[recv_at, chunk, 0],
             device_id={"lat": peer},
             device_id_type=MESH,
@@ -242,8 +246,8 @@
         count = halves if step else halves - 1
         landed(stage, chunk, lon_a.at[chunk, pl.ds(0, count)], member_at(step))
 
-    def sent(stage, part):
-        lon_copy(stage, 0, part, part, my_lon).wait_send()
+    def sent(stage, chunk, part):
+        lon_copy(stage, chunk, part, part, my_lon).wait_send()
 
     def x_load(sample):
         return pltpu.make_async_copy(x_hbm.at[sample], x_all.at[sample], x_sem.at[sample])
@@ -285,6 +289,7 @@
         return pl.ds(pl.multiple_of(at * block, 16), block)
 
     def to_waves(stage, chunk, table, scale, buffer, landing):
+        slot = slot_of(chunk)
         landed(stage - 1, chunk, landing.at[chunk])
         for source in range(lon):
             wide[pl.ds(source * rows, rows), :] = landing[chunk, source, pl.ds(0, rows), :].astype(jnp.float32)
@@ -298,18 +303,19 @@
             for k in range(2):
                 slim[pl.ds(first + k, waves, stride=band), :] = got[:, k * LANES : (k + 1) * LANES]
 
-        @pl.when(chunk > 0)
+        @pl.when(chunk > 1)
         def _():
-            sent(stage, buffer.at[pl.ds(0, slots - 2)])
+            sent(stage, chunk, buffer.at[slot, pl.ds(0, slots - 2)])
 
         for target in range(slots):
-            buffer[target] = slim[pl.ds(target * block, block), :].astype(jnp.bfloat16)
-        spread_low(stage - 1, stage - 1, chunk, buffer, lat_a)
-        spread_high(stage - 1, stage - 1, chunk, buffer, lat_a)
+            buffer[slot, target] = slim[pl.ds(target * block, block), :].astype(jnp.bfloat16)
+        spread_low(stage - 1, stage - 1, chunk, buffer.at[slot], lat_a)
+        spread_high(stage - 1, stage - 1, chunk, buffer.at[slot], lat_a)
         lat_a[chunk, my_lat] = slim[own_rows(my_lat), :].astype(jnp.bfloat16)
         lat_a[chunk, lat + my_near] = slim[own_rows(lat + my_near), :].astype(jnp.bfloat16)
 
     def to_points(stage, chunk, table, scale, buffer):
+        slot = slot_of(chunk)
         landed(stage - 1, chunk, lat_b.at[chunk, pl.ds(0, slots - 2)])
         for source in range(slots):
             slim[pl.ds(source * block, block), :] = lat_b[chunk, source].astype(jnp.float32)
@@ -323,13 +329,13 @@
             for k in range(2):
                 wide[pl.ds(first + k, points, stride=band), :] = got[:, k * LANES : (k + 1) * LANES]
 
-        @pl.when(chunk > 0)
+        @pl.when(chunk > 1)
         def _():
-            sent(stage, buffer.at[pl.ds(0, lon - 1)])
+            sent(stage, chunk, buffer.at[slot, pl.ds(0, lon - 1)])
 
         for target in range(lon):
             grid = wide[pl.ds(target * rows, rows), :]
-            buffer[target, pl.ds(0, rows), :] = grid.astype(jnp.bfloat16)
+            buffer[slot, target, pl.ds(0, rows), :] = grid.astype(jnp.bfloat16)
             if stage == 8:
                 before = lon_a[chunk, target, pl.ds(0, rows), :].astype(jnp.float32)
                 norm_sums[0] += fold(grid * before)
@@ -339,7 +345,7 @@
         def send(landing):
             for step in range(1, lon):
                 peer = lax.rem(my_lon + step, lon)
-                lon_copy(stage, chunk, buffer.at[peer], landing, peer, member).start()
+                lon_copy(stage, chunk, buffer.at[slot, peer], landing, peer, member).start()
 
         def send_here():
             send(lon_b.at[chunk * group + member, half])
@@ -359,7 +365,7 @@
 
     def last_own():
         held = last_grid.at[my_lon // halves, lax.rem(my_lon, halves)]
-        return pltpu.make_async_copy(send_8.at[my_lon], held, own_sem.at[3])
+        return pltpu.make_async_copy(send_8.at[(chunks - 1) % 2, my_lon], held, own_sem.at[3])
 
     def last_mixed_copy():
         part = mixed.at[pl.ds((chunks - 1) * group, group)]
@@ -387,6 +393,7 @@
 
     def slab_first(stage, k, chunk, tables, between, buffer):
         first_table, second_table, high_table = tables
+        slot = slot_of(chunk)
         landed(stage - 1, chunk, lat_a.at[chunk, pl.ds(0, slots - 2)])
         for source in range(slots):
             slim[pl.ds(source * block, block), :] = lat_a[chunk, source].astype(jnp.float32)
@@ -394,7 +401,7 @@
             got = dot(high_table[i], wave_rows(lat, near, i))
             stack[pl.ds(packs[i], low_rows - starts[i]), :] = got[starts[i] :, :]
 
-        @pl.when(chunk > 0)
+        @pl.when(chunk > 1)
         def _():
             pack_copy(k, chunk).wait_send()
 
@@ -405,16 +412,17 @@
             low = jnp.concatenate([real, imag], axis=1).astype(jnp.bfloat16)
             put_rows(dot(second_table[m], low), lat, m)
 
-        @pl.when(chunk > 0)
+        @pl.when(chunk > 1)
         def _():
-            sent(stage, buffer.at[pl.ds(0, lat - 1)])
+            sent(stage, chunk, buffer.at[slot, pl.ds(0, lat - 1)])
 
         for target in range(lat):
-            buffer[target] = wide[pl.ds(target * block, block), :].astype(jnp.bfloat16)
-        spread_low(stage - 1, stage - 1, chunk, buffer, lat_b)
+            buffer[slot, target] = wide[pl.ds(target * block, block), :].astype(jnp.bfloat16)
+        spread_low(stage - 1, stage - 1, chunk, buffer.at[slot], lat_b)
         lat_b[chunk, my_lat] = wide[own_rows(my_lat), :].astype(jnp.bfloat16)
 
     def slab_second(stage, k, chunk, table, before, between, buffer):
+        slot = slot_of(chunk)
         landed(9 + k, chunk, pack_far.at[k, chunk])
         stack[...] = pack_own[k, chunk].astype(jnp.float32) + pack_far[k, chunk].astype(jnp.float32)
         before()
@@ -428,13 +436,13 @@
 
         if near > 1:
 
-            @pl.when(chunk > 0)
+            @pl.when(chunk > 1)
             def _():
-                sent(9 + k, buffer.at[pl.ds(lat, near - 1)])
+                sent(9 + k, chunk, buffer.at[slot, pl.ds(lat, near - 1)])
 
         for target in range(near):
-            buffer[lat + target] = wide[pl.ds(target * block, block), :].astype(jnp.bfloat16)
-        spread_high(8 + k, stage - 1, chunk, buffer, lat_b)
+            buffer[slot, lat + target] = wide[pl.ds(target * block, block), :].astype(jnp.bfloat16)
+        spread_high(8 + k, stage - 1, chunk, buffer.at[slot], lat_b)
         lat_b[chunk, lat + my_near] = wide[own_rows(my_near), :].astype(jnp.bfloat16)
 
     hidden_rows = width * hidden // LANES
@@ -460,10 +468,6 @@
                 normed[sample, h, where, :] = low[:, h * LANES : (h + 1) * LANES]
 
     def stage_1(chunk):
-        @pl.when(chunk > 0)
-        def _():
-            sent(1, lon_a.at[chunk, pl.ds(0, lon - 1)])
-
         for step in reversed(range(group)):
             k = member_at(step)
 
@@ -501,14 +505,7 @@
         to_points(4, chunk, inv, None, send_4)
 
     def stage_5a(chunk):
-        @pl.when(chunk > 0)
-        def _():
-            sent(5, lon_a.at[chunk, pl.ds(0, lon - 1)])
-
-        @pl.when(chunk == chunks - 1)
-        def _():
-            sent(1, lon_a.at[chunk, pl.ds(0, lon - 1)])
-
+        sent(1, chunk, lon_a.at[chunk, pl.ds(0, lon - 1)])
         feed_forward(chunk, range(group // 2))
 
     def stage_5b(chunk):
@@ -994,7 +991,7 @@
     if padded > rows:
         normed[:, :, rows:, :] = jnp.zeros_like(normed[:, :, rows:, :])
         for held in (send_4, send_8):
-            held[:, rows:, :] = jnp.zeros_like(held[:, rows:, :])
+            held[:, :, rows:, :] = jnp.zeros_like(held[:, :, rows:, :])
     barrier = pltpu.get_barrier_semaphore()
     for step in range(1, lon):
         pl.semaphore_signal(
@@ -1042,21 +1039,23 @@
     weight_copies(False)
     table_copies(False)
     last = chunks - 1
-    sent(5, lon_a.at[last, pl.ds(0, lon - 1)])
-    for stage, buffer, count in (
-        (2, send_2, slots - 2),
-        (3, send_3, lat - 1),
-        (4, send_4, lon - 1),
-        (6, send_6, slots - 2),
-        (7, send_7, lat - 1),
-        (8, send_8, lon - 1),
-        (9, send_3, near - 1),
-        (10, send_7, near - 1),
-    ):
-        if count:
-            sent(stage, buffer.at[pl.ds(0, count)])
-    for k in range(2):
-        pack_copy(k, last).wait_send()
+    for chunk in range(chunks):
+        sent(5, chunk, lon_a.at[chunk, pl.ds(0, lon - 1)])
+    for chunk in range(max(chunks - 2, 0), chunks):
+        for stage, buffer, count in (
+            (2, send_2, slots - 2),
+            (3, send_3, lat - 1),
+            (4, send_4, lon - 1),
+            (6, send_6, slots - 2),
+            (7, send_7, lat - 1),
+            (8, send_8, lon - 1),
+            (9, send_3, near - 1),
+            (10, send_7, near - 1),
+        ):
+            if count:
+                sent(stage, chunk, buffer.at[chunk % 2, pl.ds(0, count)])
+        for k in range(2):
+            pack_copy(k, chunk).wait_send()
     for k in range(group):
         o_store(last * group + k, k).wait()
         if chunks > 1:
@@ -1262,19 +1261,20 @@
             pltpu.VMEM((2, chunks, pack_rows, 2 * LANES), low),
             pltpu.VMEM((pack_rows, 2 * LANES), full),
             pltpu.VMEM((pack_rows, 2 * LANES), full),
-            pltpu.VMEM((lat + near, block, LANES), low),
-            pltpu.VMEM((lat + near, block, LANES), low),
-            pltpu.VMEM((lon, padded, LANES), low),
-            pltpu.VMEM((lat + near, block, LANES), low),
-            pltpu.VMEM((lat + near, block, LANES), low),
-            pltpu.VMEM((lon, padded, LANES), low),
+            pltpu.VMEM((2, lat + near, block, LANES), low),
+            pltpu.VMEM((2, lat + near, block, LANES), low),
+            pltpu.VMEM((2, lon, padded, LANES), low),
+            pltpu.VMEM((2, lat + near, block, LANES), low),
+            pltpu.VMEM((2, lat + near, block, LANES), low),
+            pltpu.VMEM((2, lon, padded, LANES), low),
             pltpu.VMEM((max(points, waves) * band, LANES), full),
             pltpu.VMEM((waves * band, LANES), full),
             pltpu.VMEM((group, rows, width), low),
             pltpu.VMEM((group, rows, width), low),
             pltpu.VMEM((group, rows, width), full),
             pltpu.SemaphoreType.DMA((10, chunks, group)),
-            pltpu.SemaphoreType.DMA((12,)),
+            pltpu.SemaphoreType.DMA((12, 2)),
+            pltpu.SemaphoreType.DMA((2, chunks)),
             pltpu.SemaphoreType.DMA((batch,)),
             pltpu.SemaphoreType.DMA((group,)),
             pltpu.SemaphoreType.DMA((group,)),

time: 322 us -> 312 us (0.969)
  Pallas kernels: 315 us -> 306 us
    pallas_call x1, Pallas kernels: 302 us -> 293 us  [per_device(): pl.pallas_call(functools.partial(block_kernel, lat, lon), out_shape=(jax....]
where the time goes in v7:
time: 312 us; the launch traced here: 311 us
  Pallas kernels  306 us (98%)
  local copies, waits for them, and re-layouts  4.84 us (2%)
    pallas_call x1, Pallas kernels, per_device(): pl.pallas_call(functools.partial(block_kernel, lat, lon), out_shape=(jax....  293 us
    pallas_call x1, Pallas kernels, per_device(): pl.pallas_call(functools.partial(result_kernel, group, width // lon, lat...  12.8 us

profile of v7, /device:TPU:0, one launch (start us, length us, event | category | flops | bytes accessed | tf_op | source)
XLA Modules:
  0.0 311.4 jit_solution(16698736682125047185)
XLA Ops:
  0.6 0.0 copy-start.3
  0.7 0.0 copy-start.5
  0.7 0.0 copy-start.6
  0.7 293.1 %shard_map.265 = (bf16[16,720,256]{2,1,0:T(8,128)(2,1)}, f32[14,720,256]{2,1,0:T(8,128)}, bf16[3072,128]{1,0:T(8,128)(2,1)}, f32[200,128]{1,0:T(8,128)}, bf16[2,...) custom-call(bf16[16,720,256]{2,1,0:T(8,128)(2,1)} %bitcast.31, bf16[16,720,256]{2,1,0:T(8,128)(2,1)} %bitcast.33, ...), custom_call_target="tpu_custom_call" | custom-call | tf_op jit(solution)/shard_map/pallas_call | solution.py:1238
  293.7 0.0 copy-done.3
  293.7 0.0 copy-done.5
  293.8 0.0 copy-done.6
  293.8 0.0 copy-start
  293.8 1.1 copy-done
  294.9 0.0 copy-start.1
  294.9 1.1 copy-done.1
  296.0 0.0 copy-start.2
  296.0 1.1 copy-done.2
  297.1 0.0 copy-start.4
  297.1 0.9 copy-done.4
  298.0 12.8 %shard_map.266 = (bf16[16,720,256]{2,1,0:T(8,128)(2,1)}, f32[16,720,256]{2,1,0:T(8,128)}, f32[2,64,96]{2,1,0:T(8,128)}, f32[256,256]{1,0:T(8,128)}, f32[256,512]...) custom-call(bf16[16,720,256]{2,1,0:T(8,128)(2,1)} %get-tuple-element.26.out_from, ...), custom_call_target="tpu_custom_call" | custom-call | tf_op jit(solution)/shard_map/pallas_call | solution.py:1357
  310.8 0.6 fusion
Async XLA Ops:
  0.6 293.1 %copy-start.3 = (bf16[256,256]{1,0:T(8,128)(2,1)S(1)}, bf16[256,256]{1,0:T(8,128)(2,1)}, u32[]{:S(2)}) copy-start(bf16[256,256]{1,0:T(8,128)(2,1)} %skip.3) | copy-start | bytes 393220
  0.7 293.1 %copy-start.5 = (f32[256]{0:T(256)S(1)}, f32[256]{0:T(256)}, u32[]{:S(2)}) copy-start(f32[256]{0:T(256)} %param.23) | copy-start | bytes 3076
  0.7 293.1 %copy-start.6 = (f32[256]{0:T(256)S(1)}, f32[256]{0:T(256)}, u32[]{:S(2)}) copy-start(f32[256]{0:T(256)} %param.24) | copy-start | bytes 3076
  293.8 1.1 copy-start
  294.9 1.1 copy-start.1
  296.0 1.1 copy-start.2
  297.1 0.9 copy-start.4

commit v8 on v7

--- a/solution.py
+++ b/solution.py
@@ -16,8 +16,8 @@
 root = math.sqrt(2.0 / math.pi)
 cubic = 0.044715
 
-OFFSET = {"1": 0, "2": 1, "3a": 3, "3b": 4, "4": 5, "5a": 6, "5b": 6, "6": 8, "7a": 10, "7b": 11, "8": 12, "9": 13}
-ORDER = ("1", "3b", "3a", "7b", "7a", "4", "5a", "6", "2", "5b", "8", "9")
+OFFSET = {"1": 0, "2": 1, "3a": 3, "3b": 4, "4": 5, "5a": 7, "5b": 7, "6": 9, "7a": 12, "7b": 13, "8": 14, "9": 15}
+ORDER = ("8", "1", "7b", "7a", "5a", "4", "5b", "3b", "3a", "6", "2", "9")
 
 
 def split_orders(orders, lat):
@@ -471,7 +471,7 @@
         for step in reversed(range(group)):
             k = member_at(step)
 
-            @pl.when(chunk > 0)
+            @pl.when(jnp.logical_or(chunk > 0, step == 0))
             def _(k=k):
                 normalize(chunk * group + k)
 
@@ -958,15 +958,16 @@
     end = chunks - 1
     aside = {
         (0, "1"): build,
-        (end + 6, "5b"): run((last_mixed_start, None), (norm_skip, None), (fold_start, 0)),
-        (end + 7, "7b"): run((fold_end, 0), (fold_start, 1)),
-        (end + 7, "9"): run((fold_end, 1), (fold_start, 2)),
-        (end + 8, "6"): run((fold_end, 2), (fold_start, 3)),
-        (end + 9, "7a"): run((fold_end, 3), (spread_start, 3)),
-        (end + 10, "7b"): run((spread_end, 3), (spread_start, 2)),
-        (end + 11, "7b"): run((spread_end, 2), (spread_start, 1), (spec_start, None)),
-        (end + 12, "8"): run((spread_end, 1), (spread_start, 0), (norm_middle, None), (spec_back, None)),
-        (end + 11, "9"): run((spec_middle, None)),
+        (end + 7, "5b"): run((last_mixed_start, None), (norm_skip, None), (fold_start, 0)),
+        (end + 8, "7a"): run((fold_end, 0), (fold_start, 1)),
+        (end + 9, "7b"): run((fold_end, 1), (fold_start, 2)),
+        (end + 10, "8"): run((fold_end, 2), (fold_start, 3)),
+        (end + 11, "8"): run((fold_end, 3), (spread_start, 3)),
+        (end + 11, "9"): run((spread_end, 3), (spread_start, 2)),
+        (end + 12, "9"): run((spread_end, 2), (spread_start, 1)),
+        (end + 14, "8"): run((spread_end, 1), (spread_start, 0), (norm_middle, None), (spec_back, None)),
+        (end + 13, "7b"): run((spec_start, None)),
+        (end + 13, "9"): run((spec_middle, None)),
     }
 
     stages = {
@@ -1001,8 +1002,8 @@
         pl.semaphore_signal(
             barrier, inc=1, device_id={"lat": lax.rem(my_lat + step, lat)}, device_id_type=MESH
         )
-    for k in range(group):
-        normalize(k)
+    for step in range(1, group):
+        normalize(member_at(step))
     for sample in range(group, batch):
         x_load(sample).start()
     for k in range(group):
@@ -1068,8 +1069,8 @@
     norm_at,
     out_from,
     gin_from,
-    total,
-    small,
+    total_hbm,
+    small_hbm,
     last_mixed,
     last_grid,
     x_hbm,
@@ -1089,6 +1090,8 @@
     x_held,
     mixed_held,
     grid_held,
+    total,
+    small,
     sems,
     last_sems,
 ):
@@ -1114,17 +1117,32 @@
     last = [
         pltpu.make_async_copy(source, held, last_sems.at[at])
         for at, (source, held) in enumerate(
-            ((x_hbm.at[pl.ds(first, group)], x_held), (last_mixed, mixed_held), (last_grid, grid_held))
+            (
+                (x_hbm.at[pl.ds(first, group)], x_held),
+                (last_mixed, mixed_held),
+                (last_grid, grid_held),
+                (total_hbm, total),
+                (small_hbm, small),
+            )
         )
     ]
-    for copy in last:
+    for copy in last[:3]:
         copy.start()
     for sample in range(batch):
         for copy in reads(sample):
             copy.start()
-    for copy in last:
+    for copy in last[3:]:
+        copy.start()
+    for copy in last[:3]:
         copy.wait()
 
+    def pass_on(samples):
+        for sample in samples:
+            for read, write in zip(reads(sample), writes(sample)):
+                read.wait()
+                write.start()
+
+    pass_on(range(batch // 2))
     back_tile = row_tile(rows, 144)
     for k in range(group):
 
@@ -1141,10 +1159,9 @@
 
         gin_write(first + k).start()
 
-    for sample in range(batch):
-        for read, write in zip(reads(sample), writes(sample)):
-            read.wait()
-            write.start()
+    pass_on(range(batch // 2, batch))
+    for copy in last[3:]:
+        copy.wait()
 
     def tile(base, height, q):
         return total[pl.ds(base + q * height, height), :].astype(jnp.float32)
@@ -1357,7 +1374,7 @@
     output, grad_inputs, grad_spec, grad_skip, grad_in, grad_out, in_bias, vectors = pl.pallas_call(
         functools.partial(result_kernel, group, width // lon, lat * spec_rows),
         out_shape=tuple(jax.ShapeDtypeStruct(*shape) for shape in shapes),
-        in_specs=[fixed, fixed, vmem, vmem, fixed, fixed, fixed, vmem, vmem, vmem],
+        in_specs=[fixed] * 7 + [vmem] * 3,
         out_specs=(fixed, fixed) + (vmem,) * 6,
         scratch_shapes=[
             pltpu.VMEM((batch, rows, width), full),
@@ -1365,10 +1382,12 @@
             pltpu.VMEM((group, rows, width), low),
             pltpu.VMEM((group, halves, padded, LANES), low),
             pltpu.VMEM((group, halves, padded, LANES), low),
+            pltpu.VMEM((total_rows, LANES), low),
+            pltpu.VMEM((lat * spec_rows + 8, LANES), full),
             pltpu.SemaphoreType.DMA((4, batch)),
-            pltpu.SemaphoreType.DMA((3,)),
+            pltpu.SemaphoreType.DMA((5,)),
         ],
-        compiler_params=pltpu.CompilerParams(vmem_limit_bytes=48 * 2**20),
+        compiler_params=pltpu.CompilerParams(vmem_limit_bytes=63 * 2**20),
     )(*results, flat(inputs), skip_weight, row(gain_first), row(bias_first))
 
     def unflat(values):

time: 312 us -> 302 us (0.968)
  Pallas kernels: 306 us -> 299 us
  local copies, waits for them, and re-layouts: 4.84 us -> 1.27 us
    pallas_call x1, Pallas kernels: 293 us -> 285 us  [per_device(): pl.pallas_call(functools.partial(block_kernel, lat, lon), out_shape=(jax....]
    unnamed x14 -> x0, local copies, waits for them, and re-layouts: 4.26 us -> none
where the time goes in v8:
time: 302 us; the launch traced here: 301 us
  Pallas kernels  299 us (99%)
    pallas_call x1, Pallas kernels, per_device(): pl.pallas_call(functools.partial(block_kernel, lat, lon), out_shape=(jax....  285 us
    pallas_call x1, Pallas kernels, per_device(): pl.pallas_call(functools.partial(result_kernel, group, width // lon, lat...  14.8 us

profile of v8, /device:TPU:0, one launch (start us, length us, event | category | flops | bytes accessed | tf_op | source)
XLA Modules:
  0.0 301.3 jit_solution(13101670182754280725)
XLA Ops:
  0.6 284.5 %shard_map.265 = (bf16[16,720,256]{2,1,0:T(8,128)(2,1)}, f32[14,720,256]{2,1,0:T(8,128)}, bf16[3072,128]{1,0:T(8,128)(2,1)}, f32[200,128]{1,0:T(8,128)}, bf16[2,...) custom-call(bf16[16,720,256]{2,1,0:T(8,128)(2,1)} %bitcast.27, bf16[16,720,256]{2,1,0:T(8,128)(2,1)} %bitcast.29, ...), custom_call_target="tpu_custom_call" | custom-call | tf_op jit(solution)/shard_map/pallas_call | solution.py:1255
  285.2 14.8 %shard_map.266 = (bf16[16,720,256]{2,1,0:T(8,128)(2,1)}, f32[16,720,256]{2,1,0:T(8,128)}, f32[2,64,96]{2,1,0:T(8,128)}, f32[256,256]{1,0:T(8,128)}, f32[256,512]...) custom-call(bf16[16,720,256]{2,1,0:T(8,128)(2,1)} %get-tuple-element.26.out_from, ...), custom_call_target="tpu_custom_call" | custom-call | tf_op jit(solution)/shard_map/pallas_call | solution.py:1374
  300.0 1.3 fusion

commit v9 on v8

--- a/solution.py
+++ b/solution.py
@@ -1284,8 +1284,8 @@
             pltpu.VMEM((2, lat + near, block, LANES), low),
             pltpu.VMEM((2, lat + near, block, LANES), low),
             pltpu.VMEM((2, lon, padded, LANES), low),
-            pltpu.VMEM((max(points, waves) * band, LANES), full),
-            pltpu.VMEM((waves * band, LANES), full),
+            pltpu.VMEM((max(points, waves) * band + 8, LANES), full),
+            pltpu.VMEM((waves * band + 8, LANES), full),
             pltpu.VMEM((group, rows, width), low),
             pltpu.VMEM((group, rows, width), low),
             pltpu.VMEM((group, rows, width), full),

time: 302 us -> 303 us (level)
  no operation moved by 1% of the time
where the time goes in v9:
time: 303 us
  Pallas kernels  301 us (99%)
    pallas_call x1, Pallas kernels, per_device(): pl.pallas_call(functools.partial(block_kernel, lat, lon), out_shape=(jax....  286 us
    pallas_call x1, Pallas kernels, per_device(): pl.pallas_call(functools.partial(result_kernel, group, width // lon, lat...  14.8 us

profile of v9, /device:TPU:0, one launch (start us, length us, event | category | flops | bytes accessed | tf_op | source)
XLA Modules:
  0.0 303.3 jit_solution(6521106665888474588)
XLA Ops:
  0.6 286.5 %shard_map.265 = (bf16[16,720,256]{2,1,0:T(8,128)(2,1)}, f32[14,720,256]{2,1,0:T(8,128)}, bf16[3072,128]{1,0:T(8,128)(2,1)}, f32[200,128]{1,0:T(8,128)}, bf16[2,...) custom-call(bf16[16,720,256]{2,1,0:T(8,128)(2,1)} %bitcast.27, bf16[16,720,256]{2,1,0:T(8,128)(2,1)} %bitcast.29, ...), custom_call_target="tpu_custom_call" | custom-call | tf_op jit(solution)/shard_map/pallas_call | solution.py:1255
  287.2 14.8 %shard_map.266 = (bf16[16,720,256]{2,1,0:T(8,128)(2,1)}, f32[16,720,256]{2,1,0:T(8,128)}, f32[2,64,96]{2,1,0:T(8,128)}, f32[256,256]{1,0:T(8,128)}, f32[256,512]...) custom-call(bf16[16,720,256]{2,1,0:T(8,128)(2,1)} %get-tuple-element.26.out_from, ...), custom_call_target="tpu_custom_call" | custom-call | tf_op jit(solution)/shard_map/pallas_call | solution.py:1374
  302.0 1.3 fusion
